TPU v7x, 32 devices: a whole 2x2x4 slice. The times are simulated.
32 devices in a mesh: tm: 8 (over z, x), mp: 4 (over y, core).
Axes of the slice: x: 2, y: 2, z: 4, core: 2. Of those that a mesh axis runs over, the one named last changes fastest.
Arguments:
- inputs: bfloat16 [1, 2048, 2304], P(None, 'tm', 'mp'), may hold values from -6 to 6
- first_weight: bfloat16 [4608, 3, 2304], P('tm', None, 'mp'), may hold values from -0.09375 to 0.09375
- first_bias: float32 [3, 2304], P(None, 'mp'), may hold values from -2 to 8, as said below
- second_weight: bfloat16 [4608, 3, 2304], P('tm', None, 'mp'), may hold values from -0.09375 to 0.09375
- second_bias: float32 [3, 2304], P(None, 'mp'), may hold values from -2 to 8, as said below
- cotangent: bfloat16 [1, 2048, 2304], P(None, 'tm', 'mp'), may hold values from -6 to 6
Outputs:
- outputs: bfloat16 [1, 2048, 2304], P(None, 'tm', 'mp')
- input_grad: float32 [1, 2048, 2304], P(None, 'tm', 'mp')
- first_weightgrad: float32 [4608, 3, 2304], P('tm', None, 'mp')
- first_biasgrad: float32 [3, 2304], P(None, 'mp')
- second_weightgrad: float32 [4608, 3, 2304], P('tm', None, 'mp')
- second_biasgrad: float32 [3, 2304], P(None, 'mp')
Inputs may be any that keep to these rules, and one draw needn't show every extreme that they name: `first_bias`: gate biases in the rows candidate, forget, output. `second_bias`: gate biases in the rows candidate, forget, output.
All inputs are finite; a program needn't handle non-finite values.
Results may differ from a plain program's by a relative error of at most 0.0047.
Values may be sent and summed in bfloat16 or wider, within the bound.
No kernel may reach another device: no remote copies, remote signals or barrier semaphores. Data moves between devices by JAX's collectives and lax.ppermute only.
A program may use at most 256 MiB of HBM per device.

v0:
```python
import jax
import jax.numpy as jnp
from jax import lax
from jax.sharding import PartitionSpec as P


def prefix(value, axis, join, neutral, backward):
    count, mine = (lax.axis_size(axis), lax.axis_index(axis))
    pieces = jax.tree.map(lambda part: lax.all_gather(part, axis), value)
    if backward:
        pieces = jax.tree.map(lambda part: part[::-1], pieces)
        mine = count - 1 - mine
    total = jax.tree.map(
        lambda part, zero: jnp.full_like(part, 0) + jnp.asarray(zero, part.dtype), value, neutral
    )

    def hop(position, total):
        longer = join(total, jax.tree.map(lambda part: part[position], pieces))
        return jax.tree.map(lambda new, old: jnp.where(position < mine, new, old), longer, total)

    return lax.fori_loop(0, count - 1, hop, total)


def passed_along(array, axis, by):
    size = lax.axis_size(axis)
    pairs = [(i, i + by) for i in range(size) if 0 <= i + by < size]
    return lax.ppermute(array, axis, pairs)


def affine_join(earlier, later):
    return (earlier[0] * later[0], later[0] * earlier[1] + later[1])


def weight_view(gathered):
    return gathered.reshape(2, gathered.shape[0] // 2, gathered.shape[1] * gathered.shape[2])


def span_prefix(product, offset):
    identity = (jnp.ones_like(product), jnp.zeros_like(offset))
    result = prefix((product, offset), "tm", affine_join, identity, False)
    return result[1]


def span_suffix(product, offset):
    identity = (jnp.ones_like(product), jnp.zeros_like(offset))
    result = prefix((product, offset), "tm", affine_join, identity, True)
    return result[1]


def forward_layer(layer_in, view, bias):
    seq_count, length, channels = layer_in.shape
    prev_row = passed_along(layer_in[:, length - 1 :], "tm", 1)
    previous = jnp.concatenate([prev_row, layer_in[:, : length - 1]], axis=1)
    stacked = jnp.stack([previous, layer_in])
    summed = jnp.einsum(
        "jsck,jkn->scn",
        lax.all_gather(stacked, "mp", axis=3, tiled=True),
        view,
        preferred_element_type=jnp.float32,
    )
    gates = summed.reshape(seq_count, length, 3, channels) + bias
    candidate = jnp.tanh(gates[:, :, 0])
    forget = jax.nn.sigmoid(gates[:, :, 1])
    outgate = jax.nn.sigmoid(gates[:, :, 2])
    product, offset = lax.associative_scan(
        affine_join, (forget, (1.0 - forget) * candidate), axis=1
    )
    carry_in = span_prefix(product[:, length - 1], offset[:, length - 1])
    cells = offset + product * carry_in[:, None]
    cells_prev = jnp.concatenate([carry_in[:, None], cells[:, : length - 1]], axis=1)
    return (outgate * cells, (stacked, candidate, forget, outgate, cells, cells_prev))


def backward_layer(grad_in, saved, view):
    stacked, candidate, forget, outgate, cells, cells_prev = saved
    seq_count, length, channels = grad_in.shape
    driven = grad_in * outgate
    next_forget = jnp.concatenate([forget[:, 1:], jnp.ones_like(forget[:, :1])], axis=1)
    reach, local_adj = lax.associative_scan(
        affine_join, (next_forget[:, ::-1], driven[:, ::-1]), axis=1
    )
    reach = reach[:, ::-1]
    local_adj = local_adj[:, ::-1]
    first_forget = forget[:, 0]
    incoming = span_suffix(first_forget * reach[:, 0], first_forget * local_adj[:, 0])
    adjoint = local_adj + reach * incoming[:, None]
    grad_cand = adjoint * (1.0 - forget) * (1.0 - candidate * candidate)
    grad_forget = adjoint * (cells_prev - candidate) * forget * (1.0 - forget)
    grad_outgate = grad_in * cells * outgate * (1.0 - outgate)
    gate_grad = jnp.stack([grad_cand, grad_forget, grad_outgate], axis=2).astype(jnp.bfloat16)
    flat_grad = gate_grad.reshape(seq_count, length, 3 * channels)
    bias_part = jnp.sum(gate_grad, axis=(0, 1), dtype=jnp.float32)
    back_both = jnp.einsum("scn,jkn->jsck", flat_grad, view, preferred_element_type=jnp.float32)
    from_prev = back_both[0]
    from_current = back_both[1]
    local_grad = from_current + jnp.concatenate(
        [from_prev[:, 1:], jnp.zeros_like(from_prev[:, :1])], axis=1
    )
    tail_rows = from_prev[:, :1]
    shard_grad, tail_shard = (
        lax.psum_scatter(local_grad, "mp", scatter_dimension=2, tiled=True),
        lax.psum_scatter(tail_rows, "mp", scatter_dimension=2, tiled=True),
    )
    tail_next = passed_along(tail_shard, "tm", -1)
    layer_grad = shard_grad + jnp.concatenate(
        [jnp.zeros_like(shard_grad[:, : length - 1]), tail_next], axis=1
    )
    weight_full = jnp.einsum(
        "jsck,scn->jkn",
        lax.all_gather(stacked, "mp", axis=3, tiled=True),
        flat_grad,
        preferred_element_type=jnp.float32,
    )
    weight_full = weight_full.reshape(2 * weight_full.shape[1], 3, channels)
    weight_shard = lax.psum_scatter(weight_full, "tm", scatter_dimension=0, tiled=True)
    bias_grad = lax.psum(bias_part, "tm")
    return (layer_grad, weight_shard, bias_grad)


def per_device(inputs, first_weight, first_bias, second_weight, second_bias, cotangent):
    full_first, full_second = (
        lax.all_gather(first_weight, "tm", axis=0, tiled=True),
        lax.all_gather(second_weight, "tm", axis=0, tiled=True),
    )
    view_first = weight_view(full_first)
    view_second = weight_view(full_second)
    hidden_out, saved_first = forward_layer(inputs, view_first, first_bias)
    hidden = hidden_out.astype(jnp.bfloat16)
    top_out, saved_second = forward_layer(hidden, view_second, second_bias)
    again_first, again_second = (
        lax.all_gather(first_weight, "tm", axis=0, tiled=True),
        lax.all_gather(second_weight, "tm", axis=0, tiled=True),
    )
    back_first = weight_view(again_first)
    back_second = weight_view(again_second)
    hidden_grad, second_weightgrad, second_biasgrad = backward_layer(
        cotangent.astype(jnp.float32), saved_second, back_second
    )
    input_grad, first_weightgrad, first_biasgrad = backward_layer(
        hidden_grad, saved_first, back_first
    )
    return (
        top_out.astype(jnp.bfloat16),
        input_grad,
        first_weightgrad,
        first_biasgrad,
        second_weightgrad,
        second_biasgrad,
    )


def solution(mesh):
    placed = (
        P(None, "tm", "mp"),
        P("tm", None, "mp"),
        P(None, "mp"),
        P("tm", None, "mp"),
        P(None, "mp"),
        P(None, "tm", "mp"),
    )
    return jax.shard_map(
        per_device,
        mesh=mesh,
        in_specs=placed,
        out_specs=(
            P(None, "tm", "mp"),
            P(None, "tm", "mp"),
            P("tm", None, "mp"),
            P(None, "mp"),
            P("tm", None, "mp"),
            P(None, "mp"),
        ),
        check_vma=False,
    )
```

profile of v0, /device:TPU:8, one launch (start us, length us, event | category | flops | bytes accessed | tf_op | source)
XLA Modules:
  0.0 3953.6 jit_solution(12734370376274467602)
XLA Ops:
  21.7 22.9 all-gather.5.cloned.1.call-done
  51.4 335.2 %all-gather.7.cloned.1.call-done = bf16[4608,3,576]{2,0,1:T(8,128)(2,1)} async-done(((bf16[576,3,576]{2,0,1:T(8,128)(2,1)}), bf16[4608,3,576]{2,0,1:T(8,128)(2,1)}) %all-gather.7.cloned.1.call-update) | async-done | bytes 15925264 | tf_op jit(solution)/shard_map/all_gather | solution.py:122
  386.6 22.8 copy.372
  409.4 21.3 reshape.565
  844.7 27.8 all_gather.46
  872.5 30.3 all_gather.47
  914.6 23.0 copy.389
  937.6 21.2 reshape.567
  1009.8 13.4 slice.1144
  1884.3 28.5 all_gather.50
  1942.6 31.5 all_gather.51
  1995.3 32.0 all_gather.52
  2029.7 32.0 all_gather.53
  2072.9 14.6 fusion.8
  2096.7 24.4 reduce-scatter.16.cloned.1.call-done
  2126.7 13.5 slice.1303
  2367.1 13.4 slice.1365
  2618.4 28.6 all_gather.54
  2649.5 31.8 all_gather.55
  2719.0 15.2 fusion.25
  2736.3 14.5 fusion.27
  2760.3 32.2 all-reduce.137
  2797.5 573.2 %reduce-scatter.14.cloned.1.call-done = f32[576,3,576]{2,0,1:T(8,128)} async-done(((f32[4608,3,576]{2,0,1:T(8,128)}), f32[576,3,576]{2,0,1:T(8,128)}) %reduce-scatter.14.cloned.1.call-update) | async-done | bytes 3981328 | tf_op jit(solution)/shard_map/reduce_scatter | solution.py:115
  3370.7 575.6 %reduce-scatter.12.cloned.1.call-done = f32[576,3,576]{2,0,1:T(8,128)} async-done(((f32[4608,3,576]{2,0,1:T(8,128)}), f32[576,3,576]{2,0,1:T(8,128)}) %reduce-scatter.12.cloned.1.call-update) | async-done | bytes 3981328 | tf_op jit(solution)/shard_map/reduce_scatter | solution.py:115
  (772 shorter events, 1973.3 us)
Async XLA Ops:
  7.2 37.5 all-gather.5.cloned.1.call-start
  8.2 8.4 collective-permute-start
  20.2 366.4 %all-gather.7.cloned.1.call-start = ((), (), s32[]{:S(2)}) async-start(), calls=%async_computation.6 | async-start | bytes 19906560 | tf_op jit(solution)/shard_map/all_gather | solution.py:122
  21.0 893.6 %all-gather.11.cloned.1.call-start = ((), (), s32[]{:S(2)}) async-start(), calls=%async_computation.8 | async-start | bytes 19906560 | tf_op jit(solution)/shard_map/all_gather | solution.py:123
  21.7 937.1 %all-gather.9.cloned.1.call-start = ((), (), s32[]{:S(2)}) async-start(), calls=%async_computation.7 | async-start | bytes 2949120 | tf_op jit(solution)/shard_map/all_gather | solution.py:57
  409.4 21.3 copy-start.52
  441.8 11.8 copy-start.30
  465.6 190.5 %copy-start.1 = (f32[1,256,576]{1,2,0:T(8,128)}, f32[1,256,576]{1,2,0:T(8,128)S(1)}, u32[]{:S(2)}) copy-start(f32[1,256,576]{1,2,0:T(8,128)S(1)} %fusion.45) | copy-start | bytes 1769476
  680.4 16.9 copy-start.17
  702.9 13.2 copy-start.14
  726.6 15.7 copy-start.10
  805.9 14.5 copy-start.48
  805.9 25.9 slice-start.1
  805.9 25.9 copy-start.46
  832.0 71.1 %copy-start.37 = (f32[1,256,576]{1,2,0:T(8,128)S(1)}, f32[1,256,576]{1,2,0:T(8,128)}, u32[]{:S(2)}) copy-start(f32[1,256,576]{1,2,0:T(8,128)} %pad.415) | copy-start | bytes 1769476
  905.5 7.9 collective-permute-start.1
  914.5 1206.7 %reduce-scatter.16.cloned.1.call-start = ((), (), s32[]{:S(2)}) async-start(), calls=%async_computation.12 | async-start | bytes 1474560
  2092.5 84.5 %reduce-scatter.10.cloned.1.call-start = ((), (), s32[]{:S(2)}) async-start(), calls=%async_computation.9 | async-start | bytes 2949120 | tf_op jit(solution)/shard_map/reduce_scatter | solution.py:101
  2096.7 656.9 %reduce-scatter.18.cloned.1.call-start = ((), (), s32[]{:S(2)}) async-start(), calls=%async_computation.13 | async-start | bytes 1474560
  2121.2 55.9 %collective-permute-start.2 = (f32[1,1,576]{1,2,0:T(8,128)}, f32[1,1,576]{1,2,0:T(8,128)}, u32[]{:S(2)}, u32[]{:S(2)}) collective-permute-start(f32[1,1,576]{1,2,0:T(8,128)} %bitcast.334), channel_id=1, source_target_pairs={{4,0},{8,4},{12,8},{16,12},{20,16},{24,20},{28,24},{5,1},{9,5},{13... | collective-permute-start | bytes 6920 | tf_op jit(solution)/shard_map/ppermute | solution.py:27
  2707.3 87.5 %all-reduce.140.cloned.1.call-start = ((), (), s32[]{:S(2)}) async-start(), calls=%async_computation.14 | async-start | bytes 4718592
  2717.8 652.9 %reduce-scatter.14.cloned.1.call-start = ((), (), s32[]{:S(2)}) async-start(), calls=%async_computation.11 | async-start | bytes 39813120 | tf_op jit(solution)/shard_map/reduce_scatter | solution.py:115
  2734.2 1212.1 %reduce-scatter.12.cloned.1.call-start = ((), (), s32[]{:S(2)}) async-start(), calls=%async_computation.10 | async-start | bytes 39813120 | tf_op jit(solution)/shard_map/reduce_scatter | solution.py:115
  2753.6 38.9 collective-permute-start.3
  (46 other events, 209.7 us)
Sparse Core Ops, SparseCore 0:
  20.3 24.3 all-gather.4
  46.2 340.2 all-gather.6
  388.1 340.3 all-gather.10
  914.6 25.3 all-gather.8
  2092.7 28.4 reduce-scatter.15
  2124.3 33.0 reduce-scatter.9
  2707.4 29.1 reduce-scatter.17
  2739.1 55.6 all-reduce.139
  2799.7 570.9 reduce-scatter.13
  3375.0 571.1 reduce-scatter.11
where the time goes:
time: 3990 us; the launch traced here: 3950 us
  local copies, waits for them, and re-layouts  1690 us (42%)
  waiting for transfers between devices  1550 us (39%)
  other arithmetic  335 us (8%)
  blocking collectives  275 us (7%)
  matrix products  74.4 us (2%)
    reduce_scatter x2, waiting for transfers between devices, backward_layer(): lax.psum_scatter(weight_full, 'tm', scatter_dimension=0, tiled=True)  1150 us
    slice x96, local copies, waits for them, and re-layouts, backward_layer(): lax.associative_scan(affine_join, (next_forget[:, ::-1], driven[:, ::-1])...  477 us
    slice x86, local copies, waits for them, and re-layouts, forward_layer(): lax.associative_scan(affine_join, (forget, (1.0 - forget) * candidate), a...  422 us
    all_gather x1, waiting for transfers between devices, per_device(): lax.all_gather(first_weight, 'tm', axis=0, tiled=True)  335 us
    pad x56, local copies, waits for them, and re-layouts, backward_layer(): lax.associative_scan(affine_join, (next_forget[:, ::-1], driven[:, ::-1])...  292 us
    pad x56, local copies, waits for them, and re-layouts, forward_layer(): lax.associative_scan(affine_join, (forget, (1.0 - forget) * candidate), a...  268 us
    all_gather x8, blocking collectives, prefix(): pieces = jax.tree.map(lambda part: lax.all_gather(part, axis), value)  242 us
  transfers between devices with their start and end apart: 14, of which 8 were waited for; matrix products, arithmetic and copies ran while one was open for 16% of the time, Pallas kernels for 0%

commit v1 on v0

--- a/solution.py
+++ b/solution.py
@@ -1,7 +1,543 @@
 import jax
 import jax.numpy as jnp
 from jax import lax
+from jax.experimental import pallas as pl
+from jax.experimental.pallas import tpu as pltpu
 from jax.sharding import PartitionSpec as P
+
+BF = jnp.bfloat16
+F32 = jnp.float32
+LANES = 128
+MIB = 2**20
+
+NZ = 4
+
+
+def mod(value):
+    return lax.rem(value + NZ, NZ)
+
+
+def flip(bit, by):
+    return bit if by == 0 else 1 - bit
+
+
+def moved(array, target):
+    pairs = []
+    for z in range(NZ):
+        for x in range(2):
+            for y in range(2):
+                for c in range(2):
+                    tz, tx, ty, tc = target(z, x, y, c)
+                    pairs.append(((z * 2 + x) * 4 + y * 2 + c, (tz * 2 + tx) * 4 + ty * 2 + tc))
+    return lax.ppermute(array, ("tm", "mp"), pairs)
+
+
+def over_x(array):
+    return moved(array, lambda z, x, y, c: (z, 1 - x, y, c))
+
+
+def over_y(array):
+    return moved(array, lambda z, x, y, c: (z, x, 1 - y, c))
+
+
+def over_core(array):
+    return moved(array, lambda z, x, y, c: (z, x, y, 1 - c))
+
+
+def over_z(array):
+    return moved(array, lambda z, x, y, c: ((z + 1) % NZ, x, y, c))
+
+
+def call(body, outs, args, scratch=(), vmem=48):
+    whole = pl.BlockSpec(memory_space=pltpu.VMEM)
+    specs = [pl.BlockSpec(memory_space=pltpu.SMEM)] + [whole] * (len(args) - 1)
+    return pl.pallas_call(
+        body,
+        out_shape=[jax.ShapeDtypeStruct(shape, kind) for shape, kind in outs],
+        in_specs=specs,
+        out_specs=[whole] * len(outs),
+        scratch_shapes=list(scratch),
+        compiler_params=pltpu.CompilerParams(vmem_limit_bytes=vmem * MIB),
+    )(*args)
+
+
+def pack_weight(ids, weight):
+    rows, gates, columns = weight.shape
+    own = columns // 8
+
+    def body(ids, w, *rest):
+        outs, turned = rest[:8], rest[8]
+        z, c = ids[0], ids[3]
+        for g in range(gates):
+            turned[...] = w[g].astype(F32).T
+            for dz in range(NZ):
+                for r in range(2):
+                    i = mod(z + dz) * 2 + flip(c, r)
+                    outs[dz * 2 + r][g] = turned[pl.ds(pl.multiple_of(i * own, 8), own)].astype(BF)
+
+    return call(
+        body,
+        [((gates, own, rows), BF)] * 8,
+        [ids, jnp.transpose(weight, (1, 0, 2))],
+        [pltpu.VMEM((columns, rows), F32)],
+    )
+
+
+def send_blocks(blocks):
+    return [
+        moved(blocks[dz * 2 + r], lambda z, x, y, c, dz=dz, r=r: ((z + dz) % NZ, c ^ r, y, x))
+        for dz in range(NZ)
+        for r in range(2)
+    ]
+
+
+def return_blocks(blocks):
+    def back(dz, r):
+        return lambda z, x, y, c: ((z - dz) % NZ, c, y, x ^ r)
+
+    return [moved(blocks[dz * 2 + r], back(dz, r)) for dz in range(NZ) for r in range(2)]
+
+
+def join_weight(ids, blocks):
+    gates, own, rows = blocks[0].shape
+    part = gates * own
+
+    def body(ids, *rest):
+        ins, (wide, tall), joined = rest[:8], rest[8:10], rest[10]
+        z, x = ids[0], ids[1]
+        for dz in range(NZ):
+            for r in range(2):
+                source = mod(z - dz)
+                base = (flip(x, r) * 2 + source // 2) * part
+                for g in range(gates):
+                    at = pl.ds(pl.multiple_of(base + g * own, 8), own)
+                    joined[lax.rem(source, 2), at, :] = ins[dz * 2 + r][g].astype(F32)
+        for half in range(2):
+            at = pl.ds(half * 2 * part, 2 * part)
+            both = jnp.concatenate([joined[0, at, :], joined[1, at, :]], axis=1)
+            wide[at, :] = both.astype(BF)
+        for y in range(2):
+            tall[pl.ds(y * rows, rows), :] = joined[y].T.astype(BF)
+
+    return call(
+        body,
+        [((4 * part, 2 * rows), BF), ((2 * rows, 4 * part), BF)],
+        [ids, *blocks],
+        [pltpu.VMEM((2, 4 * part, rows), F32)],
+    )
+
+
+def halves(array, axis):
+    half = array.shape[axis] // 2
+    return lax.slice_in_dim(array, 0, half, axis=axis), lax.slice_in_dim(array, half, 2 * half, axis=axis)
+
+
+def gather_chips(piece, axis):
+    found = []
+    for dz in range(NZ):
+        if dz:
+            piece = over_z(piece)
+        from_x, from_y = over_x(piece), over_y(piece)
+        found += [piece, from_x, from_y, over_y(halves(from_x, axis)[0]), over_x(halves(from_y, axis)[1])]
+    return found
+
+
+def sum_chips(parts, axis):
+    running = None
+    for step in range(NZ):
+        own, to_x, to_y, diag_a, diag_b = parts[5 * step : 5 * step + 5]
+        at_x, at_y = over_y(diag_a), over_x(diag_b)
+        xa, xb = halves(to_x, axis)
+        ya, yb = halves(to_y, axis)
+        sent_x = jnp.concatenate([(xa + at_x).astype(BF), xb.astype(BF)], axis=axis)
+        sent_y = jnp.concatenate([ya.astype(BF), (yb + at_y).astype(BF)], axis=axis)
+        plane = own + over_x(sent_x) + over_y(sent_y)
+        if running is not None:
+            plane = plane + over_z(running.astype(BF))
+        running = plane
+    return running
+
+
+def partial_gates(ids, wide, found, channel_pieces):
+    total, depth = wide.shape
+    part = total // 4
+    rows = depth // 2
+    if channel_pieces:
+        own, length = found[0].shape
+    else:
+        length = found[0].shape[1] * 8
+    span = 512
+
+    def body(ids, w, *rest):
+        ins, (u, mine, theirs), (prev, cur) = rest[:20], rest[20:23], rest[23:]
+        z, x, y, c = ids[0], ids[1], ids[2], ids[3]
+        for dz in range(NZ):
+            near, at_x, at_y, diag_a, diag_b = ins[5 * dz : 5 * dz + 5]
+            source = mod(z - dz)
+            if channel_pieces:
+                half = length // 2
+                for other in range(2):
+                    row = pl.multiple_of(flip(y, other) * rows + source * 2 * own, 16)
+                    for k in range(2):
+                        cols = pl.ds(k * half, half)
+                        if other:
+                            a, b = at_y[:, cols], (diag_a, diag_b)[k][...]
+                        else:
+                            a, b = near[:, cols], at_x[:, cols]
+                        a, b = a.astype(F32), b.astype(F32)
+                        pair = jnp.concatenate([jnp.where(x == 0, a, b), jnp.where(x == 0, b, a)], axis=0)
+                        u[pl.ds(row, 2 * own), cols] = pair.astype(BF)
+            else:
+                block = length // 8
+                here = pl.ds(pl.multiple_of((source * 2 + x) * block, block), block)
+                there = pl.ds(pl.multiple_of((source * 2 + 1 - x) * block, block), block)
+                top = pl.multiple_of(y * rows, 16)
+                low = pl.multiple_of((1 - y) * rows, 16)
+                u[pl.ds(top, rows), here] = near[...]
+                u[pl.ds(top, rows), there] = at_x[...]
+                u[pl.ds(low, rows), here] = at_y[...]
+                u[pl.ds(low, rows // 2), there] = diag_a[...]
+                u[pl.ds(pl.multiple_of(low + rows // 2, 16), rows // 2), there] = diag_b[...]
+        for start in range(0, length, span):
+            cols = pl.ds(start, span)
+            made = jnp.dot(w[...], u[:, cols], preferred_element_type=F32)
+            for core in range(2):
+                prev[core, :, cols] = made[2 * core * part : (2 * core + 1) * part]
+                cur[core, :, cols] = made[(2 * core + 1) * part : (2 * core + 2) * part]
+        first = lax.broadcasted_iota(jnp.int32, (part, length), 1) == 0
+        for out, core in ((mine, c), (theirs, 1 - c)):
+            out[...] = cur[core] + jnp.where(first, 0.0, pltpu.roll(prev[core], 1, 1))
+
+    return call(
+        body,
+        [((depth, length), BF), ((part, length), F32), ((part, length), F32)],
+        [ids, wide, *found],
+        [pltpu.VMEM((2, part, length), F32), pltpu.VMEM((2, part, length), F32)],
+    )
+
+
+def scan_lanes(forget, driven, backward):
+    own, length = driven.shape
+    lane = lax.broadcasted_iota(jnp.int32, (own, LANES), 1)
+    count = length // LANES
+    blocks = [None] * count
+    carry = jnp.zeros((own, 1), F32)
+    for block in range(count)[:: -1 if backward else 1]:
+        cols = slice(block * LANES, (block + 1) * LANES)
+        reach, state = forget[:, cols], driven[:, cols]
+        by = 1
+        while by < LANES:
+            shift = LANES - by if backward else by
+            inside = lane < LANES - by if backward else lane >= by
+            state = state + jnp.where(inside, reach * pltpu.roll(state, shift, 1), 0.0)
+            reach = jnp.where(inside, reach * pltpu.roll(reach, shift, 1), reach)
+            by *= 2
+        state = state + reach * carry
+        carry = state[:, :1] if backward else state[:, LANES - 1 :]
+        blocks[block] = state
+    return blocks
+
+
+def squash(value):
+    return 1.0 / (1.0 + jnp.exp(-value))
+
+
+def activate(mine, theirs, bias, own):
+    gates = [
+        mine[pl.ds(g * own, own), :] + theirs[pl.ds(g * own, own), :] + bias[pl.ds(g * own, own), :]
+        for g in range(3)
+    ]
+    return jnp.tanh(gates[0]), squash(gates[1]), squash(gates[2])
+
+
+def put_blocks(ref, blocks):
+    for at, block in enumerate(blocks):
+        ref[:, pl.ds(at * LANES, LANES)] = block
+
+
+def gate_gradients(grad, candidate, forget, outgate, cells, adjoint, wide, gate_grad, bias_grad):
+    own, length = grad.shape
+    driven = grad[...] * outgate[...]
+    last = lax.broadcasted_iota(jnp.int32, (own, length), 1) == length - 1
+    later = jnp.where(last, 0.0, pltpu.roll(forget[...], length - 1, 1))
+    put_blocks(adjoint, scan_lanes(later, driven, True))
+    f, a = forget[...], candidate[...]
+    away = 1.0 - f
+    before = jnp.where(
+        lax.broadcasted_iota(jnp.int32, (own, length), 1) == 0, 0.0, pltpu.roll(cells[...], 1, 1)
+    )
+    wide[pl.ds(0, own), :] = adjoint[...] * away * (1.0 - a * a)
+    wide[pl.ds(own, own), :] = adjoint[...] * (before - a) * f * away
+    o = outgate[...]
+    wide[pl.ds(2 * own, own), :] = grad[...] * cells[...] * o * (1.0 - o)
+    rounded = wide[...].astype(BF)
+    gate_grad[...] = rounded
+    total = jnp.sum(rounded.astype(F32), axis=1, keepdims=True)
+    bias_grad[...] = jnp.broadcast_to(total, bias_grad.shape)
+
+
+def first_cells(ids, mine, theirs, bias):
+    part, length = mine.shape
+    own = part // 3
+
+    def body(ids, mine, theirs, bias, hidden, cand, forg, outg, cells):
+        candidate, forget, outgate = activate(mine, theirs, bias, own)
+        cand[...], forg[...], outg[...] = candidate, forget, outgate
+        put_blocks(cells, scan_lanes(forget, (1.0 - forget) * candidate, False))
+        hidden[...] = (outgate * cells[...]).astype(BF)
+
+    return call(
+        body,
+        [((own, length), BF)] + [((own, length), F32)] * 4,
+        [ids, mine, theirs, bias],
+    )
+
+
+def first_gate_grad(ids, grad, saved):
+    own, length = grad.shape
+
+    def body(ids, grad, cand, forg, outg, cells, gate_grad, bias_grad, adjoint, wide):
+        gate_gradients(grad, cand, forg, outg, cells, adjoint, wide, gate_grad, bias_grad)
+
+    return call(
+        body,
+        [((3 * own, length), BF), ((3 * own, LANES), F32)],
+        [ids, grad, *saved],
+        [pltpu.VMEM((own, length), F32), pltpu.VMEM((3 * own, length), F32)],
+    )
+
+
+def second_cells(ids, mine, theirs, bias, cot_pieces):
+    part, length = mine.shape
+    own = part // 3
+    block = length // 8
+
+    def body(ids, mine, theirs, bias, *rest):
+        cots, outs = rest[:8], rest[8:16]
+        gate_grad, bias_grad = rest[16:18]
+        grad, cand, forg, outg, cells, adjoint, wide = rest[18:]
+        z, x = ids[0], ids[1]
+        for dz in range(NZ):
+            for dx in range(2):
+                i = mod(z - dz) * 2 + flip(x, dx)
+                grad[:, pl.ds(pl.multiple_of(i * block, block), block)] = cots[dz * 2 + dx][...].astype(F32)
+        candidate, forget, outgate = activate(mine, theirs, bias, own)
+        cand[...], forg[...], outg[...] = candidate, forget, outgate
+        put_blocks(cells, scan_lanes(forget, (1.0 - forget) * candidate, False))
+        adjoint[...] = outgate * cells[...]
+        for dz in range(NZ):
+            for dx in range(2):
+                i = mod(z + dz) * 2 + flip(x, dx)
+                piece = adjoint[:, pl.ds(pl.multiple_of(i * block, block), block)]
+                outs[dz * 2 + dx][...] = piece.astype(BF)
+        gate_gradients(grad, cand, forg, outg, cells, adjoint, wide, gate_grad, bias_grad)
+
+    made = call(
+        body,
+        [((own, block), BF)] * 8 + [((part, length), BF), ((part, LANES), F32)],
+        [ids, mine, theirs, bias, *cot_pieces],
+        [pltpu.VMEM((own, length), F32)] * 6 + [pltpu.VMEM((part, length), F32)],
+    )
+    return made[:8], made[8], made[9]
+
+
+def split_cotangent(ids, cotangent):
+    channels, block = cotangent.shape
+    own = channels // 8
+
+    def body(ids, cot, *rest):
+        outs, wide = rest[:8], rest[8]
+        wide[...] = cot[...].astype(F32)
+        for dz in range(NZ):
+            for dx in range(2):
+                i = mod(ids[0] + dz) * 2 + flip(ids[1], dx)
+                outs[dz * 2 + dx][...] = wide[pl.ds(pl.multiple_of(i * own, 8), own), :].astype(BF)
+
+    return call(body, [((own, block), BF)] * 8, [ids, cotangent], [pltpu.VMEM((channels, block), F32)])
+
+
+def over_tm(pieces):
+    return [
+        pieces[dz * 2 + dx]
+        if dz == 0 and dx == 0
+        else moved(pieces[dz * 2 + dx], lambda z, x, y, c, dz=dz, dx=dx: ((z + dz) % NZ, x ^ dx, y, c))
+        for dz in range(NZ)
+        for dx in range(2)
+    ]
+
+
+def join_outputs(ids, pieces):
+    own, block = pieces[0].shape
+
+    def body(ids, *rest):
+        ins, out, wide = rest[:8], rest[8], rest[9]
+        for dz in range(NZ):
+            for dx in range(2):
+                i = mod(ids[0] - dz) * 2 + flip(ids[1], dx)
+                wide[pl.ds(pl.multiple_of(i * own, 8), own), :] = ins[dz * 2 + dx][...].astype(F32)
+        out[...] = wide[...].astype(BF)
+
+    return call(body, [((8 * own, block), BF)], [ids, *pieces], [pltpu.VMEM((8 * own, block), F32)])[0]
+
+
+def input_parts(ids, tall, mine, theirs, channel_pieces):
+    depth, total = tall.shape
+    part, length = mine.shape
+    rows = depth // 2
+    own = rows // 8
+    block = length // 8
+    span = 512
+    shape = (own, length) if channel_pieces else (rows, block)
+    half = (own, length // 2) if channel_pieces else (rows // 2, block)
+
+    def body(ids, w, mine, theirs, grads, *rest):
+        outs, v = rest[:20], rest[20]
+        z, x, y, c = ids[0], ids[1], ids[2], ids[3]
+        last = lax.broadcasted_iota(jnp.int32, (part, length), 1) == length - 1
+        for core in range(2):
+            now = jnp.where(c == core, mine[...].astype(F32), theirs[...].astype(F32))
+            after = jnp.where(last, 0.0, pltpu.roll(now, length - 1, 1))
+            grads[pl.ds(core * 2 * part, 2 * part), :] = jnp.concatenate([after, now], axis=0).astype(BF)
+        for start in range(0, length, span):
+            cols = pl.ds(start, span)
+            v[:, cols] = jnp.dot(w[...], grads[:, cols], preferred_element_type=F32)
+        for step in range(NZ):
+            target = mod(z - 1 - step)
+
+            def piece(dx, dy, k=None):
+                i = target * 2 + flip(x, dx)
+                if channel_pieces:
+                    row = pl.multiple_of(flip(y, dy) * rows + i * own, 8)
+                    cols = slice(None) if k is None else pl.ds(k * length // 2, length // 2)
+                    return v[pl.ds(row, own), cols]
+                cols = pl.ds(pl.multiple_of(i * block, block), block)
+                row = flip(y, dy) * rows
+                if k is None:
+                    return v[pl.ds(pl.multiple_of(row, 8), rows), cols]
+                return v[pl.ds(pl.multiple_of(row + k * rows // 2, 8), rows // 2), cols]
+
+            o = outs[5 * step : 5 * step + 5]
+            o[0][...] = piece(0, 0)
+            o[1][...] = piece(1, 0)
+            o[2][...] = piece(0, 1)
+            o[3][...] = piece(1, 1, 0).astype(BF)
+            o[4][...] = piece(1, 1, 1).astype(BF)
+
+    made = call(
+        body,
+        [((total, length), BF)] + [(shape, F32), (shape, F32), (shape, F32), (half, BF), (half, BF)] * NZ,
+        [ids, tall, mine, theirs],
+        [pltpu.VMEM((depth, length), F32)],
+    )
+    return made[0], made[1:]
+
+
+def weight_blocks(ids, grads, u, bias_mine, bias_theirs):
+    total, length = grads.shape
+    depth = u.shape[0]
+    part, rows = total // 4, depth // 2
+    lanes = -(-(rows + 2) // LANES) * LANES
+
+    def body(ids, grads, u, bias_mine, bias_theirs, *rest):
+        outs, made = rest[:8], rest[8]
+        z, x, c = ids[0], ids[1], ids[3]
+        for y in range(2):
+            made[y, :, pl.ds(0, rows)] = lax.dot_general(
+                grads[...], u[pl.ds(y * rows, rows), :], (((1,), (1,)), ((), ())), preferred_element_type=F32
+            )
+        lane = lax.broadcasted_iota(jnp.int32, (part, lanes), 1)
+        for r in range(2):
+            core = flip(x, r)
+            bias = jnp.where(core == c, bias_mine[:, :1], bias_theirs[:, :1])
+            high = bias.astype(BF).astype(F32)
+            for dz in range(NZ):
+                source = mod(z - dz)
+                at = pl.ds(pl.multiple_of((core * 2 + source // 2) * part, 8), part)
+                block = made[lax.rem(source, 2), at, :]
+                block = jnp.where(lane < rows, block, jnp.where(lane == rows, high, bias - high))
+                outs[dz * 2 + r][...] = block.astype(BF)
+
+    return call(
+        body,
+        [((part, lanes), BF)] * 8,
+        [ids, grads, u, bias_mine, bias_theirs],
+        [pltpu.VMEM((2, total, lanes), F32)],
+    )
+
+
+def unpack_weight(ids, blocks, rows):
+    part, lanes = blocks[0].shape
+    own = part // 3
+    columns = own * 8
+
+    def body(ids, *rest):
+        ins, (out, bias), joined = rest[:8], rest[8:10], rest[10]
+        z, c = ids[0], ids[3]
+        for dz in range(NZ):
+            for r in range(2):
+                i = mod(z + dz) * 2 + flip(c, r)
+                for g in range(3):
+                    at = pl.ds(pl.multiple_of(i * own, 8), own)
+                    joined[g, at, :] = ins[dz * 2 + r][pl.ds(g * own, own), :].astype(F32)
+        for g in range(3):
+            turned = joined[g].T
+            out[g] = turned[:rows]
+            bias[pl.ds(g, 1), :] = turned[rows : rows + 1] + turned[rows + 1 : rows + 2]
+
+    grad, bias = call(
+        body,
+        [((3, rows, columns), F32), ((3, columns), F32)],
+        [ids, *blocks],
+        [pltpu.VMEM((3, columns, lanes), F32)],
+    )
+    return jnp.transpose(grad, (1, 0, 2)), bias
+
+
+def owned_bias(bias, own):
+    i = lax.axis_index("tm")
+    return lax.dynamic_slice_in_dim(bias, i * own, own, axis=1).reshape(3 * own, 1)
+
+
+def owned_channels(inputs, first_weight, first_bias, second_weight, second_bias, cotangent):
+    tm, mp = lax.axis_index("tm"), lax.axis_index("mp")
+    ids = jnp.stack([tm // 2, tm % 2, mp // 2, mp % 2]).astype(jnp.int32)
+    rows = first_weight.shape[0]
+    own = first_weight.shape[2] // 8
+
+    w1_sent = send_blocks(pack_weight(ids, first_weight))
+    u_found = gather_chips(inputs[0].T, 0)
+    wide_1, tall_1 = join_weight(ids, w1_sent)
+    w2_sent = send_blocks(pack_weight(ids, second_weight))
+    cot_pieces = over_tm(split_cotangent(ids, cotangent[0].T))
+
+    u, mine, theirs = partial_gates(ids, wide_1, u_found, False)
+    hidden, *saved = first_cells(ids, mine, over_core(theirs), owned_bias(first_bias, own))
+    wide_2, tall_2 = join_weight(ids, w2_sent)
+    h_found = gather_chips(hidden, 1)
+    h, mine, theirs = partial_gates(ids, wide_2, h_found, True)
+    out_pieces, gate_grad, bias_2 = second_cells(
+        ids, mine, over_core(theirs), owned_bias(second_bias, own), cot_pieces
+    )
+    outputs = join_outputs(ids, over_tm(out_pieces))
+
+    grads, parts = input_parts(ids, tall_2, gate_grad, over_core(gate_grad), True)
+    hidden_grad = sum_chips(parts, 1)
+    blocks = weight_blocks(ids, grads, h, bias_2, over_core(bias_2))
+    second_grad, second_bias_grad = unpack_weight(ids, return_blocks(blocks), rows)
+
+    gate_grad, bias_1 = first_gate_grad(ids, hidden_grad, saved)
+    grads, parts = input_parts(ids, tall_1, gate_grad, over_core(gate_grad), False)
+    input_grad = sum_chips(parts, 0)
+    blocks = weight_blocks(ids, grads, u, bias_1, over_core(bias_1))
+    first_grad, first_bias_grad = unpack_weight(ids, return_blocks(blocks), rows)
+    return (
+        outputs.T[None],
+        input_grad.T[None],
+        first_grad,
+        first_bias_grad,
+        second_grad,
+        second_bias_grad,
+    )
 
 
 def prefix(value, axis, join, neutral, backward):
@@ -149,6 +685,15 @@
     )
 
 
+def choose(owned):
+    def run(inputs, first_weight, *rest):
+        sizes = inputs.shape[0] == 1 and inputs.shape[1] == 256 and first_weight.shape == (576, 3, 576)
+        plan = owned_channels if owned and sizes else per_device
+        return plan(inputs, first_weight, *rest)
+
+    return run
+
+
 def solution(mesh):
     placed = (
         P(None, "tm", "mp"),
@@ -158,8 +703,9 @@
         P(None, "mp"),
         P(None, "tm", "mp"),
     )
+    owned = mesh.shape["tm"] == 2 * NZ and mesh.shape["mp"] == 4
     return jax.shard_map(
-        per_device,
+        choose(owned),
         mesh=mesh,
         in_specs=placed,
         out_specs=(

time: 3990 us -> 545 us (0.14)
  local copies, waits for them, and re-layouts: 1690 us -> 20.9 us
  waiting for transfers between devices: 1550 us -> 184 us
  other arithmetic: 335 us -> 3.67 us
  blocking collectives: 275 us -> 0 us
  starting transfers between devices: 15.9 us -> 218 us
  Pallas kernels: 0 us -> 109 us
  matrix products: 74.4 us -> 0 us
    reduce_scatter x3 -> x0, waiting for transfers between devices: 1150 us -> none  [the longest x2 1150 us: backward_layer(): lax.psum_scatter(weight_full, 'tm', scatter_dimension=0, tiled=True)]
    slice x193 -> x32, local copies, waits for them, and re-layouts: 909 us -> 4.56 us  [the longest x16 4.33 us: halves(): lax.slice_in_dim(array, 0, half, axis=axis)]
    pad x112 -> x0, local copies, waits for them, and re-layouts: 559 us -> none  [the longest x56 292 us: backward_layer(): lax.associative_scan(affine_join, (next_forget[:, ::-1], driven[:, ::-1])...]
    all_gather x4 -> x0, waiting for transfers between devices: 358 us -> none  [the longest x1 335 us: per_device(): lax.all_gather(first_weight, 'tm', axis=0, tiled=True)]
    all_gather x8 -> x0, blocking collectives: 242 us -> none  [prefix(): pieces = jax.tree.map(lambda part: lax.all_gather(part, axis), value)]
    ppermute x4 -> x128, starting transfers between devices: 15.5 us -> 218 us  [moved(): return lax.ppermute(array, ('tm', 'mp'), pairs)]
    add x110 -> x1, other arithmetic: 182 us -> 0.12 us  [sum_chips(): plane = plane + over_z(running.astype(BF))]
    ppermute x4 -> x128, waiting for transfers between devices: 10.9 us -> 184 us  [moved(): return lax.ppermute(array, ('tm', 'mp'), pairs)]
  transfers between devices with their start and end apart: 14 -> 128, of which waited for: 8 -> 46; matrix products, arithmetic and copies ran while one was open for 16% -> 2% of each run, Pallas kernels for 0% -> 7%
where the time goes in v1:
time: 545 us; the launch traced here: 537 us
  starting transfers between devices  218 us (40%)
  waiting for transfers between devices  184 us (34%)
  Pallas kernels  109 us (20%)
  local copies, waits for them, and re-layouts  20.9 us (4%)
    ppermute x128, starting transfers between devices, moved(): return lax.ppermute(array, ('tm', 'mp'), pairs)  218 us
    ppermute x128, waiting for transfers between devices, moved(): return lax.ppermute(array, ('tm', 'mp'), pairs)  184 us
    pallas_call x17, Pallas kernels, call(): pl.pallas_call(body, out_shape=[jax.ShapeDtypeStruct(shape, kind) for sha...  109 us
    unnamed x108, local copies, waits for them, and re-layouts  15.2 us
  transfers between devices with their start and end apart: 128, of which 46 were waited for; matrix products, arithmetic and copies ran while one was open for 2% of the time, Pallas kernels for 7%

profile of v1, /device:TPU:8, one launch (start us, length us, event | category | flops | bytes accessed | tf_op | source)
XLA Modules:
  0.0 537.5 jit_solution(2989087445022194035)
XLA Ops:
  21.5 19.7 %collective-permute-done.11.rest_3_ = bf16[3,72,576]{2,1,0:T(8,128)(2,1)S(1)} collective-permute-done((bf16[3,72,576]{2,1,0:T(8,128)(2,1)S(1)}, bf16[3,72,576]{2,1,0:T(8,128)(2,1)S(1)}, u32[]{:S(2)}, u32[]{:S(2)}) %collective-permute-start.11) | collective-permute-done | bytes 248864 | tf_op jit(solution)/shard_map/ppermute | solution.py:32
  63.1 8.5 %collective-permute-start.14 = (bf16[3,72,576]{2,1,0:T(8,128)(2,1)S(1)}, bf16[3,72,576]{2,1,0:T(8,128)(2,1)S(1)}, u32[]{:S(2)}, u32[]{:S(2)}) collective-permute-start(bf16[3,72,576]{2,1,0:T(8,128)(2,1)S(1)} %get-tuple-element.134), channel_id=1, source_target_pairs={{0,24},{1,28},{2,26},{3,30},{4,25},{5,29},{6,27},{7,31},{8,0},{9,4... | collective-permute-start | bytes 746504 | tf_op jit(solution)/shard_map/ppermute | solution.py:32
  94.8 9.3 %shard_map.113 = (bf16[1152,2048]{1,0:T(8,128)(2,1)}, f32[216,2048]{1,0:T(8,128)}, f32[216,2048]{1,0:T(8,128)}) custom-call(s32[4]{0:T(128)S(1)} %pad_add_fusion.ids, bf16[864,1152]{1,0:T(8,128)(2,1)} %copy-done.7, bf16[576,256]{1,0:T(8,128)(2,1)S(1)} %bitcast.27, bf16[576,256]{1,0:T(8,128)(2,1)S(1)} %collective-permute-done.16.rest_1_, ...), custom_call_target="tpu_custom_call" | custom-call | tf_op jit(solution)/shard_map/pallas_call | solution.py:54
  109.6 7.5 %shard_map.114 = (bf16[72,2048]{1,0:T(8,128)(2,1)S(1)}, f32[72,2048]{1,0:T(8,128)S(1)}, f32[72,2048]{1,0:T(8,128)S(1)}, f32[72,2048]{1,0:T(8,128)S(1)}, f32[72,2048]{1,0:T(8,128)S(1)}) custom-call(s32[4]{0:T(128)S(1)} %pad_add_fusion.ids, f32[216,2048]{1,0:T(8,128)S(1)} %copy-done.9, f32[216,2048]{1,0:T(8,128)} %collective-permute-done.35.theirs, ...), custom_call_target="tpu_custom_call" | custom-call | tf_op jit(solution)/shard_map/pallas_call | solution.py:54
  125.5 7.7 %collective-permute-done.40.rest_5_ = bf16[72,2048]{1,0:T(8,128)(2,1)S(1)} collective-permute-done((bf16[72,2048]{1,0:T(8,128)(2,1)S(1)}, bf16[72,2048]{1,0:T(8,128)(2,1)S(1)}, u32[]{:S(2)}, u32[]{:S(2)}) %collective-permute-start.40) | collective-permute-done | bytes 294944 | tf_op jit(solution)/shard_map/ppermute | solution.py:32
  144.4 6.1 %collective-permute-done.3.rest_3_ = bf16[3,72,576]{2,1,0:T(8,128)(2,1)S(1)} collective-permute-done((bf16[3,72,576]{2,1,0:T(8,128)(2,1)S(1)}, bf16[3,72,576]{2,1,0:T(8,128)(2,1)S(1)}, u32[]{:S(2)}, u32[]{:S(2)}) %collective-permute-start.3) | collective-permute-done | bytes 248864 | tf_op jit(solution)/shard_map/ppermute | solution.py:32
  152.0 6.0 %collective-permute-start.50 = (bf16[72,2048]{1,0:T(8,128)(2,1)S(1)}, bf16[72,2048]{1,0:T(8,128)(2,1)S(1)}, u32[]{:S(2)}, u32[]{:S(2)}) collective-permute-start(bf16[72,2048]{1,0:T(8,128)(2,1)S(1)} %collective-permute-done.45.rest_10_), channel_id=1, source_target_pairs={{0,8},{1,9},{2,10},{3,11},{4,12},{5,13},{6,14},{7,15},{8,16},{9,17... | collective-permute-start | bytes 884744 | tf_op jit(solution)/shard_map/ppermute | solution.py:32
  158.0 6.6 %collective-permute-done.4.rest_4_ = bf16[3,72,576]{2,1,0:T(8,128)(2,1)S(1)} collective-permute-done((bf16[3,72,576]{2,1,0:T(8,128)(2,1)S(1)}, bf16[3,72,576]{2,1,0:T(8,128)(2,1)S(1)}, u32[]{:S(2)}, u32[]{:S(2)}) %collective-permute-start.4) | collective-permute-done | bytes 248864 | tf_op jit(solution)/shard_map/ppermute | solution.py:32
  180.5 14.0 %collective-permute-start.6 = (bf16[3,72,576]{2,1,0:T(8,128)(2,1)S(1)}, bf16[3,72,576]{2,1,0:T(8,128)(2,1)S(1)}, u32[]{:S(2)}, u32[]{:S(2)}) collective-permute-start(bf16[3,72,576]{2,1,0:T(8,128)(2,1)S(1)} %get-tuple-element.125), channel_id=1, source_target_pairs={{0,24},{1,28},{2,26},{3,30},{4,25},{5,29},{6,27},{7,31},{8,0},{9,4... | collective-permute-start | bytes 746504 | tf_op jit(solution)/shard_map/ppermute | solution.py:32
  217.7 11.7 %shard_map.115 = (bf16[1152,2048]{1,0:T(8,128)(2,1)}, f32[216,2048]{1,0:T(8,128)}, f32[216,2048]{1,0:T(8,128)}) custom-call(s32[4]{0:T(128)S(1)} %pad_add_fusion.ids, bf16[864,1152]{1,0:T(8,128)(2,1)} %copy-done.6, bf16[72,2048]{1,0:T(8,128)(2,1)S(1)} %get-tuple-element.139.rest_0_, bf16[72,2048]{1,0:T(8,128)(2,1)S(1)} %collective-permute-done.36.rest_1_, ...), custom_call_target="tpu_custom_call" | custom-call | tf_op jit(solution)/shard_map/pallas_call | solution.py:54
  248.2 14.7 %shard_map.117 = (bf16[72,256]{1,0:T(8,128)(2,1)S(1)}, bf16[72,256]{1,0:T(8,128)(2,1)}, bf16[72,256]{1,0:T(8,128)(2,1)S(1)}, bf16[72,256]{1,0:T(8,128)(2,1)S(1)}...) custom-call(s32[4]{0:T(128)S(1)} %pad_add_fusion.ids, ...), custom_call_target="tpu_custom_call" | custom-call | tf_op jit(solution)/shard_map/pallas_call | solution.py:54
  269.3 10.7 %shard_map.119 = (bf16[864,2048]{1,0:T(8,128)(2,1)}, f32[72,2048]{1,0:T(8,128)S(1)}, f32[72,2048]{1,0:T(8,128)S(1)}, f32[72,2048]{1,0:T(8,128)S(1)}, bf16[72,102...) custom-call(s32[4]{0:T(128)S(1)} %pad_add_fusion.ids, ...), custom_call_target="tpu_custom_call" | custom-call | tf_op jit(solution)/shard_map/pallas_call | solution.py:54
  297.2 6.4 %collective-permute-done.86 = bf16[72,2048]{1,0:T(8,128)(2,1)S(1)} collective-permute-done((bf16[72,2048]{1,0:T(8,128)(2,1)S(1)}, bf16[72,2048]{1,0:T(8,128)(2,1)S(1)}, u32[]{:S(2)}, u32[]{:S(2)}) %collective-permute-start.86) | collective-permute-done | bytes 294944 | tf_op jit(solution)/shard_map/ppermute | solution.py:32
  323.0 6.0 %collective-permute-done.89 = bf16[72,2048]{1,0:T(8,128)(2,1)S(1)} collective-permute-done((bf16[72,2048]{1,0:T(8,128)(2,1)S(1)}, bf16[72,2048]{1,0:T(8,128)(2,1)S(1)}, u32[]{:S(2)}, u32[]{:S(2)}) %collective-permute-start.89) | collective-permute-done | bytes 294944 | tf_op jit(solution)/shard_map/ppermute | solution.py:32
  329.2 8.3 %shard_map.120 = (bf16[216,2048]{1,0:T(8,128)(2,1)S(1)}, f32[216,128]{1,0:T(8,128)S(1)}) custom-call(s32[4]{0:T(128)S(1)} %pad_add_fusion.ids, f32[72,2048]{1,0:T(8,128)S(1)} %convert_add_fusion.grad, f32[72,2048]{1,0:T(8,128)S(1)} %get-tuple-element.181.cand, f32[72,2048]{1,0:T(8,128)S(1)} %get-tuple-element.182.forg, f32[72,2048]{1,0:T(8,128)S(1)} %copy-done.13, ...), custom_call_target="tpu_custom_call" | custom-call | tf_op jit(solution)/shard_map/pallas_call | solution.py:54
  340.9 10.7 %shard_map.121 = (bf16[864,2048]{1,0:T(8,128)(2,1)}, f32[576,256]{1,0:T(8,128)S(1)}, f32[576,256]{1,0:T(8,128)S(1)}, f32[576,256]{1,0:T(8,128)S(1)}, bf16[288,25...) custom-call(s32[4]{0:T(128)S(1)} %pad_add_fusion.ids, ...), custom_call_target="tpu_custom_call" | custom-call | tf_op jit(solution)/shard_map/pallas_call | solution.py:54
  358.6 8.4 %shard_map.124 = (bf16[216,640]{1,0:T(8,128)(2,1)S(1)}, bf16[216,640]{1,0:T(8,128)(2,1)S(1)}, bf16[216,640]{1,0:T(8,128)(2,1)S(1)}, bf16[216,640]{1,0:T(8,128)(2...) custom-call(s32[4]{0:T(128)S(1)} %pad_add_fusion.ids, ...), custom_call_target="tpu_custom_call" | custom-call | tf_op jit(solution)/shard_map/pallas_call | solution.py:54
  370.8 8.3 %shard_map.122 = (bf16[216,640]{1,0:T(8,128)(2,1)S(1)}, bf16[216,640]{1,0:T(8,128)(2,1)S(1)}, bf16[216,640]{1,0:T(8,128)(2,1)S(1)}, bf16[216,640]{1,0:T(8,128)(2...) custom-call(s32[4]{0:T(128)S(1)} %pad_add_fusion.ids, ...), custom_call_target="tpu_custom_call" | custom-call | tf_op jit(solution)/shard_map/pallas_call | solution.py:54
  411.8 6.4 %collective-permute-done.121.rest_1_ = bf16[216,640]{1,0:T(8,128)(2,1)S(1)} collective-permute-done((bf16[216,640]{1,0:T(8,128)(2,1)S(1)}, bf16[216,640]{1,0:T(8,128)(2,1)S(1)}, u32[]{:S(2)}, u32[]{:S(2)}) %collective-permute-start.121) | collective-permute-done | bytes 276512 | tf_op jit(solution)/shard_map/ppermute | solution.py:32
  427.2 25.5 %collective-permute-done.123.rest_3_ = bf16[216,640]{1,0:T(8,128)(2,1)S(1)} collective-permute-done((bf16[216,640]{1,0:T(8,128)(2,1)S(1)}, bf16[216,640]{1,0:T(8,128)(2,1)S(1)}, u32[]{:S(2)}, u32[]{:S(2)}) %collective-permute-start.123) | collective-permute-done | bytes 276512 | tf_op jit(solution)/shard_map/ppermute | solution.py:32
  458.2 6.9 %collective-permute-start.108 = (bf16[576,256]{1,0:T(8,128)(2,1)S(1)}, bf16[576,256]{1,0:T(8,128)(2,1)S(1)}, u32[]{:S(2)}, u32[]{:S(2)}) collective-permute-start(bf16[576,256]{1,0:T(8,128)(2,1)S(1)} %add_convert_fusion.1), channel_id=1, source_target_pairs={{0,8},{1,9},{2,10},{3,11},{4,12},{5,13},{6,14},{7,15},{8,16},{9,17... | collective-permute-start | bytes 884744 | tf_op jit(solution)/shard_map/ppermute | solution.py:32
  490.8 12.1 %collective-permute-done.115.rest_4_ = bf16[216,640]{1,0:T(8,128)(2,1)S(1)} collective-permute-done((bf16[216,640]{1,0:T(8,128)(2,1)S(1)}, bf16[216,640]{1,0:T(8,128)(2,1)S(1)}, u32[]{:S(2)}, u32[]{:S(2)}) %collective-permute-start.115) | collective-permute-done | bytes 276512 | tf_op jit(solution)/shard_map/ppermute | solution.py:32
  502.9 7.0 %collective-permute-start.117 = (bf16[216,640]{1,0:T(8,128)(2,1)S(1)}, bf16[216,640]{1,0:T(8,128)(2,1)S(1)}, u32[]{:S(2)}, u32[]{:S(2)}) collective-permute-start(bf16[216,640]{1,0:T(8,128)(2,1)S(1)} %get-tuple-element.215), channel_id=1, source_target_pairs={{0,8},{1,12},{2,10},{3,14},{4,9},{5,13},{6,11},{7,15},{8,16},{9,20... | collective-permute-start | bytes 829448 | tf_op jit(solution)/shard_map/ppermute | solution.py:32
  509.9 12.4 %collective-permute-start.118 = (bf16[216,640]{1,0:T(8,128)(2,1)S(1)}, bf16[216,640]{1,0:T(8,128)(2,1)S(1)}, u32[]{:S(2)}, u32[]{:S(2)}) collective-permute-start(bf16[216,640]{1,0:T(8,128)(2,1)S(1)} %get-tuple-element.216), channel_id=1, source_target_pairs={{0,9},{1,13},{2,11},{3,15},{4,8},{5,12},{6,10},{7,14},{8,17},{9,21... | collective-permute-start | bytes 829448 | tf_op jit(solution)/shard_map/ppermute | solution.py:32
  (434 shorter events, 294.6 us)
Async XLA Ops:
  10.5 32.2 %collective-permute-start.25 = (bf16[576,256]{1,0:T(8,128)(2,1)S(1)}, bf16[576,256]{1,0:T(8,128)(2,1)S(1)}, u32[]{:S(2)}, u32[]{:S(2)}) collective-permute-start(bf16[576,256]{1,0:T(8,128)(2,1)S(1)} %collective-permute-done.20.rest_5_), channel_id=1, source_target_pairs={{0,8},{1,9},{2,10},{3,11},{4,12},{5,13},{6,14},{7,15},{8,16},{9,17... | collective-permute-start | bytes 884744 | tf_op jit(solution)/shard_map/ppermute | solution.py:32
  11.2 29.9 %collective-permute-start.11 = (bf16[3,72,576]{2,1,0:T(8,128)(2,1)S(1)}, bf16[3,72,576]{2,1,0:T(8,128)(2,1)S(1)}, u32[]{:S(2)}, u32[]{:S(2)}) collective-permute-start(bf16[3,72,576]{2,1,0:T(8,128)(2,1)S(1)} %get-tuple-element.131), channel_id=1, source_target_pairs={{0,12},{1,8},{2,14},{3,10},{4,13},{5,9},{6,15},{7,11},{8,20},{9,16... | collective-permute-start | bytes 746504 | tf_op jit(solution)/shard_map/ppermute | solution.py:32
  13.7 33.8 %collective-permute-start.12 = (bf16[3,72,576]{2,1,0:T(8,128)(2,1)S(1)}, bf16[3,72,576]{2,1,0:T(8,128)(2,1)S(1)}, u32[]{:S(2)}, u32[]{:S(2)}) collective-permute-start(bf16[3,72,576]{2,1,0:T(8,128)(2,1)S(1)} %get-tuple-element.132), channel_id=1, source_target_pairs={{0,16},{1,20},{2,18},{3,22},{4,17},{5,21},{6,19},{7,23},{8,24},{9,... | collective-permute-start | bytes 746504 | tf_op jit(solution)/shard_map/ppermute | solution.py:32
  18.3 36.7 %collective-permute-start.16 = (bf16[576,256]{1,0:T(8,128)(2,1)S(1)}, bf16[576,256]{1,0:T(8,128)(2,1)S(1)}, u32[]{:S(2)}, u32[]{:S(2)}) collective-permute-start(bf16[576,256]{1,0:T(8,128)(2,1)S(1)} %bitcast.25), channel_id=1, source_target_pairs={{0,4},{1,5},{2,6},{3,7},{4,0},{5,1},{6,2},{7,3},{8,12},{9,13},{10,... | collective-permute-start | bytes 884744 | tf_op jit(solution)/shard_map/ppermute | solution.py:32
  20.8 32.7 %collective-permute-start.13 = (bf16[3,72,576]{2,1,0:T(8,128)(2,1)S(1)}, bf16[3,72,576]{2,1,0:T(8,128)(2,1)S(1)}, u32[]{:S(2)}, u32[]{:S(2)}) collective-permute-start(bf16[3,72,576]{2,1,0:T(8,128)(2,1)S(1)} %get-tuple-element.133), channel_id=1, source_target_pairs={{0,20},{1,16},{2,22},{3,18},{4,21},{5,17},{6,23},{7,19},{8,28},{9,... | collective-permute-start | bytes 746504 | tf_op jit(solution)/shard_map/ppermute | solution.py:32
  135.5 29.1 %collective-permute-start.4 = (bf16[3,72,576]{2,1,0:T(8,128)(2,1)S(1)}, bf16[3,72,576]{2,1,0:T(8,128)(2,1)S(1)}, u32[]{:S(2)}, u32[]{:S(2)}) collective-permute-start(bf16[3,72,576]{2,1,0:T(8,128)(2,1)S(1)} %get-tuple-element.123), channel_id=1, source_target_pairs={{0,16},{1,20},{2,18},{3,22},{4,17},{5,21},{6,19},{7,23},{8,24},{9,... | collective-permute-start | bytes 746504 | tf_op jit(solution)/shard_map/ppermute | solution.py:32
  139.5 32.5 %collective-permute-start.36 = (bf16[72,2048]{1,0:T(8,128)(2,1)S(1)}, bf16[72,2048]{1,0:T(8,128)(2,1)S(1)}, u32[]{:S(2)}, u32[]{:S(2)}) collective-permute-start(bf16[72,2048]{1,0:T(8,128)(2,1)S(1)} %get-tuple-element.139.rest_0_), channel_id=1, source_target_pairs={{0,4},{1,5},{2,6},{3,7},{4,0},{5,1},{6,2},{7,3},{8,12},{9,13},{10,... | collective-permute-start | bytes 884744 | tf_op jit(solution)/shard_map/ppermute | solution.py:32
  144.4 26.2 %collective-permute-start.5 = (bf16[3,72,576]{2,1,0:T(8,128)(2,1)S(1)}, bf16[3,72,576]{2,1,0:T(8,128)(2,1)S(1)}, u32[]{:S(2)}, u32[]{:S(2)}) collective-permute-start(bf16[3,72,576]{2,1,0:T(8,128)(2,1)S(1)} %get-tuple-element.124), channel_id=1, source_target_pairs={{0,20},{1,16},{2,22},{3,18},{4,21},{5,17},{6,23},{7,19},{8,28},{9,... | collective-permute-start | bytes 746504 | tf_op jit(solution)/shard_map/ppermute | solution.py:32
  172.2 24.8 %collective-permute-start.47 = (bf16[72,2048]{1,0:T(8,128)(2,1)S(1)}, bf16[72,2048]{1,0:T(8,128)(2,1)S(1)}, u32[]{:S(2)}, u32[]{:S(2)}) collective-permute-start(bf16[72,2048]{1,0:T(8,128)(2,1)S(1)} %collective-permute-done.45.rest_10_), channel_id=1, source_target_pairs={{0,2},{1,3},{2,0},{3,1},{4,6},{5,7},{6,4},{7,5},{8,10},{9,11},{10,... | collective-permute-start | bytes 884744 | tf_op jit(solution)/shard_map/ppermute | solution.py:32
  352.9 26.3 %collective-permute-start.105 = (bf16[288,256]{1,0:T(8,128)(2,1)}, bf16[288,256]{1,0:T(8,128)(2,1)}, u32[]{:S(2)}, u32[]{:S(2)}) collective-permute-start(bf16[288,256]{1,0:T(8,128)(2,1)} %get-tuple-element.205), channel_id=1, source_target_pairs={{0,4},{1,5},{2,6},{3,7},{4,0},{5,1},{6,2},{7,3},{8,12},{9,13},{10,... | collective-permute-start | bytes 442376 | tf_op jit(solution)/shard_map/ppermute | solution.py:32
  354.5 39.9 %collective-permute-start.63 = (bf16[72,256]{1,0:T(8,128)(2,1)}, bf16[72,256]{1,0:T(8,128)(2,1)S(1)}, u32[]{:S(2)}, u32[]{:S(2)}) collective-permute-start(bf16[72,256]{1,0:T(8,128)(2,1)} %get-tuple-element.151), channel_id=1, source_target_pairs={{0,4},{1,5},{2,6},{3,7},{4,0},{5,1},{6,2},{7,3},{8,12},{9,13},{10,... | collective-permute-start | bytes 110600 | tf_op jit(solution)/shard_map/ppermute | solution.py:32
  355.5 41.8 %collective-permute-start.64 = (bf16[72,256]{1,0:T(8,128)(2,1)S(1)}, bf16[72,256]{1,0:T(8,128)(2,1)S(1)}, u32[]{:S(2)}, u32[]{:S(2)}) collective-permute-start(bf16[72,256]{1,0:T(8,128)(2,1)S(1)} %copy-done.43), channel_id=1, source_target_pairs={{0,8},{1,9},{2,10},{3,11},{4,12},{5,13},{6,14},{7,15},{8,16},{9,17... | collective-permute-start | bytes 110600 | tf_op jit(solution)/shard_map/ppermute | solution.py:32
  355.5 42.5 %collective-permute-start.65 = (bf16[72,256]{1,0:T(8,128)(2,1)S(1)}, bf16[72,256]{1,0:T(8,128)(2,1)S(1)}, u32[]{:S(2)}, u32[]{:S(2)}) collective-permute-start(bf16[72,256]{1,0:T(8,128)(2,1)S(1)} %copy-done.41), channel_id=1, source_target_pairs={{0,12},{1,13},{2,14},{3,15},{4,8},{5,9},{6,10},{7,11},{8,20},{9,21... | collective-permute-start | bytes 110600 | tf_op jit(solution)/shard_map/ppermute | solution.py:32
  418.2 34.5 %collective-permute-start.123 = (bf16[216,640]{1,0:T(8,128)(2,1)S(1)}, bf16[216,640]{1,0:T(8,128)(2,1)S(1)}, u32[]{:S(2)}, u32[]{:S(2)}) collective-permute-start(bf16[216,640]{1,0:T(8,128)(2,1)S(1)} %get-tuple-element.225), channel_id=1, source_target_pairs={{0,25},{1,29},{2,27},{3,31},{4,24},{5,28},{6,26},{7,30},{8,1},{9,5... | collective-permute-start | bytes 829448 | tf_op jit(solution)/shard_map/ppermute | solution.py:32
  418.2 34.5 %collective-permute-start.124 = (bf16[216,640]{1,0:T(8,128)(2,1)S(1)}, bf16[216,640]{1,0:T(8,128)(2,1)S(1)}, u32[]{:S(2)}, u32[]{:S(2)}) collective-permute-start(bf16[216,640]{1,0:T(8,128)(2,1)S(1)} %get-tuple-element.226), channel_id=1, source_target_pairs={{0,16},{1,20},{2,18},{3,22},{4,17},{5,21},{6,19},{7,23},{8,24},{9,... | collective-permute-start | bytes 829448 | tf_op jit(solution)/shard_map/ppermute | solution.py:32
  419.8 33.6 %collective-permute-start.125 = (bf16[216,640]{1,0:T(8,128)(2,1)S(1)}, bf16[216,640]{1,0:T(8,128)(2,1)S(1)}, u32[]{:S(2)}, u32[]{:S(2)}) collective-permute-start(bf16[216,640]{1,0:T(8,128)(2,1)S(1)} %get-tuple-element.227), channel_id=1, source_target_pairs={{0,17},{1,21},{2,19},{3,23},{4,16},{5,20},{6,18},{7,22},{8,25},{9,... | collective-permute-start | bytes 829448 | tf_op jit(solution)/shard_map/ppermute | solution.py:32
  424.4 33.3 %collective-permute-start.126 = (bf16[216,640]{1,0:T(8,128)(2,1)S(1)}, bf16[216,640]{1,0:T(8,128)(2,1)S(1)}, u32[]{:S(2)}, u32[]{:S(2)}) collective-permute-start(bf16[216,640]{1,0:T(8,128)(2,1)S(1)} %get-tuple-element.228), channel_id=1, source_target_pairs={{0,8},{1,12},{2,10},{3,14},{4,9},{5,13},{6,11},{7,15},{8,16},{9,20... | collective-permute-start | bytes 829448 | tf_op jit(solution)/shard_map/ppermute | solution.py:32
  424.7 33.5 %collective-permute-start.91 = (bf16[288,256]{1,0:T(8,128)(2,1)S(1)}, bf16[288,256]{1,0:T(8,128)(2,1)S(1)}, u32[]{:S(2)}, u32[]{:S(2)}) collective-permute-start(bf16[288,256]{1,0:T(8,128)(2,1)S(1)} %copy-done.23), channel_id=1, source_target_pairs={{0,2},{1,3},{2,0},{3,1},{4,6},{5,7},{6,4},{7,5},{8,10},{9,11},{10,... | collective-permute-start | bytes 442376 | tf_op jit(solution)/shard_map/ppermute | solution.py:32
  472.8 30.1 %collective-permute-start.115 = (bf16[216,640]{1,0:T(8,128)(2,1)S(1)}, bf16[216,640]{1,0:T(8,128)(2,1)S(1)}, u32[]{:S(2)}, u32[]{:S(2)}) collective-permute-start(bf16[216,640]{1,0:T(8,128)(2,1)S(1)} %get-tuple-element.213), channel_id=1, source_target_pairs={{0,16},{1,20},{2,18},{3,22},{4,17},{5,21},{6,19},{7,23},{8,24},{9,... | collective-permute-start | bytes 829448 | tf_op jit(solution)/shard_map/ppermute | solution.py:32
  474.4 35.5 %collective-permute-start.116 = (bf16[216,640]{1,0:T(8,128)(2,1)S(1)}, bf16[216,640]{1,0:T(8,128)(2,1)S(1)}, u32[]{:S(2)}, u32[]{:S(2)}) collective-permute-start(bf16[216,640]{1,0:T(8,128)(2,1)S(1)} %get-tuple-element.214), channel_id=1, source_target_pairs={{0,17},{1,21},{2,19},{3,23},{4,16},{5,20},{6,18},{7,22},{8,25},{9,... | collective-permute-start | bytes 829448 | tf_op jit(solution)/shard_map/ppermute | solution.py:32
  477.7 58.5 %collective-permute-start.94 = (bf16[576,256]{1,0:T(8,128)(2,1)S(1)}, bf16[576,256]{1,0:T(8,128)(2,1)S(1)}, u32[]{:S(2)}, u32[]{:S(2)}) collective-permute-start(bf16[576,256]{1,0:T(8,128)(2,1)S(1)} %pad_maximum_fusion.9), channel_id=1, source_target_pairs={{0,2},{1,3},{2,0},{3,1},{4,6},{5,7},{6,4},{7,5},{8,10},{9,11},{10,... | collective-permute-start | bytes 884744 | tf_op jit(solution)/shard_map/ppermute | solution.py:32
  480.3 55.9 %collective-permute-start.92 = (bf16[576,256]{1,0:T(8,128)(2,1)S(1)}, bf16[576,256]{1,0:T(8,128)(2,1)S(1)}, u32[]{:S(2)}, u32[]{:S(2)}) collective-permute-start(bf16[576,256]{1,0:T(8,128)(2,1)S(1)} %pad_maximum_fusion.8), channel_id=1, source_target_pairs={{0,4},{1,5},{2,6},{3,7},{4,0},{5,1},{6,2},{7,3},{8,12},{9,13},{10,... | collective-permute-start | bytes 884744 | tf_op jit(solution)/shard_map/ppermute | solution.py:32
  488.4 47.9 %collective-permute-start.109 = (bf16[576,256]{1,0:T(8,128)(2,1)S(1)}, bf16[576,256]{1,0:T(8,128)(2,1)S(1)}, u32[]{:S(2)}, u32[]{:S(2)}) collective-permute-start(bf16[576,256]{1,0:T(8,128)(2,1)S(1)} %add_convert_fusion), channel_id=1, source_target_pairs={{0,8},{1,9},{2,10},{3,11},{4,12},{5,13},{6,14},{7,15},{8,16},{9,17... | collective-permute-start | bytes 884744 | tf_op jit(solution)/shard_map/ppermute | solution.py:32
  502.9 25.0 %collective-permute-start.117 = (bf16[216,640]{1,0:T(8,128)(2,1)S(1)}, bf16[216,640]{1,0:T(8,128)(2,1)S(1)}, u32[]{:S(2)}, u32[]{:S(2)}) collective-permute-start(bf16[216,640]{1,0:T(8,128)(2,1)S(1)} %get-tuple-element.215), channel_id=1, source_target_pairs={{0,8},{1,12},{2,10},{3,14},{4,9},{5,13},{6,11},{7,15},{8,16},{9,20... | collective-permute-start | bytes 829448 | tf_op jit(solution)/shard_map/ppermute | solution.py:32
  (158 other events, 1804.2 us)

commit v2 on v1

--- a/solution.py
+++ b/solution.py
@@ -14,7 +14,7 @@
 
 
 def mod(value):
-    return lax.rem(value + NZ, NZ)
+    return lax.rem(value + 2 * NZ, NZ)
 
 
 def flip(bit, by):
@@ -44,74 +44,156 @@
     return moved(array, lambda z, x, y, c: (z, x, y, 1 - c))
 
 
-def over_z(array):
-    return moved(array, lambda z, x, y, c: ((z + 1) % NZ, x, y, c))
-
-
-def call(body, outs, args, scratch=(), vmem=48):
+def over_z(array, by):
+    return moved(array, lambda z, x, y, c: ((z + by) % NZ, x, y, c))
+
+
+def call(body, outs, args, scratch=(), vmem=28, flops=0, after=()):
     whole = pl.BlockSpec(memory_space=pltpu.VMEM)
+    moved_bytes = sum(a.size * a.dtype.itemsize for a in args)
+    for shape, kind in outs:
+        size = jnp.dtype(kind).itemsize
+        for extent in shape:
+            size *= extent
+        moved_bytes += size
     specs = [pl.BlockSpec(memory_space=pltpu.SMEM)] + [whole] * (len(args) - 1)
+    specs += [pl.BlockSpec(memory_space=pl.ANY)] * len(after)
+    count = len(args)
+
+    def run(*refs):
+        body(*refs[:count], *refs[count + len(after) :])
+
     return pl.pallas_call(
-        body,
+        run,
         out_shape=[jax.ShapeDtypeStruct(shape, kind) for shape, kind in outs],
         in_specs=specs,
         out_specs=[whole] * len(outs),
         scratch_shapes=list(scratch),
         compiler_params=pltpu.CompilerParams(vmem_limit_bytes=vmem * MIB),
-    )(*args)
-
-
-def pack_weight(ids, weight):
+        cost_estimate=pl.CostEstimate(flops=flops, bytes_accessed=moved_bytes, transcendentals=0),
+    )(*args, *after)
+
+
+EARLY = 10**11
+
+
+def relay(array, after, flops=EARLY):
+    anywhere = pl.BlockSpec(memory_space=pl.ANY)
+
+    def body(*refs):
+        pass
+
+    return pl.pallas_call(
+        body,
+        out_shape=jax.ShapeDtypeStruct(array.shape, array.dtype),
+        in_specs=[anywhere] * (1 + len(after)),
+        out_specs=anywhere,
+        input_output_aliases={0: 0},
+        cost_estimate=pl.CostEstimate(flops=flops, bytes_accessed=0, transcendentals=0),
+    )(array, *after)
+
+
+def pack_weight(ids, weight, along=None, after=()):
     rows, gates, columns = weight.shape
     own = columns // 8
+    extra = [] if along is None else [along]
 
     def body(ids, w, *rest):
-        outs, turned = rest[:8], rest[8]
+        outs, turned = rest[len(extra) : len(extra) + 2], rest[-1]
+        if extra:
+            rest[-2][...] = rest[0][...]
         z, c = ids[0], ids[3]
         for g in range(gates):
-            turned[...] = w[g].astype(F32).T
-            for dz in range(NZ):
-                for r in range(2):
-                    i = mod(z + dz) * 2 + flip(c, r)
-                    outs[dz * 2 + r][g] = turned[pl.ds(pl.multiple_of(i * own, 8), own)].astype(BF)
+            turned[g] = w[g].astype(F32).T
+        for r in range(2):
+            for pair in range(NZ // 2):
+                both = []
+                for dz in (2 * pair, 2 * pair + 1):
+                    at = pl.ds(pl.multiple_of((mod(z + dz) * 2 + flip(c, r)) * own, 8), own)
+                    both.append(jnp.concatenate([turned[g, at, :] for g in range(gates)], axis=0))
+                outs[r][pair] = jnp.concatenate(both, axis=1).astype(BF)
 
     return call(
         body,
-        [((gates, own, rows), BF)] * 8,
-        [ids, jnp.transpose(weight, (1, 0, 2))],
-        [pltpu.VMEM((columns, rows), F32)],
-    )
-
-
-def send_blocks(blocks):
-    return [
-        moved(blocks[dz * 2 + r], lambda z, x, y, c, dz=dz, r=r: ((z + dz) % NZ, c ^ r, y, x))
-        for dz in range(NZ)
-        for r in range(2)
-    ]
-
-
-def return_blocks(blocks):
-    def back(dz, r):
-        return lambda z, x, y, c: ((z - dz) % NZ, c, y, x ^ r)
-
-    return [moved(blocks[dz * 2 + r], back(dz, r)) for dz in range(NZ) for r in range(2)]
+        [((NZ // 2, gates * own, 2 * rows), BF)] * 2 + [(a.shape, a.dtype) for a in extra],
+        [ids, jnp.transpose(weight, (1, 0, 2)), *extra],
+        [pltpu.VMEM((gates, columns, rows), F32)],
+        after=after,
+    )
+
+
+def blocks_over_x(groups, back=False):
+    def to(r):
+        if back:
+            return lambda z, x, y, c: (z, c, y, x ^ r)
+        return lambda z, x, y, c: (z, c ^ r, y, x)
+
+    return [moved(groups[r], to(r)) for r in range(2)]
+
+
+def blocks_over_z(both, sign):
+    return [both[0]] + [over_z(both[dz], sign * dz) for dz in range(1, NZ)]
+
+
+def regroup(ids, pieces, groups, small=(), after=()):
+    count = len(pieces)
+    _, part, width = groups[0].shape
+    rows = width // 2
+    near_shape = (count,) + pieces[0].shape
+    small_shape = (2,) + small[0].shape[1:] if small else None
+
+    def body(ids, *rest):
+        ins, (r0, r1) = rest[:count], rest[count : count + 2]
+        tiny = rest[count + 2 : count + 2 + len(small)]
+        outs = rest[count + 2 + len(small) :]
+        for at in range(count):
+            outs[0][at] = ins[at][...]
+        for dz in range(NZ):
+            lanes = slice((dz % 2) * rows, (dz % 2 + 1) * rows)
+            parts = [group[dz // 2].astype(F32)[:, lanes] for group in (r0, r1)]
+            outs[1 + dz][...] = jnp.concatenate(parts, axis=1).astype(BF)
+        for at in range(NZ if small else 0):
+            for k in range(2):
+                outs[1 + NZ + at][k] = tiny[k][at]
+
+    made = call(
+        body,
+        [(near_shape, BF)] + [((part, width), BF)] * NZ + ([(small_shape, BF)] * NZ if small else []),
+        [ids, *pieces, *groups, *small],
+        after=after,
+    )
+    return made[0], made[1 : 1 + NZ], made[1 + NZ :]
+
+
+def regroup_back(ids, both, after=()):
+    part, width = both[0].shape
+    rows = width // 2
+
+    def body(ids, *rest):
+        ins, outs = rest[:NZ], rest[NZ:]
+        for r in range(2):
+            lanes = slice(r * rows, (r + 1) * rows)
+            for pair in range(NZ // 2):
+                parts = [ins[2 * pair + k][...].astype(F32)[:, lanes] for k in range(2)]
+                outs[r][pair] = jnp.concatenate(parts, axis=1).astype(BF)
+
+    return call(body, [((NZ // 2, part, width), BF)] * 2, [ids, *both], after=after, flops=EARLY)
 
 
 def join_weight(ids, blocks):
-    gates, own, rows = blocks[0].shape
-    part = gates * own
+    part, width = blocks[0].shape
+    rows = width // 2
 
     def body(ids, *rest):
-        ins, (wide, tall), joined = rest[:8], rest[8:10], rest[10]
+        ins, (wide, tall), joined = rest[:NZ], rest[NZ : NZ + 2], rest[NZ + 2]
         z, x = ids[0], ids[1]
         for dz in range(NZ):
+            source = mod(z - dz)
+            both = ins[dz][...].astype(F32)
             for r in range(2):
-                source = mod(z - dz)
                 base = (flip(x, r) * 2 + source // 2) * part
-                for g in range(gates):
-                    at = pl.ds(pl.multiple_of(base + g * own, 8), own)
-                    joined[lax.rem(source, 2), at, :] = ins[dz * 2 + r][g].astype(F32)
+                at = pl.ds(pl.multiple_of(base, 8), part)
+                joined[lax.rem(source, 2), at, :] = both[:, r * rows : (r + 1) * rows]
         for half in range(2):
             at = pl.ds(half * 2 * part, 2 * part)
             both = jnp.concatenate([joined[0, at, :], joined[1, at, :]], axis=1)
@@ -124,6 +206,7 @@
         [((4 * part, 2 * rows), BF), ((2 * rows, 4 * part), BF)],
         [ids, *blocks],
         [pltpu.VMEM((2, 4 * part, rows), F32)],
+        flops=EARLY,
     )
 
 
@@ -132,47 +215,63 @@
     return lax.slice_in_dim(array, 0, half, axis=axis), lax.slice_in_dim(array, half, 2 * half, axis=axis)
 
 
-def gather_chips(piece, axis):
-    found = []
-    for dz in range(NZ):
-        if dz:
-            piece = over_z(piece)
-        from_x, from_y = over_x(piece), over_y(piece)
-        found += [piece, from_x, from_y, over_y(halves(from_x, axis)[0]), over_x(halves(from_y, axis)[1])]
-    return found
-
-
-def sum_chips(parts, axis):
-    running = None
-    for step in range(NZ):
-        own, to_x, to_y, diag_a, diag_b = parts[5 * step : 5 * step + 5]
-        at_x, at_y = over_y(diag_a), over_x(diag_b)
-        xa, xb = halves(to_x, axis)
-        ya, yb = halves(to_y, axis)
-        sent_x = jnp.concatenate([(xa + at_x).astype(BF), xb.astype(BF)], axis=axis)
-        sent_y = jnp.concatenate([ya.astype(BF), (yb + at_y).astype(BF)], axis=axis)
-        plane = own + over_x(sent_x) + over_y(sent_y)
-        if running is not None:
-            plane = plane + over_z(running.astype(BF))
-        running = plane
-    return running
-
-
-def partial_gates(ids, wide, found, channel_pieces):
+def along_z(piece):
+    return [piece] + [over_z(piece, dz) for dz in range(1, NZ)]
+
+
+def gather_plane(near, axis):
+    from_x, from_y = over_x(near), over_y(near)
+    return [near, from_x, from_y, over_y(halves(from_x, axis + 1)[0]), over_x(halves(from_y, axis + 1)[1])]
+
+
+def add_diagonal(ids, parts, axis, after=()):
+    _, to_x, to_y, diag_a, diag_b = parts
+    half = diag_a.shape[axis + 1]
+    first = (slice(None),) * (axis + 1) + (pl.ds(0, half),)
+    second = (slice(None),) * (axis + 1) + (pl.ds(half, half),)
+
+    def body(ids, to_x, to_y, at_x, at_y, out_x, out_y):
+        out_x[first] = (to_x[first] + at_x[...].astype(F32)).astype(BF)
+        out_x[second] = to_x[second].astype(BF)
+        out_y[first] = to_y[first].astype(BF)
+        out_y[second] = (to_y[second] + at_y[...].astype(F32)).astype(BF)
+
+    args = [ids, to_x, to_y, over_y(diag_a), over_x(diag_b)]
+    return call(body, [(to_x.shape, BF)] * 2, args, after=after)
+
+
+def add_plane(ids, own, from_x, from_y, after=()):
+    def body(ids, own, from_x, from_y, *outs):
+        for step in range(NZ):
+            plane = own[step] + from_x[step].astype(F32) + from_y[step].astype(F32)
+            outs[step][...] = plane.astype(outs[step].dtype)
+
+    outs = [(own.shape[1:], BF)] * (NZ - 1) + [(own.shape[1:], F32)]
+    return call(body, outs, [ids, own, from_x, from_y], after=after)
+
+
+def sum_planes(planes):
+    total = planes[NZ - 1]
+    for step in range(NZ - 1):
+        total = total + over_z(planes[step], step + 1).astype(F32)
+    return total
+
+
+def partial_gates(ids, wide, found, channel_pieces, after=()):
     total, depth = wide.shape
     part = total // 4
     rows = depth // 2
     if channel_pieces:
-        own, length = found[0].shape
+        own, length = found[0].shape[1:]
     else:
-        length = found[0].shape[1] * 8
+        length = found[0].shape[2] * 8
     span = 512
 
     def body(ids, w, *rest):
-        ins, (u, mine, theirs), (prev, cur) = rest[:20], rest[20:23], rest[23:]
+        ins, (u, mine, theirs), (prev, cur) = rest[:5], rest[5:8], rest[8:]
         z, x, y, c = ids[0], ids[1], ids[2], ids[3]
         for dz in range(NZ):
-            near, at_x, at_y, diag_a, diag_b = ins[5 * dz : 5 * dz + 5]
+            near, at_x, at_y, diag_a, diag_b = [part.at[dz] for part in ins]
             source = mod(z - dz)
             if channel_pieces:
                 half = length // 2
@@ -213,6 +312,8 @@
         [((depth, length), BF), ((part, length), F32), ((part, length), F32)],
         [ids, wide, *found],
         [pltpu.VMEM((2, part, length), F32), pltpu.VMEM((2, part, length), F32)],
+        after=after,
+        flops=2 * total * depth * length,
     )
 
 
@@ -220,21 +321,26 @@
     own, length = driven.shape
     lane = lax.broadcasted_iota(jnp.int32, (own, LANES), 1)
     count = length // LANES
+    order = list(range(count))[:: -1 if backward else 1]
     blocks = [None] * count
     carry = jnp.zeros((own, 1), F32)
-    for block in range(count)[:: -1 if backward else 1]:
-        cols = slice(block * LANES, (block + 1) * LANES)
-        reach, state = forget[:, cols], driven[:, cols]
+    together = 4
+    for start in range(0, count, together):
+        group = order[start : start + together]
+        reach = [forget[:, block * LANES : (block + 1) * LANES] for block in group]
+        state = [driven[:, block * LANES : (block + 1) * LANES] for block in group]
         by = 1
         while by < LANES:
             shift = LANES - by if backward else by
             inside = lane < LANES - by if backward else lane >= by
-            state = state + jnp.where(inside, reach * pltpu.roll(state, shift, 1), 0.0)
-            reach = jnp.where(inside, reach * pltpu.roll(reach, shift, 1), reach)
+            for at in range(len(group)):
+                r, s = reach[at], state[at]
+                state[at] = s + jnp.where(inside, r * pltpu.roll(s, shift, 1), 0.0)
+                reach[at] = jnp.where(inside, r * pltpu.roll(r, shift, 1), r)
             by *= 2
-        state = state + reach * carry
-        carry = state[:, :1] if backward else state[:, LANES - 1 :]
-        blocks[block] = state
+        for at, block in enumerate(group):
+            blocks[block] = state[at] + reach[at] * carry
+            carry = blocks[block][:, :1] if backward else blocks[block][:, LANES - 1 :]
     return blocks
 
 
@@ -255,7 +361,7 @@
         ref[:, pl.ds(at * LANES, LANES)] = block
 
 
-def gate_gradients(grad, candidate, forget, outgate, cells, adjoint, wide, gate_grad, bias_grad):
+def gate_gradients(grad, candidate, forget, outgate, cells, adjoint, wide, gate_grad):
     own, length = grad.shape
     driven = grad[...] * outgate[...]
     last = lax.broadcasted_iota(jnp.int32, (own, length), 1) == length - 1
@@ -270,13 +376,10 @@
     wide[pl.ds(own, own), :] = adjoint[...] * (before - a) * f * away
     o = outgate[...]
     wide[pl.ds(2 * own, own), :] = grad[...] * cells[...] * o * (1.0 - o)
-    rounded = wide[...].astype(BF)
-    gate_grad[...] = rounded
-    total = jnp.sum(rounded.astype(F32), axis=1, keepdims=True)
-    bias_grad[...] = jnp.broadcast_to(total, bias_grad.shape)
-
-
-def first_cells(ids, mine, theirs, bias):
+    gate_grad[...] = wide[...].astype(BF)
+
+
+def first_cells(ids, mine, theirs, bias, after=()):
     part, length = mine.shape
     own = part // 3
 
@@ -290,21 +393,23 @@
         body,
         [((own, length), BF)] + [((own, length), F32)] * 4,
         [ids, mine, theirs, bias],
-    )
-
-
-def first_gate_grad(ids, grad, saved):
+        after=after,
+    )
+
+
+def first_gate_grad(ids, grad, saved, after=()):
     own, length = grad.shape
 
-    def body(ids, grad, cand, forg, outg, cells, gate_grad, bias_grad, adjoint, wide):
-        gate_gradients(grad, cand, forg, outg, cells, adjoint, wide, gate_grad, bias_grad)
+    def body(ids, grad, cand, forg, outg, cells, gate_grad, adjoint, wide):
+        gate_gradients(grad, cand, forg, outg, cells, adjoint, wide, gate_grad)
 
     return call(
         body,
-        [((3 * own, length), BF), ((3 * own, LANES), F32)],
+        [((3 * own, length), BF)],
         [ids, grad, *saved],
         [pltpu.VMEM((own, length), F32), pltpu.VMEM((3 * own, length), F32)],
-    )
+        after=after,
+    )[0]
 
 
 def second_cells(ids, mine, theirs, bias, cot_pieces):
@@ -313,14 +418,13 @@
     block = length // 8
 
     def body(ids, mine, theirs, bias, *rest):
-        cots, outs = rest[:8], rest[8:16]
-        gate_grad, bias_grad = rest[16:18]
-        grad, cand, forg, outg, cells, adjoint, wide = rest[18:]
+        cots, outs, gate_grad = rest[:NZ], rest[NZ : NZ + 2], rest[NZ + 2]
+        grad, cand, forg, outg, cells, adjoint, wide = rest[NZ + 3 :]
         z, x = ids[0], ids[1]
         for dz in range(NZ):
             for dx in range(2):
                 i = mod(z - dz) * 2 + flip(x, dx)
-                grad[:, pl.ds(pl.multiple_of(i * block, block), block)] = cots[dz * 2 + dx][...].astype(F32)
+                grad[:, pl.ds(pl.multiple_of(i * block, block), block)] = cots[dz][dx].astype(F32)
         candidate, forget, outgate = activate(mine, theirs, bias, own)
         cand[...], forg[...], outg[...] = candidate, forget, outgate
         put_blocks(cells, scan_lanes(forget, (1.0 - forget) * candidate, False))
@@ -329,16 +433,16 @@
             for dx in range(2):
                 i = mod(z + dz) * 2 + flip(x, dx)
                 piece = adjoint[:, pl.ds(pl.multiple_of(i * block, block), block)]
-                outs[dz * 2 + dx][...] = piece.astype(BF)
-        gate_gradients(grad, cand, forg, outg, cells, adjoint, wide, gate_grad, bias_grad)
+                outs[dx][dz] = piece.astype(BF)
+        gate_gradients(grad, cand, forg, outg, cells, adjoint, wide, gate_grad)
 
     made = call(
         body,
-        [((own, block), BF)] * 8 + [((part, length), BF), ((part, LANES), F32)],
+        [((NZ, own, block), BF)] * 2 + [((part, length), BF)],
         [ids, mine, theirs, bias, *cot_pieces],
         [pltpu.VMEM((own, length), F32)] * 6 + [pltpu.VMEM((part, length), F32)],
     )
-    return made[:8], made[8], made[9]
+    return made[:2], made[2]
 
 
 def split_cotangent(ids, cotangent):
@@ -346,63 +450,59 @@
     own = channels // 8
 
     def body(ids, cot, *rest):
-        outs, wide = rest[:8], rest[8]
+        outs, wide = rest[:2], rest[2]
         wide[...] = cot[...].astype(F32)
         for dz in range(NZ):
             for dx in range(2):
                 i = mod(ids[0] + dz) * 2 + flip(ids[1], dx)
-                outs[dz * 2 + dx][...] = wide[pl.ds(pl.multiple_of(i * own, 8), own), :].astype(BF)
-
-    return call(body, [((own, block), BF)] * 8, [ids, cotangent], [pltpu.VMEM((channels, block), F32)])
-
-
-def over_tm(pieces):
-    return [
-        pieces[dz * 2 + dx]
-        if dz == 0 and dx == 0
-        else moved(pieces[dz * 2 + dx], lambda z, x, y, c, dz=dz, dx=dx: ((z + dz) % NZ, x ^ dx, y, c))
-        for dz in range(NZ)
-        for dx in range(2)
-    ]
+                outs[dx][dz] = wide[pl.ds(pl.multiple_of(i * own, 8), own), :].astype(BF)
+
+    return call(body, [((NZ, own, block), BF)] * 2, [ids, cotangent], [pltpu.VMEM((channels, block), F32)])
+
+
+def pair_up(ids, first, second, after=()):
+    shape = (2,) + first.shape[1:]
+
+    def body(ids, first, second, *outs):
+        for at in range(NZ):
+            outs[at][0] = first[at]
+            outs[at][1] = second[at]
+
+    return call(body, [(shape, BF)] * NZ, [ids, first, second], after=after)
 
 
 def join_outputs(ids, pieces):
-    own, block = pieces[0].shape
+    _, own, block = pieces[0].shape
 
     def body(ids, *rest):
-        ins, out, wide = rest[:8], rest[8], rest[9]
+        ins, out, wide = rest[:NZ], rest[NZ], rest[NZ + 1]
         for dz in range(NZ):
             for dx in range(2):
                 i = mod(ids[0] - dz) * 2 + flip(ids[1], dx)
-                wide[pl.ds(pl.multiple_of(i * own, 8), own), :] = ins[dz * 2 + dx][...].astype(F32)
+                wide[pl.ds(pl.multiple_of(i * own, 8), own), :] = ins[dz][dx].astype(F32)
         out[...] = wide[...].astype(BF)
 
     return call(body, [((8 * own, block), BF)], [ids, *pieces], [pltpu.VMEM((8 * own, block), F32)])[0]
 
 
-def input_parts(ids, tall, mine, theirs, channel_pieces):
+def input_parts(ids, tall, grads, channel_pieces, after=()):
     depth, total = tall.shape
-    part, length = mine.shape
+    length = grads.shape[1]
     rows = depth // 2
     own = rows // 8
     block = length // 8
     span = 512
-    shape = (own, length) if channel_pieces else (rows, block)
-    half = (own, length // 2) if channel_pieces else (rows // 2, block)
-
-    def body(ids, w, mine, theirs, grads, *rest):
-        outs, v = rest[:20], rest[20]
-        z, x, y, c = ids[0], ids[1], ids[2], ids[3]
-        last = lax.broadcasted_iota(jnp.int32, (part, length), 1) == length - 1
-        for core in range(2):
-            now = jnp.where(c == core, mine[...].astype(F32), theirs[...].astype(F32))
-            after = jnp.where(last, 0.0, pltpu.roll(now, length - 1, 1))
-            grads[pl.ds(core * 2 * part, 2 * part), :] = jnp.concatenate([after, now], axis=0).astype(BF)
+    shape = (NZ, own, length) if channel_pieces else (NZ, rows, block)
+    half = (NZ, own, length // 2) if channel_pieces else (NZ, rows // 2, block)
+
+    def body(ids, w, grads, *rest):
+        outs, v = rest[:5], rest[5]
+        z, x, y = ids[0], ids[1], ids[2]
         for start in range(0, length, span):
             cols = pl.ds(start, span)
             v[:, cols] = jnp.dot(w[...], grads[:, cols], preferred_element_type=F32)
         for step in range(NZ):
-            target = mod(z - 1 - step)
+            target = mod(z + 1 + step)
 
             def piece(dx, dy, k=None):
                 i = target * 2 + flip(x, dx)
@@ -416,81 +516,96 @@
                     return v[pl.ds(pl.multiple_of(row, 8), rows), cols]
                 return v[pl.ds(pl.multiple_of(row + k * rows // 2, 8), rows // 2), cols]
 
-            o = outs[5 * step : 5 * step + 5]
-            o[0][...] = piece(0, 0)
-            o[1][...] = piece(1, 0)
-            o[2][...] = piece(0, 1)
-            o[3][...] = piece(1, 1, 0).astype(BF)
-            o[4][...] = piece(1, 1, 1).astype(BF)
+            outs[0][step] = piece(0, 0)
+            outs[1][step] = piece(1, 0)
+            outs[2][step] = piece(0, 1)
+            outs[3][step] = piece(1, 1, 0).astype(BF)
+            outs[4][step] = piece(1, 1, 1).astype(BF)
+
+    return call(
+        body,
+        [(shape, F32), (shape, F32), (shape, F32), (half, BF), (half, BF)],
+        [ids, tall, grads],
+        [pltpu.VMEM((depth, length), F32)],
+        after=after,
+        flops=2 * depth * total * length,
+    )
+
+
+def weight_blocks(ids, mine, theirs, u, after=()):
+    part, length = mine.shape
+    depth = u.shape[0]
+    total, rows = 4 * part, depth // 2
+
+    def body(ids, mine, theirs, u, grads, *rest):
+        outs, made = rest[:NZ], rest[NZ]
+        z, x, c = ids[0], ids[1], ids[3]
+        last = lax.broadcasted_iota(jnp.int32, (part, length), 1) == length - 1
+        for core in range(2):
+            now = jnp.where(c == core, mine[...].astype(F32), theirs[...].astype(F32))
+            after = jnp.where(last, 0.0, pltpu.roll(now, length - 1, 1))
+            grads[pl.ds(core * 2 * part, 2 * part), :] = jnp.concatenate([after, now], axis=0).astype(BF)
+        contract = (((1,), (1,)), ((), ()))
+        for y in range(2):
+            made[y] = lax.dot_general(
+                grads[...], u[pl.ds(y * rows, rows), :], contract, preferred_element_type=F32
+            )
+        sums = lax.dot_general(jnp.ones((8, length), BF), grads[...], contract, preferred_element_type=F32)
+        line = lax.broadcasted_iota(jnp.int32, (8, part), 0)
+        tails = []
+        for r in range(2):
+            bias = jnp.where(flip(x, r) == 0, sums[:, part : 2 * part], sums[:, 3 * part : 4 * part])
+            high = bias.astype(BF).astype(F32)
+            tail = jnp.where(line == 0, high, jnp.where(line == 1, bias - high, 0.0))
+            tails.append(jnp.concatenate([tail, jnp.zeros((8, rows - part), F32)], axis=1))
+        for dz in range(NZ):
+            source = mod(z - dz)
+            both = []
+            for r in range(2):
+                at = pl.ds(pl.multiple_of((flip(x, r) * 2 + source // 2) * part, 8), part)
+                both.append(jnp.concatenate([made[lax.rem(source, 2), at, :], tails[r]], axis=0))
+            outs[dz][...] = jnp.concatenate(both, axis=1).astype(BF)
 
     made = call(
         body,
-        [((total, length), BF)] + [(shape, F32), (shape, F32), (shape, F32), (half, BF), (half, BF)] * NZ,
-        [ids, tall, mine, theirs],
-        [pltpu.VMEM((depth, length), F32)],
+        [((total, length), BF)] + [((part + 8, 2 * rows), BF)] * NZ,
+        [ids, mine, theirs, u],
+        [pltpu.VMEM((2, total, rows), F32)],
+        after=after,
+        flops=2 * depth * total * length,
     )
     return made[0], made[1:]
 
 
-def weight_blocks(ids, grads, u, bias_mine, bias_theirs):
-    total, length = grads.shape
-    depth = u.shape[0]
-    part, rows = total // 4, depth // 2
-    lanes = -(-(rows + 2) // LANES) * LANES
-
-    def body(ids, grads, u, bias_mine, bias_theirs, *rest):
-        outs, made = rest[:8], rest[8]
-        z, x, c = ids[0], ids[1], ids[3]
-        for y in range(2):
-            made[y, :, pl.ds(0, rows)] = lax.dot_general(
-                grads[...], u[pl.ds(y * rows, rows), :], (((1,), (1,)), ((), ())), preferred_element_type=F32
-            )
-        lane = lax.broadcasted_iota(jnp.int32, (part, lanes), 1)
-        for r in range(2):
-            core = flip(x, r)
-            bias = jnp.where(core == c, bias_mine[:, :1], bias_theirs[:, :1])
-            high = bias.astype(BF).astype(F32)
-            for dz in range(NZ):
-                source = mod(z - dz)
-                at = pl.ds(pl.multiple_of((core * 2 + source // 2) * part, 8), part)
-                block = made[lax.rem(source, 2), at, :]
-                block = jnp.where(lane < rows, block, jnp.where(lane == rows, high, bias - high))
-                outs[dz * 2 + r][...] = block.astype(BF)
-
-    return call(
-        body,
-        [((part, lanes), BF)] * 8,
-        [ids, grads, u, bias_mine, bias_theirs],
-        [pltpu.VMEM((2, total, lanes), F32)],
-    )
-
-
-def unpack_weight(ids, blocks, rows):
-    part, lanes = blocks[0].shape
+def unpack_weight(ids, groups):
+    _, height, width = groups[0].shape
+    part, rows = height - 8, width // 2
     own = part // 3
     columns = own * 8
 
-    def body(ids, *rest):
-        ins, (out, bias), joined = rest[:8], rest[8:10], rest[10]
+    def body(ids, r0, r1, out, bias, joined):
         z, c = ids[0], ids[3]
-        for dz in range(NZ):
-            for r in range(2):
-                i = mod(z + dz) * 2 + flip(c, r)
-                for g in range(3):
-                    at = pl.ds(pl.multiple_of(i * own, 8), own)
-                    joined[g, at, :] = ins[dz * 2 + r][pl.ds(g * own, own), :].astype(F32)
+        for r, group in enumerate((r0, r1)):
+            for pair in range(NZ // 2):
+                both = group[pair].astype(F32)
+                for k in range(2):
+                    i = mod(z + 2 * pair + k) * 2 + flip(c, r)
+                    block = both[:, k * rows : (k + 1) * rows]
+                    for g in range(3):
+                        at = pl.ds(pl.multiple_of(i * own, 8), own)
+                        joined[g, at, :] = block[g * own : (g + 1) * own]
+                    bias[pl.ds(i, 1), :] = (block[part : part + 1] + block[part + 1 : part + 2])[:, :part]
         for g in range(3):
-            turned = joined[g].T
-            out[g] = turned[:rows]
-            bias[pl.ds(g, 1), :] = turned[rows : rows + 1] + turned[rows + 1 : rows + 2]
+            out[g] = joined[g].T
 
     grad, bias = call(
         body,
-        [((3, rows, columns), F32), ((3, columns), F32)],
-        [ids, *blocks],
-        [pltpu.VMEM((3, columns, lanes), F32)],
-    )
-    return jnp.transpose(grad, (1, 0, 2)), bias
+        [((3, rows, columns), F32), ((8, part), F32)],
+        [ids, *groups],
+        [pltpu.VMEM((3, columns, rows), F32)],
+    )
+    bias = jnp.transpose(bias.reshape(8, 3, own), (1, 0, 2)).reshape(3, columns)
+    return grad, bias
 
 
 def owned_bias(bias, own):
@@ -501,35 +616,49 @@
 def owned_channels(inputs, first_weight, first_bias, second_weight, second_bias, cotangent):
     tm, mp = lax.axis_index("tm"), lax.axis_index("mp")
     ids = jnp.stack([tm // 2, tm % 2, mp // 2, mp % 2]).astype(jnp.int32)
-    rows = first_weight.shape[0]
     own = first_weight.shape[2] // 8
 
-    w1_sent = send_blocks(pack_weight(ids, first_weight))
-    u_found = gather_chips(inputs[0].T, 0)
-    wide_1, tall_1 = join_weight(ids, w1_sent)
-    w2_sent = send_blocks(pack_weight(ids, second_weight))
-    cot_pieces = over_tm(split_cotangent(ids, cotangent[0].T))
-
-    u, mine, theirs = partial_gates(ids, wide_1, u_found, False)
-    hidden, *saved = first_cells(ids, mine, over_core(theirs), owned_bias(first_bias, own))
-    wide_2, tall_2 = join_weight(ids, w2_sent)
-    h_found = gather_chips(hidden, 1)
-    h, mine, theirs = partial_gates(ids, wide_2, h_found, True)
-    out_pieces, gate_grad, bias_2 = second_cells(
-        ids, mine, over_core(theirs), owned_bias(second_bias, own), cot_pieces
-    )
-    outputs = join_outputs(ids, over_tm(out_pieces))
-
-    grads, parts = input_parts(ids, tall_2, gate_grad, over_core(gate_grad), True)
-    hidden_grad = sum_chips(parts, 1)
-    blocks = weight_blocks(ids, grads, h, bias_2, over_core(bias_2))
-    second_grad, second_bias_grad = unpack_weight(ids, return_blocks(blocks), rows)
-
-    gate_grad, bias_1 = first_gate_grad(ids, hidden_grad, saved)
-    grads, parts = input_parts(ids, tall_1, gate_grad, over_core(gate_grad), False)
-    input_grad = sum_chips(parts, 0)
-    blocks = weight_blocks(ids, grads, u, bias_1, over_core(bias_1))
-    first_grad, first_bias_grad = unpack_weight(ids, return_blocks(blocks), rows)
+    *w1, u_piece = pack_weight(ids, first_weight, inputs[0].T)
+    near, w1, _ = regroup(ids, along_z(u_piece), blocks_over_x(w1))
+    u_found = gather_plane(near, 0)
+    wide_1, tall_1 = join_weight(ids, blocks_over_z(w1, 1))
+    w2 = pack_weight(ids, second_weight, after=u_found[3:])
+
+    u, mine, theirs = partial_gates(ids, wide_1, u_found, False, after=w2)
+    w2 = blocks_over_x(w2)
+    hidden, *saved = first_cells(relay(ids, w2), mine, over_core(theirs), owned_bias(first_bias, own))
+    cot_here, cot_there = split_cotangent(ids, cotangent[0].T)
+    cots = pair_up(ids, cot_here, over_x(cot_there))
+    near, w2, _ = regroup(ids, along_z(hidden), w2, after=cots)
+    h_found = gather_plane(near, 1)
+    wide_2, tall_2 = join_weight(ids, blocks_over_z(w2, 1))
+    cots = [cots[0]] + [over_z(cots[dz], dz) for dz in range(1, NZ)]
+    h, mine, theirs = partial_gates(ids, wide_2, h_found, True, after=cots)
+    outs, gate_grad = second_cells(ids, mine, over_core(theirs), owned_bias(second_bias, own), cots)
+
+    grads, dw2 = weight_blocks(ids, gate_grad, over_core(gate_grad), h)
+    outs = pair_up(ids, outs[0], over_x(outs[1]))
+    parts = input_parts(ids, tall_2, grads, True, after=outs)
+    dw2 = blocks_over_z(dw2, -1)
+    sent_x, sent_y = add_diagonal(ids, parts, 1)
+    dw2 = regroup_back(ids, dw2)
+    planes = add_plane(ids, parts[0], over_x(sent_x), over_y(sent_y), after=dw2)
+    hidden_grad = sum_planes(planes)
+    dw2 = blocks_over_x(dw2, True)
+    gate_grad = first_gate_grad(ids, hidden_grad, saved, after=dw2)
+
+    grads, dw1 = weight_blocks(ids, gate_grad, over_core(gate_grad), u)
+    outs = [outs[0]] + [over_z(outs[dz], dz) for dz in range(1, NZ)]
+    parts = input_parts(ids, tall_1, grads, False, after=outs)
+    dw1 = blocks_over_z(dw1, -1)
+    second_grad, second_bias_grad = unpack_weight(ids, dw2)
+    outputs = join_outputs(ids, outs)
+    sent_x, sent_y = add_diagonal(ids, parts, 0, after=[second_grad, outputs])
+    dw1 = regroup_back(ids, dw1)
+    planes = add_plane(ids, parts[0], over_x(sent_x), over_y(sent_y), after=dw1)
+    input_grad = sum_planes(planes)
+    first_grad, first_bias_grad = unpack_weight(ids, blocks_over_x(dw1, True))
+    first_grad, second_grad = (jnp.transpose(grad, (1, 0, 2)) for grad in (first_grad, second_grad))
     return (
         outputs.T[None],
         input_grad.T[None],

time: 545 us -> 482 us (0.88)
  starting transfers between devices: 218 us -> 71.5 us
  waiting for transfers between devices: 184 us -> 281 us
  Pallas kernels: 109 us -> 91.7 us
  local copies, waits for them, and re-layouts: 20.9 us -> 30.3 us
    ppermute x128 -> x60, starting transfers between devices: 218 us -> 71.5 us  [moved(): return lax.ppermute(array, ('tm', 'mp'), pairs)]
    ppermute x128 -> x60, waiting for transfers between devices: 184 us -> 281 us  [moved(): return lax.ppermute(array, ('tm', 'mp'), pairs)]
    pallas_call x17 -> x28, Pallas kernels: 109 us -> 91.7 us  [the longest x27 91.7 us: call(): pl.pallas_call(run, out_shape=[jax.ShapeDtypeStruct(shape, kind) for shap...]
    unnamed x108 -> x93, local copies, waits for them, and re-layouts: 15.2 us -> 24.4 us
  transfers between devices with their start and end apart: 128 -> 60, of which waited for: 46 -> 35; matrix products, arithmetic and copies ran while one was open for 2% -> 1% of each run, Pallas kernels for 7% -> 9%
where the time goes in v2:
time: 482 us; the launch traced here: 478 us
  waiting for transfers between devices  281 us (58%)
  Pallas kernels  91.7 us (19%)
  starting transfers between devices  71.5 us (15%)
  local copies, waits for them, and re-layouts  30.3 us (6%)
    ppermute x60, waiting for transfers between devices, moved(): return lax.ppermute(array, ('tm', 'mp'), pairs)  281 us
    pallas_call x27, Pallas kernels, call(): pl.pallas_call(run, out_shape=[jax.ShapeDtypeStruct(shape, kind) for shap...  91.7 us
    ppermute x60, starting transfers between devices, moved(): return lax.ppermute(array, ('tm', 'mp'), pairs)  71.5 us
    unnamed x93, local copies, waits for them, and re-layouts  24.4 us
  transfers between devices with their start and end apart: 60, of which 35 were waited for; matrix products, arithmetic and copies ran while one was open for 1% of the time, Pallas kernels for 9%

profile of v2, /device:TPU:8, one launch (start us, length us, event | category | flops | bytes accessed | tf_op | source)
XLA Modules:
  0.0 478.1 jit_solution(15971921883503334722)
XLA Ops:
  13.0 16.8 %collective-permute-done.refs_2_ = bf16[576,256]{1,0:T(8,128)(2,1)S(1)} collective-permute-done((bf16[576,256]{1,0:T(8,128)(2,1)S(1)}, bf16[576,256]{1,0:T(8,128)(2,1)S(1)}, u32[]{:S(2)}, u32[]{:S(2)}) %collective-permute-start) | collective-permute-done | bytes 294944 | tf_op jit(solution)/shard_map/ppermute | solution.py:32
  29.9 5.7 %collective-permute-done.1.refs_3_ = bf16[576,256]{1,0:T(8,128)(2,1)S(1)} collective-permute-done((bf16[576,256]{1,0:T(8,128)(2,1)S(1)}, bf16[576,256]{1,0:T(8,128)(2,1)S(1)}, u32[]{:S(2)}, u32[]{:S(2)}) %collective-permute-start.1) | collective-permute-done | bytes 294944 | tf_op jit(solution)/shard_map/ppermute | solution.py:32
  43.5 24.6 %collective-permute-done.5.refs_3_ = bf16[4,576,256]{2,1,0:T(8,128)(2,1)S(1)} collective-permute-done((bf16[4,576,256]{2,1,0:T(8,128)(2,1)S(1)}, bf16[4,576,256]{2,1,0:T(8,128)(2,1)S(1)}, u32[]{:S(2)}, u32[]{:S(2)}) %collective-permute-start.5) | collective-permute-done | bytes 1179680 | tf_op jit(solution)/shard_map/ppermute | solution.py:32
  77.4 6.2 %collective-permute-done.6.refs_2_.refs_5_ = bf16[4,288,256]{2,1,0:T(8,128)(2,1)S(1)} collective-permute-done((bf16[4,288,256]{2,1,0:T(8,128)(2,1)}, bf16[4,288,256]{2,1,0:T(8,128)(2,1)S(1)}, u32[]{:S(2)}, u32[]{:S(2)}) %collective-permute-start.6) | collective-permute-done | bytes 589856 | tf_op jit(solution)/shard_map/ppermute | solution.py:32
  90.7 15.1 %collective-permute-done.11.refs_2_ = bf16[216,1152]{1,0:T(8,128)(2,1)} collective-permute-done((bf16[216,1152]{1,0:T(8,128)(2,1)}, bf16[216,1152]{1,0:T(8,128)(2,1)}, u32[]{:S(2)}, u32[]{:S(2)}) %collective-permute-start.11) | collective-permute-done | bytes 497696 | tf_op jit(solution)/shard_map/ppermute | solution.py:32
  105.9 8.8 %collective-permute-done.12.refs_3_ = bf16[216,1152]{1,0:T(8,128)(2,1)} collective-permute-done((bf16[216,1152]{1,0:T(8,128)(2,1)}, bf16[216,1152]{1,0:T(8,128)(2,1)}, u32[]{:S(2)}, u32[]{:S(2)}) %collective-permute-start.12) | collective-permute-done | bytes 497696 | tf_op jit(solution)/shard_map/ppermute | solution.py:32
  120.1 8.0 %shard_map.114 = (bf16[1152,2048]{1,0:T(8,128)(2,1)S(1)}, f32[216,2048]{1,0:T(8,128)S(1)}, f32[216,2048]{1,0:T(8,128)}) custom-call(s32[4]{0:T(128)S(1)} %pad_add_fusion.refs_0_, bf16[864,1152]{1,0:T(8,128)(2,1)S(1)} %get-tuple-element.99.refs_1_, bf16[4,576,256]{2,1,0:T(8,128)(2,1)S(1)} %copy-done.34, bf16[4,576,256]{2,1,0:T(8,128)(2,1)S(1)} %copy-done.19, ...), custom_call_target="tpu_custom_call" | custom-call | flops 4076863488 | bytes 14966800 | tf_op jit(solution)/shard_map/pallas_call | solution.py:66
  152.6 16.0 %collective-permute-done.16.refs_3_ = bf16[72,2048]{1,0:T(8,128)(2,1)S(1)} collective-permute-done((bf16[72,2048]{1,0:T(8,128)(2,1)S(1)}, bf16[72,2048]{1,0:T(8,128)(2,1)S(1)}, u32[]{:S(2)}, u32[]{:S(2)}) %collective-permute-start.16) | collective-permute-done | bytes 294944 | tf_op jit(solution)/shard_map/ppermute | solution.py:32
  176.8 23.1 %collective-permute-done.22.refs_3_ = bf16[4,72,2048]{2,1,0:T(8,128)(2,1)S(1)} collective-permute-done((bf16[4,72,2048]{2,1,0:T(8,128)(2,1)S(1)}, bf16[4,72,2048]{2,1,0:T(8,128)(2,1)S(1)}, u32[]{:S(2)}, u32[]{:S(2)}) %collective-permute-start.22) | collective-permute-done | bytes 1179680 | tf_op jit(solution)/shard_map/ppermute | solution.py:32
  203.9 16.7 %collective-permute-done.20.refs_3_ = bf16[216,1152]{1,0:T(8,128)(2,1)S(1)} collective-permute-done((bf16[216,1152]{1,0:T(8,128)(2,1)S(1)}, bf16[216,1152]{1,0:T(8,128)(2,1)S(1)}, u32[]{:S(2)}, u32[]{:S(2)}) %collective-permute-start.20) | collective-permute-done | bytes 497696 | tf_op jit(solution)/shard_map/ppermute | solution.py:32
  225.1 8.3 %collective-permute-done.24.refs_5_ = bf16[4,72,1024]{2,1,0:T(8,128)(2,1)S(1)} collective-permute-done((bf16[4,72,1024]{2,1,0:T(8,128)(2,1)S(1)}, bf16[4,72,1024]{2,1,0:T(8,128)(2,1)S(1)}, u32[]{:S(2)}, u32[]{:S(2)}) %collective-permute-start.24) | collective-permute-done | bytes 589856 | tf_op jit(solution)/shard_map/ppermute | solution.py:32
  236.0 9.1 %shard_map.120 = (bf16[1152,2048]{1,0:T(8,128)(2,1)S(1)}, f32[216,2048]{1,0:T(8,128)S(1)}, f32[216,2048]{1,0:T(8,128)}) custom-call(s32[4]{0:T(128)S(1)} %pad_add_fusion.refs_0_, bf16[864,1152]{1,0:T(8,128)(2,1)S(1)} %get-tuple-element.113.refs_1_, bf16[4,72,2048]{2,1,0:T(8,128)(2,1)S(1)} %get-tuple-element.114.refs_2_, ...), custom_call_target="tpu_custom_call" | custom-call | flops 4076863488 | bytes 14966800 | tf_op jit(solution)/shard_map/pallas_call | solution.py:66
  255.7 7.4 %shard_map.121 = (bf16[4,72,256]{2,1,0:T(8,128)(2,1)S(1)}, bf16[4,72,256]{2,1,0:T(8,128)(2,1)S(1)}, bf16[216,2048]{1,0:T(8,128)(2,1)S(1)}) custom-call(s32[4]{0:T(128)S(1)} %pad_add_fusion.refs_0_, f32[216,2048]{1,0:T(8,128)S(1)} %get-tuple-element.115.refs_1_, f32[216,2048]{1,0:T(8,128)S(1)} %collective-permute-done.29.refs_2_, f32[216,1]{1,0:T(8,128)S(1)} %copy-done.17, ...), custom_call_target="tpu_custom_call" | custom-call | bytes 5014384 | tf_op jit(solution)/shard_map/pallas_call | solution.py:66
  272.3 7.9 %shard_map.124 = (bf16[864,2048]{1,0:T(8,128)(2,1)S(1)}, bf16[224,1152]{1,0:T(8,128)(2,1)S(1)}, bf16[224,1152]{1,0:T(8,128)(2,1)S(1)}, bf16[224,1152]{1,0:T(8,128)(2,1)S(1)}, bf16[224,1152]{1,0:T(8,128)(2,1)S(1)}) custom-call(s32[4]{0:T(128)S(1)} %pad_add_fusion.refs_0_, bf16[216,2048]{1,0:T(8,128)(2,1)S(1)} %get-tuple-element.125.refs_1_, ...), custom_call_target="tpu_custom_call" | custom-call | flops 4076863488 | bytes 12091408 | tf_op jit(solution)/shard_map/pallas_call | solution.py:66
  280.2 6.2 %shard_map.125 = (f32[4,72,2048]{2,1,0:T(8,128)S(1)}, f32[4,72,2048]{2,1,0:T(8,128)S(1)}, f32[4,72,2048]{2,1,0:T(8,128)S(1)}, bf16[4,72,1024]{2,1,0:T(8,128)(2,1)S(1)}, bf16[4,72,1024]{2,1,0:T(8,128)(2,1)S(1)}) custom-call(s32[4]{0:T(128)S(1)} %pad_add_fusion.refs_0_, bf16[1152,864]{1,0:T(8,128)(2,1)S(1)} %copy-done.43, ...), custom_call_target="tpu_custom_call" | custom-call | flops 4076863488 | bytes 13787152 | tf_op jit(solution)/shard_map/pallas_call | solution.py:66
  292.9 8.3 %collective-permute-done.35.refs_3_ = bf16[4,72,1024]{2,1,0:T(8,128)(2,1)S(1)} collective-permute-done((bf16[4,72,1024]{2,1,0:T(8,128)(2,1)S(1)}, bf16[4,72,1024]{2,1,0:T(8,128)(2,1)S(1)}, u32[]{:S(2)}, u32[]{:S(2)}) %collective-permute-start.35) | collective-permute-done | bytes 589856 | tf_op jit(solution)/shard_map/ppermute | solution.py:32
  305.6 20.8 %collective-permute-done.39.refs_2_ = bf16[224,1152]{1,0:T(8,128)(2,1)S(1)} collective-permute-done((bf16[224,1152]{1,0:T(8,128)(2,1)S(1)}, bf16[224,1152]{1,0:T(8,128)(2,1)S(1)}, u32[]{:S(2)}, u32[]{:S(2)}) %collective-permute-start.39) | collective-permute-done | bytes 516128 | tf_op jit(solution)/shard_map/ppermute | solution.py:32
  326.4 7.3 %collective-permute-done.41.refs_4_ = bf16[224,1152]{1,0:T(8,128)(2,1)S(1)} collective-permute-done((bf16[224,1152]{1,0:T(8,128)(2,1)S(1)}, bf16[224,1152]{1,0:T(8,128)(2,1)S(1)}, u32[]{:S(2)}, u32[]{:S(2)}) %collective-permute-start.41) | collective-permute-done | bytes 516128 | tf_op jit(solution)/shard_map/ppermute | solution.py:32
  343.7 17.4 %collective-permute-done.42 = bf16[72,2048]{1,0:T(8,128)(2,1)S(1)} collective-permute-done((bf16[72,2048]{1,0:T(8,128)(2,1)S(1)}, bf16[72,2048]{1,0:T(8,128)(2,1)S(1)}, u32[]{:S(2)}, u32[]{:S(2)}) %collective-permute-start.42) | collective-permute-done | bytes 294944 | tf_op jit(solution)/shard_map/ppermute | solution.py:32
  376.5 7.9 %shard_map.130 = (bf16[864,2048]{1,0:T(8,128)(2,1)S(1)}, bf16[224,1152]{1,0:T(8,128)(2,1)S(1)}, bf16[224,1152]{1,0:T(8,128)(2,1)S(1)}, bf16[224,1152]{1,0:T(8,128)(2,1)S(1)}, bf16[224,1152]{1,0:T(8,128)(2,1)S(1)}) custom-call(s32[4]{0:T(128)S(1)} %pad_add_fusion.refs_0_, bf16[216,2048]{1,0:T(8,128)(2,1)S(1)} %shard_map.129.refs_1_, ...), custom_call_target="tpu_custom_call" | custom-call | flops 4076863488 | bytes 12091408 | tf_op jit(solution)/shard_map/pallas_call | solution.py:66
  384.4 6.3 %shard_map.131 = (f32[4,576,256]{2,1,0:T(8,128)S(1)}, f32[4,576,256]{2,1,0:T(8,128)S(1)}, f32[4,576,256]{2,1,0:T(8,128)S(1)}, bf16[4,288,256]{2,1,0:T(8,128)(2,1)S(1)}, bf16[4,288,256]{2,1,0:T(8,128)(2,1)S(1)}) custom-call(s32[4]{0:T(128)S(1)} %pad_add_fusion.refs_0_, bf16[1152,864]{1,0:T(8,128)(2,1)S(1)} %copy-done.41, ...), custom_call_target="tpu_custom_call" | custom-call | flops 4076863488 | bytes 13787152 | tf_op jit(solution)/shard_map/pallas_call | solution.py:66
  411.2 18.3 %collective-permute-done.52.refs_2_ = bf16[224,1152]{1,0:T(8,128)(2,1)S(1)} collective-permute-done((bf16[224,1152]{1,0:T(8,128)(2,1)S(1)}, bf16[224,1152]{1,0:T(8,128)(2,1)S(1)}, u32[]{:S(2)}, u32[]{:S(2)}) %collective-permute-start.52) | collective-permute-done | bytes 516128 | tf_op jit(solution)/shard_map/ppermute | solution.py:32
  429.5 8.1 %collective-permute-done.54.refs_4_ = bf16[224,1152]{1,0:T(8,128)(2,1)S(1)} collective-permute-done((bf16[224,1152]{1,0:T(8,128)(2,1)S(1)}, bf16[224,1152]{1,0:T(8,128)(2,1)S(1)}, u32[]{:S(2)}, u32[]{:S(2)}) %collective-permute-start.54) | collective-permute-done | bytes 516128 | tf_op jit(solution)/shard_map/ppermute | solution.py:32
  451.2 15.7 %collective-permute-done.59.refs_2_ = bf16[2,224,1152]{2,1,0:T(8,128)(2,1)S(1)} collective-permute-done((bf16[2,224,1152]{2,1,0:T(8,128)(2,1)S(1)}, bf16[2,224,1152]{2,1,0:T(8,128)(2,1)S(1)}, u32[]{:S(2)}, u32[]{:S(2)}) %collective-permute-start.59) | collective-permute-done | bytes 1032224 | tf_op jit(solution)/shard_map/ppermute | solution.py:32
  (235 shorter events, 186.6 us)
Async XLA Ops:
  5.0 32.4 %collective-permute-start.3 = (bf16[2,216,1152]{2,1,0:T(8,128)(2,1)S(1)}, bf16[2,216,1152]{2,1,0:T(8,128)(2,1)S(1)}, u32[]{:S(2)}, u32[]{:S(2)}) collective-permute-start(bf16[2,216,1152]{2,1,0:T(8,128)(2,1)S(1)} %get-tuple-element.90), channel_id=1, source_target_pairs={{0,0},{1,4},{2,2},{3,6},{4,1},{5,5},{6,3},{7,7},{8,8},{9,12},{10,1... | collective-permute-start | bytes 2985992 | tf_op jit(solution)/shard_map/ppermute | solution.py:32
  5.7 31.6 %collective-permute-start.4 = (bf16[2,216,1152]{2,1,0:T(8,128)(2,1)S(1)}, bf16[2,216,1152]{2,1,0:T(8,128)(2,1)S(1)}, u32[]{:S(2)}, u32[]{:S(2)}) collective-permute-start(bf16[2,216,1152]{2,1,0:T(8,128)(2,1)S(1)} %get-tuple-element.91), channel_id=1, source_target_pairs={{0,4},{1,0},{2,6},{3,2},{4,5},{5,1},{6,7},{7,3},{8,12},{9,8},{10,1... | collective-permute-start | bytes 2985992 | tf_op jit(solution)/shard_map/ppermute | solution.py:32
  40.9 29.6 %collective-permute-start.7 = (bf16[4,576,256]{2,1,0:T(8,128)(2,1)S(1)}, bf16[4,576,256]{2,1,0:T(8,128)(2,1)S(1)}, u32[]{:S(2)}, u32[]{:S(2)}) collective-permute-start(bf16[4,576,256]{2,1,0:T(8,128)(2,1)S(1)} %get-tuple-element.92.refs_2_), channel_id=1, source_target_pairs={{0,2},{1,3},{2,0},{3,1},{4,6},{5,7},{6,4},{7,5},{8,10},{9,11},{10,... | collective-permute-start | bytes 3538952 | tf_op jit(solution)/shard_map/ppermute | solution.py:32
  72.5 33.3 %collective-permute-start.11 = (bf16[216,1152]{1,0:T(8,128)(2,1)}, bf16[216,1152]{1,0:T(8,128)(2,1)}, u32[]{:S(2)}, u32[]{:S(2)}) collective-permute-start(bf16[216,1152]{1,0:T(8,128)(2,1)} %get-tuple-element.96), channel_id=1, source_target_pairs={{0,8},{1,9},{2,10},{3,11},{4,12},{5,13},{6,14},{7,15},{8,16},{9,17... | collective-permute-start | bytes 1493000 | tf_op jit(solution)/shard_map/ppermute | solution.py:32
  72.5 42.1 %collective-permute-start.12 = (bf16[216,1152]{1,0:T(8,128)(2,1)}, bf16[216,1152]{1,0:T(8,128)(2,1)}, u32[]{:S(2)}, u32[]{:S(2)}) collective-permute-start(bf16[216,1152]{1,0:T(8,128)(2,1)} %get-tuple-element.97), channel_id=1, source_target_pairs={{0,16},{1,17},{2,18},{3,19},{4,20},{5,21},{6,22},{7,23},{8,24},{9,... | collective-permute-start | bytes 1493000 | tf_op jit(solution)/shard_map/ppermute | solution.py:32
  74.0 43.2 %collective-permute-start.13 = (bf16[216,1152]{1,0:T(8,128)(2,1)}, bf16[216,1152]{1,0:T(8,128)(2,1)}, u32[]{:S(2)}, u32[]{:S(2)}) collective-permute-start(bf16[216,1152]{1,0:T(8,128)(2,1)} %get-tuple-element.98), channel_id=1, source_target_pairs={{0,24},{1,25},{2,26},{3,27},{4,28},{5,29},{6,30},{7,31},{8,0},{9,1... | collective-permute-start | bytes 1493000 | tf_op jit(solution)/shard_map/ppermute | solution.py:32
  87.7 42.7 %collective-permute-start.10 = (bf16[2,216,1152]{2,1,0:T(8,128)(2,1)S(1)}, bf16[2,216,1152]{2,1,0:T(8,128)(2,1)}, u32[]{:S(2)}, u32[]{:S(2)}) collective-permute-start(bf16[2,216,1152]{2,1,0:T(8,128)(2,1)S(1)} %get-tuple-element.94.refs_8_), channel_id=1, source_target_pairs={{0,4},{1,0},{2,6},{3,2},{4,5},{5,1},{6,7},{7,3},{8,12},{9,8},{10,1... | collective-permute-start | bytes 2985992 | tf_op jit(solution)/shard_map/ppermute | solution.py:32
  88.6 41.7 %collective-permute-start.9 = (bf16[2,216,1152]{2,1,0:T(8,128)(2,1)S(1)}, bf16[2,216,1152]{2,1,0:T(8,128)(2,1)}, u32[]{:S(2)}, u32[]{:S(2)}) collective-permute-start(bf16[2,216,1152]{2,1,0:T(8,128)(2,1)S(1)} %get-tuple-element.93.refs_7_), channel_id=1, source_target_pairs={{0,0},{1,4},{2,2},{3,6},{4,1},{5,5},{6,3},{7,7},{8,8},{9,12},{10,1... | collective-permute-start | bytes 2985992 | tf_op jit(solution)/shard_map/ppermute | solution.py:32
  171.9 28.0 %collective-permute-start.22 = (bf16[4,72,2048]{2,1,0:T(8,128)(2,1)S(1)}, bf16[4,72,2048]{2,1,0:T(8,128)(2,1)S(1)}, u32[]{:S(2)}, u32[]{:S(2)}) collective-permute-start(bf16[4,72,2048]{2,1,0:T(8,128)(2,1)S(1)} %get-tuple-element.114.refs_2_), channel_id=1, source_target_pairs={{0,4},{1,5},{2,6},{3,7},{4,0},{5,1},{6,2},{7,3},{8,12},{9,13},{10,... | collective-permute-start | bytes 3538952 | tf_op jit(solution)/shard_map/ppermute | solution.py:32
  173.6 28.0 %collective-permute-start.19 = (bf16[216,1152]{1,0:T(8,128)(2,1)S(1)}, bf16[216,1152]{1,0:T(8,128)(2,1)S(1)}, u32[]{:S(2)}, u32[]{:S(2)}) collective-permute-start(bf16[216,1152]{1,0:T(8,128)(2,1)S(1)} %get-tuple-element.110), channel_id=1, source_target_pairs={{0,8},{1,9},{2,10},{3,11},{4,12},{5,13},{6,14},{7,15},{8,16},{9,17... | collective-permute-start | bytes 1493000 | tf_op jit(solution)/shard_map/ppermute | solution.py:32
  173.6 47.0 %collective-permute-start.20 = (bf16[216,1152]{1,0:T(8,128)(2,1)S(1)}, bf16[216,1152]{1,0:T(8,128)(2,1)S(1)}, u32[]{:S(2)}, u32[]{:S(2)}) collective-permute-start(bf16[216,1152]{1,0:T(8,128)(2,1)S(1)} %get-tuple-element.111), channel_id=1, source_target_pairs={{0,16},{1,17},{2,18},{3,19},{4,20},{5,21},{6,22},{7,23},{8,24},{9,... | collective-permute-start | bytes 1493000 | tf_op jit(solution)/shard_map/ppermute | solution.py:32
  174.8 47.3 %collective-permute-start.21 = (bf16[216,1152]{1,0:T(8,128)(2,1)S(1)}, bf16[216,1152]{1,0:T(8,128)(2,1)S(1)}, u32[]{:S(2)}, u32[]{:S(2)}) collective-permute-start(bf16[216,1152]{1,0:T(8,128)(2,1)S(1)} %get-tuple-element.112), channel_id=1, source_target_pairs={{0,24},{1,25},{2,26},{3,27},{4,28},{5,29},{6,30},{7,31},{8,0},{9,1... | collective-permute-start | bytes 1493000 | tf_op jit(solution)/shard_map/ppermute | solution.py:32
  289.6 36.8 %collective-permute-start.39 = (bf16[224,1152]{1,0:T(8,128)(2,1)S(1)}, bf16[224,1152]{1,0:T(8,128)(2,1)S(1)}, u32[]{:S(2)}, u32[]{:S(2)}) collective-permute-start(bf16[224,1152]{1,0:T(8,128)(2,1)S(1)} %get-tuple-element.136), channel_id=1, source_target_pairs={{0,24},{1,25},{2,26},{3,27},{4,28},{5,29},{6,30},{7,31},{8,0},{9,1... | collective-permute-start | bytes 1548296 | tf_op jit(solution)/shard_map/ppermute | solution.py:32
  289.6 36.8 %collective-permute-start.40 = (bf16[224,1152]{1,0:T(8,128)(2,1)S(1)}, bf16[224,1152]{1,0:T(8,128)(2,1)S(1)}, u32[]{:S(2)}, u32[]{:S(2)}) collective-permute-start(bf16[224,1152]{1,0:T(8,128)(2,1)S(1)} %get-tuple-element.137), channel_id=1, source_target_pairs={{0,16},{1,17},{2,18},{3,19},{4,20},{5,21},{6,22},{7,23},{8,24},{9,... | collective-permute-start | bytes 1548296 | tf_op jit(solution)/shard_map/ppermute | solution.py:32
  290.6 43.1 %collective-permute-start.41 = (bf16[224,1152]{1,0:T(8,128)(2,1)S(1)}, bf16[224,1152]{1,0:T(8,128)(2,1)S(1)}, u32[]{:S(2)}, u32[]{:S(2)}) collective-permute-start(bf16[224,1152]{1,0:T(8,128)(2,1)S(1)} %get-tuple-element.138), channel_id=1, source_target_pairs={{0,8},{1,9},{2,10},{3,11},{4,12},{5,13},{6,14},{7,15},{8,16},{9,17... | collective-permute-start | bytes 1548296 | tf_op jit(solution)/shard_map/ppermute | solution.py:32
  303.3 34.2 %collective-permute-start.37 = (bf16[4,72,2048]{2,1,0:T(8,128)(2,1)S(1)}, bf16[4,72,2048]{2,1,0:T(8,128)(2,1)S(1)}, u32[]{:S(2)}, u32[]{:S(2)}) collective-permute-start(bf16[4,72,2048]{2,1,0:T(8,128)(2,1)S(1)} %get-tuple-element.133), channel_id=1, source_target_pairs={{0,4},{1,5},{2,6},{3,7},{4,0},{5,1},{6,2},{7,3},{8,12},{9,13},{10,... | collective-permute-start | bytes 3538952 | tf_op jit(solution)/shard_map/ppermute | solution.py:32
  305.0 32.5 %collective-permute-start.38 = (bf16[4,72,2048]{2,1,0:T(8,128)(2,1)S(1)}, bf16[4,72,2048]{2,1,0:T(8,128)(2,1)S(1)}, u32[]{:S(2)}, u32[]{:S(2)}) collective-permute-start(bf16[4,72,2048]{2,1,0:T(8,128)(2,1)S(1)} %get-tuple-element.134), channel_id=1, source_target_pairs={{0,2},{1,3},{2,0},{3,1},{4,6},{5,7},{6,4},{7,5},{8,10},{9,11},{10,... | collective-permute-start | bytes 3538952 | tf_op jit(solution)/shard_map/ppermute | solution.py:32
  334.6 34.3 %collective-permute-start.45 = (bf16[2,224,1152]{2,1,0:T(8,128)(2,1)S(1)}, bf16[2,224,1152]{2,1,0:T(8,128)(2,1)S(1)}, u32[]{:S(2)}, u32[]{:S(2)}) collective-permute-start(bf16[2,224,1152]{2,1,0:T(8,128)(2,1)S(1)} %get-tuple-element.139.refs_4_), channel_id=1, source_target_pairs={{0,0},{1,4},{2,2},{3,6},{4,1},{5,5},{6,3},{7,7},{8,8},{9,12},{10,1... | collective-permute-start | bytes 3096584 | tf_op jit(solution)/shard_map/ppermute | solution.py:32
  335.4 33.6 %collective-permute-start.46 = (bf16[2,224,1152]{2,1,0:T(8,128)(2,1)S(1)}, bf16[2,224,1152]{2,1,0:T(8,128)(2,1)S(1)}, u32[]{:S(2)}, u32[]{:S(2)}) collective-permute-start(bf16[2,224,1152]{2,1,0:T(8,128)(2,1)S(1)} %get-tuple-element.140.refs_5_), channel_id=1, source_target_pairs={{0,1},{1,5},{2,3},{3,7},{4,0},{5,4},{6,2},{7,6},{8,9},{9,13},{10,1... | collective-permute-start | bytes 3096584 | tf_op jit(solution)/shard_map/ppermute | solution.py:32
  392.7 36.8 %collective-permute-start.52 = (bf16[224,1152]{1,0:T(8,128)(2,1)S(1)}, bf16[224,1152]{1,0:T(8,128)(2,1)S(1)}, u32[]{:S(2)}, u32[]{:S(2)}) collective-permute-start(bf16[224,1152]{1,0:T(8,128)(2,1)S(1)} %get-tuple-element.160), channel_id=1, source_target_pairs={{0,24},{1,25},{2,26},{3,27},{4,28},{5,29},{6,30},{7,31},{8,0},{9,1... | collective-permute-start | bytes 1548296 | tf_op jit(solution)/shard_map/ppermute | solution.py:32
  393.2 36.3 %collective-permute-start.53 = (bf16[224,1152]{1,0:T(8,128)(2,1)S(1)}, bf16[224,1152]{1,0:T(8,128)(2,1)S(1)}, u32[]{:S(2)}, u32[]{:S(2)}) collective-permute-start(bf16[224,1152]{1,0:T(8,128)(2,1)S(1)} %get-tuple-element.161), channel_id=1, source_target_pairs={{0,16},{1,17},{2,18},{3,19},{4,20},{5,21},{6,22},{7,23},{8,24},{9,... | collective-permute-start | bytes 1548296 | tf_op jit(solution)/shard_map/ppermute | solution.py:32
  394.2 43.3 %collective-permute-start.54 = (bf16[224,1152]{1,0:T(8,128)(2,1)S(1)}, bf16[224,1152]{1,0:T(8,128)(2,1)S(1)}, u32[]{:S(2)}, u32[]{:S(2)}) collective-permute-start(bf16[224,1152]{1,0:T(8,128)(2,1)S(1)} %get-tuple-element.162), channel_id=1, source_target_pairs={{0,8},{1,9},{2,10},{3,11},{4,12},{5,13},{6,14},{7,15},{8,16},{9,17... | collective-permute-start | bytes 1548296 | tf_op jit(solution)/shard_map/ppermute | solution.py:32
  410.0 33.2 %collective-permute-start.50 = (bf16[4,576,256]{2,1,0:T(8,128)(2,1)S(1)}, bf16[4,576,256]{2,1,0:T(8,128)(2,1)S(1)}, u32[]{:S(2)}, u32[]{:S(2)}) collective-permute-start(bf16[4,576,256]{2,1,0:T(8,128)(2,1)S(1)} %get-tuple-element.157), channel_id=1, source_target_pairs={{0,4},{1,5},{2,6},{3,7},{4,0},{5,1},{6,2},{7,3},{8,12},{9,13},{10,... | collective-permute-start | bytes 3538952 | tf_op jit(solution)/shard_map/ppermute | solution.py:32
  410.4 32.7 %collective-permute-start.51 = (bf16[4,576,256]{2,1,0:T(8,128)(2,1)S(1)}, bf16[4,576,256]{2,1,0:T(8,128)(2,1)S(1)}, u32[]{:S(2)}, u32[]{:S(2)}) collective-permute-start(bf16[4,576,256]{2,1,0:T(8,128)(2,1)S(1)} %get-tuple-element.158), channel_id=1, source_target_pairs={{0,2},{1,3},{2,0},{3,1},{4,6},{5,7},{6,4},{7,5},{8,10},{9,11},{10,... | collective-permute-start | bytes 3538952 | tf_op jit(solution)/shard_map/ppermute | solution.py:32
  (82 other events, 1308.1 us)

commit v3 on v2

--- a/solution.py
+++ b/solution.py
@@ -8,6 +8,7 @@
 BF = jnp.bfloat16
 F32 = jnp.float32
 LANES = 128
+SPAN = 512
 MIB = 2**20
 
 NZ = 4
@@ -75,22 +76,24 @@
 
 
 EARLY = 10**11
-
-
-def relay(array, after, flops=EARLY):
+SOON = 10**10
+
+
+def relay(arrays, after, flops=0):
     anywhere = pl.BlockSpec(memory_space=pl.ANY)
+    count = len(arrays)
 
     def body(*refs):
         pass
 
     return pl.pallas_call(
         body,
-        out_shape=jax.ShapeDtypeStruct(array.shape, array.dtype),
-        in_specs=[anywhere] * (1 + len(after)),
-        out_specs=anywhere,
-        input_output_aliases={0: 0},
+        out_shape=[jax.ShapeDtypeStruct(array.shape, array.dtype) for array in arrays],
+        in_specs=[anywhere] * (count + len(after)),
+        out_specs=[anywhere] * count,
+        input_output_aliases={at: at for at in range(count)},
         cost_estimate=pl.CostEstimate(flops=flops, bytes_accessed=0, transcendentals=0),
-    )(array, *after)
+    )(*arrays, *after)
 
 
 def pack_weight(ids, weight, along=None, after=()):
@@ -135,34 +138,26 @@
     return [both[0]] + [over_z(both[dz], sign * dz) for dz in range(1, NZ)]
 
 
-def regroup(ids, pieces, groups, small=(), after=()):
-    count = len(pieces)
-    _, part, width = groups[0].shape
-    rows = width // 2
-    near_shape = (count,) + pieces[0].shape
-    small_shape = (2,) + small[0].shape[1:] if small else None
+def regroup(ids, pieces, groups, after=()):
+    count, wide = len(pieces), len(groups) > 0
+    outs = [((count,) + pieces[0].shape, BF)] if count else []
+    if wide:
+        _, part, width = groups[0].shape
+        rows = width // 2
+        outs += [((part, width), BF)] * NZ
 
     def body(ids, *rest):
-        ins, (r0, r1) = rest[:count], rest[count : count + 2]
-        tiny = rest[count + 2 : count + 2 + len(small)]
-        outs = rest[count + 2 + len(small) :]
+        ins, given = rest[:count], rest[count : count + len(groups)]
+        made = rest[count + len(groups) :]
         for at in range(count):
-            outs[0][at] = ins[at][...]
-        for dz in range(NZ):
+            made[0][at] = ins[at][...]
+        for dz in range(NZ if wide else 0):
             lanes = slice((dz % 2) * rows, (dz % 2 + 1) * rows)
-            parts = [group[dz // 2].astype(F32)[:, lanes] for group in (r0, r1)]
-            outs[1 + dz][...] = jnp.concatenate(parts, axis=1).astype(BF)
-        for at in range(NZ if small else 0):
-            for k in range(2):
-                outs[1 + NZ + at][k] = tiny[k][at]
-
-    made = call(
-        body,
-        [(near_shape, BF)] + [((part, width), BF)] * NZ + ([(small_shape, BF)] * NZ if small else []),
-        [ids, *pieces, *groups, *small],
-        after=after,
-    )
-    return made[0], made[1 : 1 + NZ], made[1 + NZ :]
+            parts = [group[dz // 2].astype(F32)[:, lanes] for group in given]
+            made[-NZ + dz][...] = jnp.concatenate(parts, axis=1).astype(BF)
+
+    made = list(call(body, outs, [ids, *pieces, *groups], after=after))
+    return (made[:1] if count else []) + [made[-NZ:]] * wide
 
 
 def regroup_back(ids, both, after=()):
@@ -219,25 +214,40 @@
     return [piece] + [over_z(piece, dz) for dz in range(1, NZ)]
 
 
-def gather_plane(near, axis):
-    from_x, from_y = over_x(near), over_y(near)
-    return [near, from_x, from_y, over_y(halves(from_x, axis + 1)[0]), over_x(halves(from_y, axis + 1)[1])]
+def stacked(arrays, rank):
+    found = []
+    for at, array in enumerate(arrays):
+        found += [(at, None)] if len(array.shape) == rank else [(at, k) for k in range(array.shape[0])]
+    return found
+
+
+def corner(ids, from_x, from_y, axis, after=()):
+    lists = [stacked(part, 2) for part in (from_x, from_y)]
+    piece = from_x[0].shape[-2:]
+    half = tuple(extent // 2 if at == axis else extent for at, extent in enumerate(piece))
+
+    def body(ids, *rest):
+        ins = rest[: len(from_x)], rest[len(from_x) : -2]
+        for k in range(2):
+            cut = (slice(None),) * axis + (pl.ds(k * half[axis], half[axis]),)
+            for dz, (at, index) in enumerate(lists[k]):
+                ref = ins[k][at] if index is None else ins[k][at].at[index]
+                rest[-2 + k][dz] = ref[cut]
+
+    return call(body, [((NZ,) + half, BF)] * 2, [ids, *from_x, *from_y], after=after)
 
 
 def add_diagonal(ids, parts, axis, after=()):
-    _, to_x, to_y, diag_a, diag_b = parts
-    half = diag_a.shape[axis + 1]
-    first = (slice(None),) * (axis + 1) + (pl.ds(0, half),)
-    second = (slice(None),) * (axis + 1) + (pl.ds(half, half),)
+    _, to_x, to_y, at_x, at_y = parts
+    half = at_x.shape[axis + 1]
 
     def body(ids, to_x, to_y, at_x, at_y, out_x, out_y):
-        out_x[first] = (to_x[first] + at_x[...].astype(F32)).astype(BF)
-        out_x[second] = to_x[second].astype(BF)
-        out_y[first] = to_y[first].astype(BF)
-        out_y[second] = (to_y[second] + at_y[...].astype(F32)).astype(BF)
-
-    args = [ids, to_x, to_y, over_y(diag_a), over_x(diag_b)]
-    return call(body, [(to_x.shape, BF)] * 2, args, after=after)
+        cuts = [(slice(None),) * (axis + 1) + (pl.ds(k * half, half),) for k in range(2)]
+        for k, (to, came, out) in enumerate(((to_x, at_x, out_x), (to_y, at_y, out_y))):
+            out[cuts[k]] = (to[cuts[k]] + came[...].astype(F32)).astype(BF)
+            out[cuts[1 - k]] = to[cuts[1 - k]].astype(BF)
+
+    return call(body, [(to_x.shape, BF)] * 2, [ids, to_x, to_y, at_x, at_y], after=after)
 
 
 def add_plane(ids, own, from_x, from_y, after=()):
@@ -250,28 +260,42 @@
     return call(body, outs, [ids, own, from_x, from_y], after=after)
 
 
-def sum_planes(planes):
-    total = planes[NZ - 1]
-    for step in range(NZ - 1):
-        total = total + over_z(planes[step], step + 1).astype(F32)
+def total_of(own, others):
+    total = own[...]
+    for other in others:
+        total = total + other[...].astype(F32)
     return total
 
 
-def partial_gates(ids, wide, found, channel_pieces, after=()):
+def add_all(ids, own, others):
+    def body(ids, own, *rest):
+        rest[-1][...] = total_of(own, rest[:-1])
+
+    return call(body, [(own.shape, F32)], [ids, own, *others])[0]
+
+
+def partial_gates(ids, wide, near, from_x, from_y, diagonal, channel_pieces, after=()):
     total, depth = wide.shape
     part = total // 4
     rows = depth // 2
     if channel_pieces:
-        own, length = found[0].shape[1:]
+        own, length = near[0].shape[-2:]
     else:
-        length = found[0].shape[2] * 8
-    span = 512
+        length = near[0].shape[-1] * 8
+    groups = [list(near), list(from_x), list(from_y), *[[part] for part in diagonal]]
+    found = [array for group in groups for array in group]
+    places = [stacked(group, 2) for group in groups]
+    first = [sum(len(group) for group in groups[:at]) for at in range(len(groups))]
 
     def body(ids, w, *rest):
-        ins, (u, mine, theirs), (prev, cur) = rest[:5], rest[5:8], rest[8:]
+        ins, (u, mine, theirs) = rest[:-3], rest[-3:]
         z, x, y, c = ids[0], ids[1], ids[2], ids[3]
         for dz in range(NZ):
-            near, at_x, at_y, diag_a, diag_b = [part.at[dz] for part in ins]
+            refs = []
+            for base, place in zip(first, places):
+                at, index = place[dz]
+                refs.append(ins[base + at] if index is None else ins[base + at].at[index])
+            near, at_x, at_y, diag_a, diag_b = refs
             source = mod(z - dz)
             if channel_pieces:
                 half = length // 2
@@ -297,86 +321,105 @@
                 u[pl.ds(low, rows), here] = at_y[...]
                 u[pl.ds(low, rows // 2), there] = diag_a[...]
                 u[pl.ds(pl.multiple_of(low + rows // 2, 16), rows // 2), there] = diag_b[...]
-        for start in range(0, length, span):
-            cols = pl.ds(start, span)
-            made = jnp.dot(w[...], u[:, cols], preferred_element_type=F32)
-            for core in range(2):
-                prev[core, :, cols] = made[2 * core * part : (2 * core + 1) * part]
-                cur[core, :, cols] = made[(2 * core + 1) * part : (2 * core + 2) * part]
-        first = lax.broadcasted_iota(jnp.int32, (part, length), 1) == 0
-        for out, core in ((mine, c), (theirs, 1 - c)):
-            out[...] = cur[core] + jnp.where(first, 0.0, pltpu.roll(prev[core], 1, 1))
+        lane = lax.broadcasted_iota(jnp.int32, (part, SPAN), 1)
+
+        def step(cols, k, carry):
+            lasts = []
+            for out, core, before in ((mine, c, carry[0]), (theirs, 1 - c, carry[1])):
+                rows = pl.ds(pl.multiple_of(core * 2 * part, 16), 2 * part)
+                made = jnp.dot(w[rows, :], u[:, cols], preferred_element_type=F32)
+                prev = made[:part]
+                out[:, cols] = made[part:] + jnp.where(lane == 0, before, pltpu.roll(prev, 1, 1))
+                lasts.append(prev[:, SPAN - 1 :])
+            return tuple(lasts)
+
+        zero = jnp.zeros((part, 1), F32)
+        spans(length, step, (zero, zero))
 
     return call(
         body,
         [((depth, length), BF), ((part, length), F32), ((part, length), F32)],
         [ids, wide, *found],
-        [pltpu.VMEM((2, part, length), F32), pltpu.VMEM((2, part, length), F32)],
         after=after,
         flops=2 * total * depth * length,
     )
 
 
-def scan_lanes(forget, driven, backward):
+def spans(length, step, carry, backward=False):
+    count = length // SPAN
+
+    def run(n, carry):
+        k = count - 1 - n if backward else n
+        return step(pl.ds(pl.multiple_of(k * SPAN, SPAN), SPAN), k, carry)
+
+    return lax.fori_loop(0, count, run, carry)
+
+
+def scan_span(forget, driven, carry, backward):
     own, length = driven.shape
     lane = lax.broadcasted_iota(jnp.int32, (own, LANES), 1)
-    count = length // LANES
-    order = list(range(count))[:: -1 if backward else 1]
-    blocks = [None] * count
-    carry = jnp.zeros((own, 1), F32)
-    together = 4
-    for start in range(0, count, together):
-        group = order[start : start + together]
-        reach = [forget[:, block * LANES : (block + 1) * LANES] for block in group]
-        state = [driven[:, block * LANES : (block + 1) * LANES] for block in group]
-        by = 1
-        while by < LANES:
-            shift = LANES - by if backward else by
-            inside = lane < LANES - by if backward else lane >= by
-            for at in range(len(group)):
-                r, s = reach[at], state[at]
-                state[at] = s + jnp.where(inside, r * pltpu.roll(s, shift, 1), 0.0)
-                reach[at] = jnp.where(inside, r * pltpu.roll(r, shift, 1), r)
-            by *= 2
-        for at, block in enumerate(group):
-            blocks[block] = state[at] + reach[at] * carry
-            carry = blocks[block][:, :1] if backward else blocks[block][:, LANES - 1 :]
-    return blocks
+    blocks = [slice(at, at + LANES) for at in range(0, length, LANES)]
+    reach, state = [forget[:, cols] for cols in blocks], [driven[:, cols] for cols in blocks]
+    by = 1
+    while by < LANES:
+        shift = LANES - by if backward else by
+        inside = lane < LANES - by if backward else lane >= by
+        for at in range(len(blocks)):
+            r, s = reach[at], state[at]
+            state[at] = s + jnp.where(inside, r * pltpu.roll(s, shift, 1), 0.0)
+            reach[at] = jnp.where(inside, r * pltpu.roll(r, shift, 1), r)
+        by *= 2
+    for at in range(len(blocks))[:: -1 if backward else 1]:
+        state[at] = state[at] + reach[at] * carry
+        carry = state[at][:, :1] if backward else state[at][:, LANES - 1 :]
+    return jnp.concatenate(state, axis=1), carry
 
 
 def squash(value):
     return 1.0 / (1.0 + jnp.exp(-value))
 
 
-def activate(mine, theirs, bias, own):
-    gates = [
-        mine[pl.ds(g * own, own), :] + theirs[pl.ds(g * own, own), :] + bias[pl.ds(g * own, own), :]
-        for g in range(3)
-    ]
-    return jnp.tanh(gates[0]), squash(gates[1]), squash(gates[2])
-
-
-def put_blocks(ref, blocks):
-    for at, block in enumerate(blocks):
-        ref[:, pl.ds(at * LANES, LANES)] = block
-
-
-def gate_gradients(grad, candidate, forget, outgate, cells, adjoint, wide, gate_grad):
-    own, length = grad.shape
-    driven = grad[...] * outgate[...]
-    last = lax.broadcasted_iota(jnp.int32, (own, length), 1) == length - 1
-    later = jnp.where(last, 0.0, pltpu.roll(forget[...], length - 1, 1))
-    put_blocks(adjoint, scan_lanes(later, driven, True))
-    f, a = forget[...], candidate[...]
-    away = 1.0 - f
-    before = jnp.where(
-        lax.broadcasted_iota(jnp.int32, (own, length), 1) == 0, 0.0, pltpu.roll(cells[...], 1, 1)
-    )
-    wide[pl.ds(0, own), :] = adjoint[...] * away * (1.0 - a * a)
-    wide[pl.ds(own, own), :] = adjoint[...] * (before - a) * f * away
-    o = outgate[...]
-    wide[pl.ds(2 * own, own), :] = grad[...] * cells[...] * o * (1.0 - o)
-    gate_grad[...] = wide[...].astype(BF)
+def forward_scan(mine, theirs, bias, cand, forg, outg, cells, result):
+    own, length = cells.shape
+
+    def step(cols, k, carry):
+        gates = []
+        for g in range(3):
+            rows = pl.ds(g * own, own)
+            gates.append(mine[rows, cols] + theirs[rows, cols] + bias[rows, :])
+        candidate, forget, outgate = jnp.tanh(gates[0]), squash(gates[1]), squash(gates[2])
+        state, carry = scan_span(forget, (1.0 - forget) * candidate, carry, False)
+        cand[:, cols], forg[:, cols], outg[:, cols], cells[:, cols] = candidate, forget, outgate, state
+        result(cols, outgate * state)
+        return carry
+
+    spans(length, step, jnp.zeros((own, 1), F32))
+
+
+def backward_scan(grad_of, cand, forg, outg, cells, gate_grad):
+    own, length = cells.shape
+    lane = lax.broadcasted_iota(jnp.int32, (own, SPAN), 1)
+
+    def step(cols, k, carry):
+        adjoint_after, forget_after = carry
+        grad, a, f, o, now = grad_of(cols), cand[:, cols], forg[:, cols], outg[:, cols], cells[:, cols]
+        later = jnp.where(lane == SPAN - 1, forget_after, pltpu.roll(f, SPAN - 1, 1))
+        adjoint, adjoint_first = scan_span(later, grad * o, adjoint_after, True)
+        last = cells[:, pl.ds(pl.multiple_of(jnp.maximum(k * SPAN - LANES, 0), LANES), LANES)][:, LANES - 1 :]
+        before = jnp.where(lane == 0, jnp.where(k == 0, 0.0, last), pltpu.roll(now, 1, 1))
+        away = 1.0 - f
+        gate_grad[:, cols] = jnp.concatenate(
+            [
+                adjoint * away * (1.0 - a * a),
+                adjoint * (before - a) * f * away,
+                grad * now * o * (1.0 - o),
+            ],
+            axis=0,
+        ).astype(BF)
+        return adjoint_first, f[:, :1]
+
+    zero = jnp.zeros((own, 1), F32)
+    spans(length, step, (zero, zero), True)
 
 
 def first_cells(ids, mine, theirs, bias, after=()):
@@ -384,10 +427,10 @@
     own = part // 3
 
     def body(ids, mine, theirs, bias, hidden, cand, forg, outg, cells):
-        candidate, forget, outgate = activate(mine, theirs, bias, own)
-        cand[...], forg[...], outg[...] = candidate, forget, outgate
-        put_blocks(cells, scan_lanes(forget, (1.0 - forget) * candidate, False))
-        hidden[...] = (outgate * cells[...]).astype(BF)
+        def result(cols, value):
+            hidden[:, cols] = value.astype(BF)
+
+        forward_scan(mine, theirs, bias, cand, forg, outg, cells, result)
 
     return call(
         body,
@@ -397,19 +440,21 @@
     )
 
 
-def first_gate_grad(ids, grad, saved, after=()):
-    own, length = grad.shape
-
-    def body(ids, grad, cand, forg, outg, cells, gate_grad, adjoint, wide):
-        gate_gradients(grad, cand, forg, outg, cells, adjoint, wide, gate_grad)
-
-    return call(
-        body,
-        [((3 * own, length), BF)],
-        [ids, grad, *saved],
-        [pltpu.VMEM((own, length), F32), pltpu.VMEM((3 * own, length), F32)],
-        after=after,
-    )[0]
+def first_gate_grad(ids, own, others, saved, after=()):
+    channels, length = own.shape
+
+    def body(ids, own, *rest):
+        ins, (cand, forg, outg, cells), gate_grad = rest[: len(others)], rest[-5:-1], rest[-1]
+
+        def grad_of(cols):
+            total = own[:, cols]
+            for other in ins:
+                total = total + other[:, cols].astype(F32)
+            return total
+
+        backward_scan(grad_of, cand, forg, outg, cells, gate_grad)
+
+    return call(body, [((3 * channels, length), BF)], [ids, own, *others, *saved], after=after)[0]
 
 
 def second_cells(ids, mine, theirs, bias, cot_pieces):
@@ -419,28 +464,28 @@
 
     def body(ids, mine, theirs, bias, *rest):
         cots, outs, gate_grad = rest[:NZ], rest[NZ : NZ + 2], rest[NZ + 2]
-        grad, cand, forg, outg, cells, adjoint, wide = rest[NZ + 3 :]
+        grad, cand, forg, outg, cells, made = rest[NZ + 3 :]
         z, x = ids[0], ids[1]
         for dz in range(NZ):
             for dx in range(2):
                 i = mod(z - dz) * 2 + flip(x, dx)
-                grad[:, pl.ds(pl.multiple_of(i * block, block), block)] = cots[dz][dx].astype(F32)
-        candidate, forget, outgate = activate(mine, theirs, bias, own)
-        cand[...], forg[...], outg[...] = candidate, forget, outgate
-        put_blocks(cells, scan_lanes(forget, (1.0 - forget) * candidate, False))
-        adjoint[...] = outgate * cells[...]
+                grad[:, pl.ds(pl.multiple_of(i * block, block), block)] = cots[dz][dx]
+
+        def result(cols, value):
+            made[:, cols] = value.astype(BF)
+
+        forward_scan(mine, theirs, bias, cand, forg, outg, cells, result)
         for dz in range(NZ):
             for dx in range(2):
                 i = mod(z + dz) * 2 + flip(x, dx)
-                piece = adjoint[:, pl.ds(pl.multiple_of(i * block, block), block)]
-                outs[dx][dz] = piece.astype(BF)
-        gate_gradients(grad, cand, forg, outg, cells, adjoint, wide, gate_grad)
+                outs[dx][dz] = made[:, pl.ds(pl.multiple_of(i * block, block), block)]
+        backward_scan(lambda cols: grad[:, cols].astype(F32), cand, forg, outg, cells, gate_grad)
 
     made = call(
         body,
         [((NZ, own, block), BF)] * 2 + [((part, length), BF)],
         [ids, mine, theirs, bias, *cot_pieces],
-        [pltpu.VMEM((own, length), F32)] * 6 + [pltpu.VMEM((part, length), F32)],
+        [pltpu.VMEM((own, length), BF)] + [pltpu.VMEM((own, length), F32)] * 4 + [pltpu.VMEM((own, length), BF)],
     )
     return made[:2], made[2]
 
@@ -485,22 +530,33 @@
     return call(body, [((8 * own, block), BF)], [ids, *pieces], [pltpu.VMEM((8 * own, block), F32)])[0]
 
 
-def input_parts(ids, tall, grads, channel_pieces, after=()):
+def input_parts(ids, tall, mine, theirs, channel_pieces, after=()):
     depth, total = tall.shape
-    length = grads.shape[1]
+    part, length = mine.shape
     rows = depth // 2
     own = rows // 8
     block = length // 8
-    span = 512
     shape = (NZ, own, length) if channel_pieces else (NZ, rows, block)
     half = (NZ, own, length // 2) if channel_pieces else (NZ, rows // 2, block)
 
-    def body(ids, w, grads, *rest):
+    def body(ids, w, mine, theirs, grads, *rest):
         outs, v = rest[:5], rest[5]
-        z, x, y = ids[0], ids[1], ids[2]
-        for start in range(0, length, span):
-            cols = pl.ds(start, span)
+        z, x, y, c = ids[0], ids[1], ids[2], ids[3]
+        lane = lax.broadcasted_iota(jnp.int32, (part, SPAN), 1)
+
+        def product(cols, k, carry):
+            firsts = []
+            for given, core, first in ((mine, c, carry[0]), (theirs, 1 - c, carry[1])):
+                now = given[:, cols].astype(F32)
+                later = jnp.where(lane == SPAN - 1, first, pltpu.roll(now, SPAN - 1, 1))
+                at = pl.ds(pl.multiple_of(core * 2 * part, 16), 2 * part)
+                grads[at, cols] = jnp.concatenate([later, now], axis=0).astype(BF)
+                firsts.append(now[:, :1])
             v[:, cols] = jnp.dot(w[...], grads[:, cols], preferred_element_type=F32)
+            return tuple(firsts)
+
+        zero = jnp.zeros((part, 1), F32)
+        spans(length, product, (zero, zero), True)
         for step in range(NZ):
             target = mod(z + 1 + step)
 
@@ -522,29 +578,25 @@
             outs[3][step] = piece(1, 1, 0).astype(BF)
             outs[4][step] = piece(1, 1, 1).astype(BF)
 
-    return call(
+    made = call(
         body,
-        [(shape, F32), (shape, F32), (shape, F32), (half, BF), (half, BF)],
-        [ids, tall, grads],
+        [((total, length), BF), (shape, F32), (shape, F32), (shape, F32), (half, BF), (half, BF)],
+        [ids, tall, mine, theirs],
         [pltpu.VMEM((depth, length), F32)],
         after=after,
         flops=2 * depth * total * length,
     )
-
-
-def weight_blocks(ids, mine, theirs, u, after=()):
-    part, length = mine.shape
+    return made[0], made[1:]
+
+
+def weight_blocks(ids, grads, u, after=()):
+    total, length = grads.shape
     depth = u.shape[0]
-    total, rows = 4 * part, depth // 2
-
-    def body(ids, mine, theirs, u, grads, *rest):
+    part, rows = total // 4, depth // 2
+
+    def body(ids, grads, u, *rest):
         outs, made = rest[:NZ], rest[NZ]
-        z, x, c = ids[0], ids[1], ids[3]
-        last = lax.broadcasted_iota(jnp.int32, (part, length), 1) == length - 1
-        for core in range(2):
-            now = jnp.where(c == core, mine[...].astype(F32), theirs[...].astype(F32))
-            after = jnp.where(last, 0.0, pltpu.roll(now, length - 1, 1))
-            grads[pl.ds(core * 2 * part, 2 * part), :] = jnp.concatenate([after, now], axis=0).astype(BF)
+        z, x = ids[0], ids[1]
         contract = (((1,), (1,)), ((), ()))
         for y in range(2):
             made[y] = lax.dot_general(
@@ -566,15 +618,14 @@
                 both.append(jnp.concatenate([made[lax.rem(source, 2), at, :], tails[r]], axis=0))
             outs[dz][...] = jnp.concatenate(both, axis=1).astype(BF)
 
-    made = call(
+    return call(
         body,
-        [((total, length), BF)] + [((part + 8, 2 * rows), BF)] * NZ,
-        [ids, mine, theirs, u],
+        [((part + 8, 2 * rows), BF)] * NZ,
+        [ids, grads, u],
         [pltpu.VMEM((2, total, rows), F32)],
         after=after,
         flops=2 * depth * total * length,
     )
-    return made[0], made[1:]
 
 
 def unpack_weight(ids, groups):
@@ -613,51 +664,60 @@
     return lax.dynamic_slice_in_dim(bias, i * own, own, axis=1).reshape(3 * own, 1)
 
 
+def back_rounds(ids, parts, blocks, axis, after=()):
+    blocks = blocks_over_z(blocks, -1)
+    parts = [*parts[:3], over_y(parts[3]), over_x(parts[4])]
+    sent_x, sent_y = add_diagonal(ids, parts, axis, after=after)
+    groups = regroup_back(ids, blocks)
+    *planes, own = add_plane(ids, parts[0], over_x(sent_x), over_y(sent_y), after=groups)
+    others = [over_z(plane, step + 1) for step, plane in enumerate(planes)]
+    return own, others, blocks_over_x(groups, True)
+
+
 def owned_channels(inputs, first_weight, first_bias, second_weight, second_bias, cotangent):
     tm, mp = lax.axis_index("tm"), lax.axis_index("mp")
     ids = jnp.stack([tm // 2, tm % 2, mp // 2, mp % 2]).astype(jnp.int32)
     own = first_weight.shape[2] // 8
 
     *w1, u_piece = pack_weight(ids, first_weight, inputs[0].T)
-    near, w1, _ = regroup(ids, along_z(u_piece), blocks_over_x(w1))
-    u_found = gather_plane(near, 0)
+    near, w1 = regroup(ids, along_z(u_piece), blocks_over_x(w1))
+    from_x, from_y = over_x(near), over_y(near)
     wide_1, tall_1 = join_weight(ids, blocks_over_z(w1, 1))
-    w2 = pack_weight(ids, second_weight, after=u_found[3:])
-
-    u, mine, theirs = partial_gates(ids, wide_1, u_found, False, after=w2)
-    w2 = blocks_over_x(w2)
-    hidden, *saved = first_cells(relay(ids, w2), mine, over_core(theirs), owned_bias(first_bias, own))
+    diag = corner(ids, [from_x], [from_y], 0)
+    diag = [over_y(diag[0]), over_x(diag[1])]
+    w2 = pack_weight(ids, second_weight)
     cot_here, cot_there = split_cotangent(ids, cotangent[0].T)
     cots = pair_up(ids, cot_here, over_x(cot_there))
-    near, w2, _ = regroup(ids, along_z(hidden), w2, after=cots)
-    h_found = gather_plane(near, 1)
+
+    u, mine, theirs = partial_gates(ids, wide_1, [near], [from_x], [from_y], diag, False, after=[*w2, *cots])
+    cots = [cots[0]] + [over_z(cots[dz], dz) for dz in range(1, NZ)]
+    w2 = blocks_over_x(relay(w2, diag))
+    (ids_2,) = relay([ids], [*w2, *cots[1:]], SOON)
+    hidden, *saved = first_cells(ids_2, mine, over_core(theirs), owned_bias(first_bias, own))
+
+    from_x, from_y = [over_x(hidden)], [over_y(hidden)]
+    far, w2 = regroup(ids, along_z(hidden)[1:], w2, after=[*from_x, *from_y])
+    from_x, from_y = [*from_x, over_x(far)], [*from_y, over_y(far)]
     wide_2, tall_2 = join_weight(ids, blocks_over_z(w2, 1))
-    cots = [cots[0]] + [over_z(cots[dz], dz) for dz in range(1, NZ)]
-    h, mine, theirs = partial_gates(ids, wide_2, h_found, True, after=cots)
+    diag = corner(ids, from_x, from_y, 1)
+    diag = [over_y(diag[0]), over_x(diag[1])]
+    h, mine, theirs = partial_gates(ids, wide_2, [hidden, far], from_x, from_y, diag, True)
     outs, gate_grad = second_cells(ids, mine, over_core(theirs), owned_bias(second_bias, own), cots)
 
-    grads, dw2 = weight_blocks(ids, gate_grad, over_core(gate_grad), h)
     outs = pair_up(ids, outs[0], over_x(outs[1]))
-    parts = input_parts(ids, tall_2, grads, True, after=outs)
-    dw2 = blocks_over_z(dw2, -1)
-    sent_x, sent_y = add_diagonal(ids, parts, 1)
-    dw2 = regroup_back(ids, dw2)
-    planes = add_plane(ids, parts[0], over_x(sent_x), over_y(sent_y), after=dw2)
-    hidden_grad = sum_planes(planes)
-    dw2 = blocks_over_x(dw2, True)
-    gate_grad = first_gate_grad(ids, hidden_grad, saved, after=dw2)
-
-    grads, dw1 = weight_blocks(ids, gate_grad, over_core(gate_grad), u)
+    grads, parts = input_parts(ids, tall_2, gate_grad, over_core(gate_grad), True)
+    dw2 = weight_blocks(ids, grads, h, after=outs)
+    plane, others, dw2 = back_rounds(ids, parts, dw2, 1)
+    gate_grad = first_gate_grad(ids, plane, others, saved, after=dw2)
+
+    grads, parts = input_parts(ids, tall_1, gate_grad, over_core(gate_grad), False)
     outs = [outs[0]] + [over_z(outs[dz], dz) for dz in range(1, NZ)]
-    parts = input_parts(ids, tall_1, grads, False, after=outs)
-    dw1 = blocks_over_z(dw1, -1)
+    dw1 = weight_blocks(ids, grads, u, after=outs)
     second_grad, second_bias_grad = unpack_weight(ids, dw2)
     outputs = join_outputs(ids, outs)
-    sent_x, sent_y = add_diagonal(ids, parts, 0, after=[second_grad, outputs])
-    dw1 = regroup_back(ids, dw1)
-    planes = add_plane(ids, parts[0], over_x(sent_x), over_y(sent_y), after=dw1)
-    input_grad = sum_planes(planes)
-    first_grad, first_bias_grad = unpack_weight(ids, blocks_over_x(dw1, True))
+    plane, others, dw1 = back_rounds(ids, parts, dw1, 0, [second_grad, outputs])
+    input_grad = add_all(ids, plane, others)
+    first_grad, first_bias_grad = unpack_weight(ids, dw1)
     first_grad, second_grad = (jnp.transpose(grad, (1, 0, 2)) for grad in (first_grad, second_grad))
     return (
         outputs.T[None],

time: 482 us -> 465 us (0.965)
  waiting for transfers between devices: 281 us -> 242 us
  starting transfers between devices: 71.5 us -> 86.9 us
  Pallas kernels: 91.7 us -> 104 us
    ppermute x60 -> x62, waiting for transfers between devices: 281 us -> 242 us  [moved(): return lax.ppermute(array, ('tm', 'mp'), pairs)]
    ppermute x60 -> x62, starting transfers between devices: 71.5 us -> 86.9 us  [moved(): return lax.ppermute(array, ('tm', 'mp'), pairs)]
    pallas_call x27 -> x30, Pallas kernels: 91.7 us -> 104 us  [call(): pl.pallas_call(run, out_shape=[jax.ShapeDtypeStruct(shape, kind) for shap...]
    unnamed x93 -> x83, local copies, waits for them, and re-layouts: 24.4 us -> 21.9 us
  transfers between devices with their start and end apart: 60 -> 62, of which waited for: 35 -> 27; matrix products, arithmetic and copies ran while one was open for 1% -> 1% of each run, Pallas kernels for 9% -> 11%
where the time goes in v3:
time: 465 us; the launch traced here: 461 us
  waiting for transfers between devices  242 us (52%)
  Pallas kernels  104 us (22%)
  starting transfers between devices  86.9 us (19%)
  local copies, waits for them, and re-layouts  27.1 us (6%)
    ppermute x62, waiting for transfers between devices, moved(): return lax.ppermute(array, ('tm', 'mp'), pairs)  242 us
    pallas_call x30, Pallas kernels, call(): pl.pallas_call(run, out_shape=[jax.ShapeDtypeStruct(shape, kind) for shap...  104 us
    ppermute x62, starting transfers between devices, moved(): return lax.ppermute(array, ('tm', 'mp'), pairs)  86.9 us
    unnamed x83, local copies, waits for them, and re-layouts  21.9 us
  transfers between devices with their start and end apart: 62, of which 27 were waited for; matrix products, arithmetic and copies ran while one was open for 1% of the time, Pallas kernels for 11%

profile of v3, /device:TPU:8, one launch (start us, length us, event | category | flops | bytes accessed | tf_op | source)
XLA Modules:
  0.0 461.4 jit_solution(12975639992675461143)
XLA Ops:
  13.2 16.8 %collective-permute-done.refs_2_ = bf16[576,256]{1,0:T(8,128)(2,1)S(1)} collective-permute-done((bf16[576,256]{1,0:T(8,128)(2,1)S(1)}, bf16[576,256]{1,0:T(8,128)(2,1)S(1)}, u32[]{:S(2)}, u32[]{:S(2)}) %collective-permute-start) | collective-permute-done | bytes 294944 | tf_op jit(solution)/shard_map/ppermute | solution.py:33
  30.0 5.7 %collective-permute-done.1.refs_3_ = bf16[576,256]{1,0:T(8,128)(2,1)S(1)} collective-permute-done((bf16[576,256]{1,0:T(8,128)(2,1)S(1)}, bf16[576,256]{1,0:T(8,128)(2,1)S(1)}, u32[]{:S(2)}, u32[]{:S(2)}) %collective-permute-start.1) | collective-permute-done | bytes 294944 | tf_op jit(solution)/shard_map/ppermute | solution.py:33
  44.4 25.2 %collective-permute-done.11.refs_2_ = bf16[4,72,256]{2,1,0:T(8,128)(2,1)S(1)} collective-permute-done((bf16[4,72,256]{2,1,0:T(8,128)(2,1)S(1)}, bf16[4,72,256]{2,1,0:T(8,128)(2,1)S(1)}, u32[]{:S(2)}, u32[]{:S(2)}) %collective-permute-start.11) | collective-permute-done | bytes 147488 | tf_op jit(solution)/shard_map/ppermute | solution.py:33
  75.0 10.1 %collective-permute-done.16.refs_3_ = bf16[216,1152]{1,0:T(8,128)(2,1)S(1)} collective-permute-done((bf16[216,1152]{1,0:T(8,128)(2,1)S(1)}, bf16[216,1152]{1,0:T(8,128)(2,1)S(1)}, u32[]{:S(2)}, u32[]{:S(2)}) %collective-permute-start.16) | collective-permute-done | bytes 497696 | tf_op jit(solution)/shard_map/ppermute | solution.py:33
  89.8 6.8 %shard_map.118 = (bf16[1152,2048]{1,0:T(8,128)(2,1)S(1)}, f32[216,2048]{1,0:T(8,128)S(1)}, f32[216,2048]{1,0:T(8,128)S(1)}) custom-call(s32[4]{0:T(128)S(1)} %pad_add_fusion.refs_0_, bf16[864,1152]{1,0:T(8,128)(2,1)S(1)} %get-tuple-element.114.refs_1_, bf16[4,576,256]{2,1,0:T(8,128)(2,1)S(1)} %get-tuple-element.100.refs_2_, ...), custom_call_target="tpu_custom_call" | custom-call | flops 4076863488 | bytes 14966800 | tf_op jit(solution)/shard_map/pallas_call | solution.py:67
  102.2 9.3 %collective-permute-start.9 = (bf16[2,216,1152]{2,1,0:T(8,128)(2,1)}, bf16[2,216,1152]{2,1,0:T(8,128)(2,1)}, u32[]{:S(2)}, u32[]{:S(2)}) collective-permute-start(bf16[2,216,1152]{2,1,0:T(8,128)(2,1)} %get-tuple-element.103), channel_id=1, source_target_pairs={{0,0},{1,4},{2,2},{3,6},{4,1},{5,5},{6,3},{7,7},{8,8},{9,12},{10,1... | collective-permute-start | bytes 2985992 | tf_op jit(solution)/shard_map/ppermute | solution.py:33
  142.0 16.2 %collective-permute-done.20.refs_2_ = bf16[72,2048]{1,0:T(8,128)(2,1)S(1)} collective-permute-done((bf16[72,2048]{1,0:T(8,128)(2,1)S(1)}, bf16[72,2048]{1,0:T(8,128)(2,1)S(1)}, u32[]{:S(2)}, u32[]{:S(2)}) %collective-permute-start.20) | collective-permute-done | bytes 294944 | tf_op jit(solution)/shard_map/ppermute | solution.py:33
  158.1 4.5 collective-permute-done.21.refs_3_
  167.5 18.8 %collective-permute-done.27.refs_2_.refs_5_ = bf16[3,72,2048]{2,1,0:T(8,128)(2,1)S(1)} collective-permute-done((bf16[3,72,2048]{2,1,0:T(8,128)(2,1)S(1)}, bf16[3,72,2048]{2,1,0:T(8,128)(2,1)S(1)}, u32[]{:S(2)}, u32[]{:S(2)}) %collective-permute-start.27) | collective-permute-done | bytes 884768 | tf_op jit(solution)/shard_map/ppermute | solution.py:33
  189.3 18.9 %collective-permute-done.25.refs_3_ = bf16[216,1152]{1,0:T(8,128)(2,1)S(1)} collective-permute-done((bf16[216,1152]{1,0:T(8,128)(2,1)S(1)}, bf16[216,1152]{1,0:T(8,128)(2,1)S(1)}, u32[]{:S(2)}, u32[]{:S(2)}) %collective-permute-start.25) | collective-permute-done | bytes 497696 | tf_op jit(solution)/shard_map/ppermute | solution.py:33
  211.5 8.5 %shard_map.123 = (bf16[1152,2048]{1,0:T(8,128)(2,1)S(1)}, f32[216,2048]{1,0:T(8,128)S(1)}, f32[216,2048]{1,0:T(8,128)}) custom-call(s32[4]{0:T(128)S(1)} %pad_add_fusion.refs_0_, bf16[864,1152]{1,0:T(8,128)(2,1)S(1)} %get-tuple-element.123.refs_1_, bf16[72,2048]{1,0:T(8,128)(2,1)S(1)} %get-tuple-element.118.refs_2_, ...), custom_call_target="tpu_custom_call" | custom-call | flops 4076863488 | bytes 14966800 | tf_op jit(solution)/shard_map/pallas_call | solution.py:67
  227.9 8.3 %shard_map.124 = (bf16[4,72,256]{2,1,0:T(8,128)(2,1)S(1)}, bf16[4,72,256]{2,1,0:T(8,128)(2,1)S(1)}, bf16[216,2048]{1,0:T(8,128)(2,1)S(1)}) custom-call(s32[4]{0:T(128)S(1)} %pad_add_fusion.refs_0_, f32[216,2048]{1,0:T(8,128)S(1)} %get-tuple-element.127.refs_1_, f32[216,2048]{1,0:T(8,128)S(1)} %collective-permute-done.31.refs_2_, f32[216,1]{1,0:T(8,128)S(1)} %copy-done.21, ...), custom_call_target="tpu_custom_call" | custom-call | bytes 5014384 | tf_op jit(solution)/shard_map/pallas_call | solution.py:67
  243.2 7.8 %shard_map.127 = (bf16[864,2048]{1,0:T(8,128)(2,1)S(1)}, f32[4,72,2048]{2,1,0:T(8,128)S(1)}, f32[4,72,2048]{2,1,0:T(8,128)S(1)}, f32[4,72,2048]{2,1,0:T(8,128)S(...) custom-call(s32[4]{0:T(128)S(1)} %pad_add_fusion.refs_0_, bf16[1152,864]{1,0:T(8,128)(2,1)S(1)} %copy-done.36, ...), custom_call_target="tpu_custom_call" | custom-call | flops 4076863488 | bytes 15556624 | tf_op jit(solution)/shard_map/pallas_call | solution.py:67
  254.3 7.4 %shard_map.129 = (bf16[224,1152]{1,0:T(8,128)(2,1)S(1)}, bf16[224,1152]{1,0:T(8,128)(2,1)S(1)}, bf16[224,1152]{1,0:T(8,128)(2,1)S(1)}, bf16[224,1152]{1,0:T(8,128)(2,1)S(1)}) custom-call(s32[4]{0:T(128)S(1)} %pad_add_fusion.refs_0_, bf16[864,2048]{1,0:T(8,128)(2,1)S(1)} %get-tuple-element.145.refs_1_, bf16[1152,2048]{1,0:T(8,128)(2,1)S(1)} %bitcast.31, ...), custom_call_target="tpu_custom_call" | custom-call | flops 4076863488 | bytes 10321936 | tf_op jit(solution)/shard_map/pallas_call | solution.py:67
  270.2 28.3 %collective-permute-done.41.refs_2_ = bf16[224,1152]{1,0:T(8,128)(2,1)S(1)} collective-permute-done((bf16[224,1152]{1,0:T(8,128)(2,1)S(1)}, bf16[224,1152]{1,0:T(8,128)(2,1)S(1)}, u32[]{:S(2)}, u32[]{:S(2)}) %collective-permute-start.41) | collective-permute-done | bytes 516128 | tf_op jit(solution)/shard_map/ppermute | solution.py:33
  298.5 10.1 %collective-permute-done.43.refs_4_ = bf16[224,1152]{1,0:T(8,128)(2,1)S(1)} collective-permute-done((bf16[224,1152]{1,0:T(8,128)(2,1)S(1)}, bf16[224,1152]{1,0:T(8,128)(2,1)S(1)}, u32[]{:S(2)}, u32[]{:S(2)}) %collective-permute-start.43) | collective-permute-done | bytes 516128 | tf_op jit(solution)/shard_map/ppermute | solution.py:33
  316.9 18.9 %collective-permute-done.48.refs_10_.refs_2_ = bf16[2,224,1152]{2,1,0:T(8,128)(2,1)S(1)} collective-permute-done((bf16[2,224,1152]{2,1,0:T(8,128)(2,1)S(1)}, bf16[2,224,1152]{2,1,0:T(8,128)(2,1)S(1)}, u32[]{:S(2)}, u32[]{:S(2)}) %collective-permute-start.48) | collective-permute-done | bytes 1032224 | tf_op jit(solution)/shard_map/ppermute | solution.py:33
  335.8 5.0 %collective-permute-done.45.refs_3_ = bf16[72,2048]{1,0:T(8,128)(2,1)S(1)} collective-permute-done((bf16[72,2048]{1,0:T(8,128)(2,1)S(1)}, bf16[72,2048]{1,0:T(8,128)(2,1)S(1)}, u32[]{:S(2)}, u32[]{:S(2)}) %collective-permute-start.45) | collective-permute-done | bytes 294944 | tf_op jit(solution)/shard_map/ppermute | solution.py:33
  341.7 13.3 %shard_map.132.refs_2_ = bf16[216,2048]{1,0:T(8,128)(2,1)S(1)} custom-call(s32[4]{0:T(128)S(1)} %pad_add_fusion.refs_0_, f32[72,2048]{1,0:T(8,128)S(1)} %get-tuple-element.153.refs_1_, bf16[72,2048]{1,0:T(8,128)(2,1)S(1)} %collective-permute-done.44.refs_2_, bf16[72,2048]{1,0:T(8,128)(2,1)S(1)} %collective-permute-done.45.refs_3_, ...), custom_call_target="tpu_custom_call" | custom-call | bytes 4718608 | tf_op jit(solution)/shard_map/pallas_call | solution.py:67
  359.8 7.9 %shard_map.133 = (bf16[864,2048]{1,0:T(8,128)(2,1)S(1)}, f32[4,576,256]{2,1,0:T(8,128)S(1)}, f32[4,576,256]{2,1,0:T(8,128)S(1)}, f32[4,576,256]{2,1,0:T(8,128)S(...) custom-call(s32[4]{0:T(128)S(1)} %pad_add_fusion.refs_0_, bf16[1152,864]{1,0:T(8,128)(2,1)S(1)} %copy-done.34, ...), custom_call_target="tpu_custom_call" | custom-call | flops 4076863488 | bytes 15556624 | tf_op jit(solution)/shard_map/pallas_call | solution.py:67
  369.1 7.4 %shard_map.136 = (bf16[224,1152]{1,0:T(8,128)(2,1)S(1)}, bf16[224,1152]{1,0:T(8,128)(2,1)S(1)}, bf16[224,1152]{1,0:T(8,128)(2,1)S(1)}, bf16[224,1152]{1,0:T(8,128)(2,1)S(1)}) custom-call(s32[4]{0:T(128)S(1)} %pad_add_fusion.refs_0_, bf16[864,2048]{1,0:T(8,128)(2,1)S(1)} %get-tuple-element.169.refs_1_, bf16[1152,2048]{1,0:T(8,128)(2,1)S(1)} %bitcast.29, ...), custom_call_target="tpu_custom_call" | custom-call | flops 4076863488 | bytes 10321936 | tf_op jit(solution)/shard_map/pallas_call | solution.py:67
  391.5 21.8 %collective-permute-done.54.refs_2_ = bf16[224,1152]{1,0:T(8,128)(2,1)S(1)} collective-permute-done((bf16[224,1152]{1,0:T(8,128)(2,1)S(1)}, bf16[224,1152]{1,0:T(8,128)(2,1)S(1)}, u32[]{:S(2)}, u32[]{:S(2)}) %collective-permute-start.54) | collective-permute-done | bytes 516128 | tf_op jit(solution)/shard_map/ppermute | solution.py:33
  413.3 8.1 %collective-permute-done.56.refs_4_ = bf16[224,1152]{1,0:T(8,128)(2,1)S(1)} collective-permute-done((bf16[224,1152]{1,0:T(8,128)(2,1)S(1)}, bf16[224,1152]{1,0:T(8,128)(2,1)S(1)}, u32[]{:S(2)}, u32[]{:S(2)}) %collective-permute-start.56) | collective-permute-done | bytes 516128 | tf_op jit(solution)/shard_map/ppermute | solution.py:33
  434.7 15.7 %collective-permute-done.61.refs_2_ = bf16[2,224,1152]{2,1,0:T(8,128)(2,1)S(1)} collective-permute-done((bf16[2,224,1152]{2,1,0:T(8,128)(2,1)S(1)}, bf16[2,224,1152]{2,1,0:T(8,128)(2,1)S(1)}, u32[]{:S(2)}, u32[]{:S(2)}) %collective-permute-start.61) | collective-permute-done | bytes 1032224 | tf_op jit(solution)/shard_map/ppermute | solution.py:33
  (228 shorter events, 159.1 us)
Async XLA Ops:
  5.0 32.5 %collective-permute-start.3 = (bf16[2,216,1152]{2,1,0:T(8,128)(2,1)S(1)}, bf16[2,216,1152]{2,1,0:T(8,128)(2,1)S(1)}, u32[]{:S(2)}, u32[]{:S(2)}) collective-permute-start(bf16[2,216,1152]{2,1,0:T(8,128)(2,1)S(1)} %get-tuple-element.98), channel_id=1, source_target_pairs={{0,0},{1,4},{2,2},{3,6},{4,1},{5,5},{6,3},{7,7},{8,8},{9,12},{10,1... | collective-permute-start | bytes 2985992 | tf_op jit(solution)/shard_map/ppermute | solution.py:33
  5.9 31.6 %collective-permute-start.4 = (bf16[2,216,1152]{2,1,0:T(8,128)(2,1)S(1)}, bf16[2,216,1152]{2,1,0:T(8,128)(2,1)S(1)}, u32[]{:S(2)}, u32[]{:S(2)}) collective-permute-start(bf16[2,216,1152]{2,1,0:T(8,128)(2,1)S(1)} %get-tuple-element.99), channel_id=1, source_target_pairs={{0,4},{1,0},{2,6},{3,2},{4,5},{5,1},{6,7},{7,3},{8,12},{9,8},{10,1... | collective-permute-start | bytes 2985992 | tf_op jit(solution)/shard_map/ppermute | solution.py:33
  11.4 26.1 %collective-permute-start.2 = (bf16[576,256]{1,0:T(8,128)(2,1)S(1)}, bf16[576,256]{1,0:T(8,128)(2,1)S(1)}, u32[]{:S(2)}, u32[]{:S(2)}) collective-permute-start(bf16[576,256]{1,0:T(8,128)(2,1)S(1)} %get-tuple-element.97.refs_1_), channel_id=1, source_target_pairs={{0,24},{1,25},{2,26},{3,27},{4,28},{5,29},{6,30},{7,31},{8,0},{9,1... | collective-permute-start | bytes 884744 | tf_op jit(solution)/shard_map/ppermute | solution.py:33
  38.5 33.4 %collective-permute-start.5 = (bf16[4,576,256]{2,1,0:T(8,128)(2,1)S(1)}, bf16[4,576,256]{2,1,0:T(8,128)(2,1)S(1)}, u32[]{:S(2)}, u32[]{:S(2)}) collective-permute-start(bf16[4,576,256]{2,1,0:T(8,128)(2,1)S(1)} %get-tuple-element.100.refs_2_), channel_id=1, source_target_pairs={{0,4},{1,5},{2,6},{3,7},{4,0},{5,1},{6,2},{7,3},{8,12},{9,13},{10,... | collective-permute-start | bytes 3538952 | tf_op jit(solution)/shard_map/ppermute | solution.py:33
  39.3 32.6 %collective-permute-start.6 = (bf16[4,576,256]{2,1,0:T(8,128)(2,1)S(1)}, bf16[4,576,256]{2,1,0:T(8,128)(2,1)S(1)}, u32[]{:S(2)}, u32[]{:S(2)}) collective-permute-start(bf16[4,576,256]{2,1,0:T(8,128)(2,1)S(1)} %get-tuple-element.100.refs_2_), channel_id=1, source_target_pairs={{0,2},{1,3},{2,0},{3,1},{4,6},{5,7},{6,4},{7,5},{8,10},{9,11},{10,... | collective-permute-start | bytes 3538952 | tf_op jit(solution)/shard_map/ppermute | solution.py:33
  41.5 28.2 %collective-permute-start.11 = (bf16[4,72,256]{2,1,0:T(8,128)(2,1)S(1)}, bf16[4,72,256]{2,1,0:T(8,128)(2,1)S(1)}, u32[]{:S(2)}, u32[]{:S(2)}) collective-permute-start(bf16[4,72,256]{2,1,0:T(8,128)(2,1)S(1)} %get-tuple-element.106), channel_id=1, source_target_pairs={{0,4},{1,5},{2,6},{3,7},{4,0},{5,1},{6,2},{7,3},{8,12},{9,13},{10,... | collective-permute-start | bytes 442376 | tf_op jit(solution)/shard_map/ppermute | solution.py:33
  42.8 32.2 %collective-permute-start.15 = (bf16[216,1152]{1,0:T(8,128)(2,1)S(1)}, bf16[216,1152]{1,0:T(8,128)(2,1)S(1)}, u32[]{:S(2)}, u32[]{:S(2)}) collective-permute-start(bf16[216,1152]{1,0:T(8,128)(2,1)S(1)} %get-tuple-element.111), channel_id=1, source_target_pairs={{0,8},{1,9},{2,10},{3,11},{4,12},{5,13},{6,14},{7,15},{8,16},{9,17... | collective-permute-start | bytes 1493000 | tf_op jit(solution)/shard_map/ppermute | solution.py:33
  42.8 42.2 %collective-permute-start.16 = (bf16[216,1152]{1,0:T(8,128)(2,1)S(1)}, bf16[216,1152]{1,0:T(8,128)(2,1)S(1)}, u32[]{:S(2)}, u32[]{:S(2)}) collective-permute-start(bf16[216,1152]{1,0:T(8,128)(2,1)S(1)} %get-tuple-element.112), channel_id=1, source_target_pairs={{0,16},{1,17},{2,18},{3,19},{4,20},{5,21},{6,22},{7,23},{8,24},{9,... | collective-permute-start | bytes 1493000 | tf_op jit(solution)/shard_map/ppermute | solution.py:33
  136.3 26.4 %collective-permute-start.21 = (bf16[72,2048]{1,0:T(8,128)(2,1)S(1)}, bf16[72,2048]{1,0:T(8,128)(2,1)S(1)}, u32[]{:S(2)}, u32[]{:S(2)}) collective-permute-start(bf16[72,2048]{1,0:T(8,128)(2,1)S(1)} %get-tuple-element.118.refs_2_), channel_id=1, source_target_pairs={{0,24},{1,25},{2,26},{3,27},{4,28},{5,29},{6,30},{7,31},{8,0},{9,1... | collective-permute-start | bytes 884744 | tf_op jit(solution)/shard_map/ppermute | solution.py:33
  136.3 26.4 %collective-permute-start.22 = (bf16[72,2048]{1,0:T(8,128)(2,1)S(1)}, bf16[72,2048]{1,0:T(8,128)(2,1)S(1)}, u32[]{:S(2)}, u32[]{:S(2)}) collective-permute-start(bf16[72,2048]{1,0:T(8,128)(2,1)S(1)} %get-tuple-element.118.refs_2_), channel_id=1, source_target_pairs={{0,4},{1,5},{2,6},{3,7},{4,0},{5,1},{6,2},{7,3},{8,12},{9,13},{10,... | collective-permute-start | bytes 884744 | tf_op jit(solution)/shard_map/ppermute | solution.py:33
  165.2 42.9 %collective-permute-start.25 = (bf16[216,1152]{1,0:T(8,128)(2,1)S(1)}, bf16[216,1152]{1,0:T(8,128)(2,1)S(1)}, u32[]{:S(2)}, u32[]{:S(2)}) collective-permute-start(bf16[216,1152]{1,0:T(8,128)(2,1)S(1)} %get-tuple-element.121), channel_id=1, source_target_pairs={{0,16},{1,17},{2,18},{3,19},{4,20},{5,21},{6,22},{7,23},{8,24},{9,... | collective-permute-start | bytes 1493000 | tf_op jit(solution)/shard_map/ppermute | solution.py:33
  165.2 42.9 %collective-permute-start.26 = (bf16[216,1152]{1,0:T(8,128)(2,1)S(1)}, bf16[216,1152]{1,0:T(8,128)(2,1)S(1)}, u32[]{:S(2)}, u32[]{:S(2)}) collective-permute-start(bf16[216,1152]{1,0:T(8,128)(2,1)S(1)} %get-tuple-element.122), channel_id=1, source_target_pairs={{0,24},{1,25},{2,26},{3,27},{4,28},{5,29},{6,30},{7,31},{8,0},{9,1... | collective-permute-start | bytes 1493000 | tf_op jit(solution)/shard_map/ppermute | solution.py:33
  261.7 36.8 %collective-permute-start.41 = (bf16[224,1152]{1,0:T(8,128)(2,1)S(1)}, bf16[224,1152]{1,0:T(8,128)(2,1)S(1)}, u32[]{:S(2)}, u32[]{:S(2)}) collective-permute-start(bf16[224,1152]{1,0:T(8,128)(2,1)S(1)} %get-tuple-element.148), channel_id=1, source_target_pairs={{0,24},{1,25},{2,26},{3,27},{4,28},{5,29},{6,30},{7,31},{8,0},{9,1... | collective-permute-start | bytes 1548296 | tf_op jit(solution)/shard_map/ppermute | solution.py:33
  261.7 36.8 %collective-permute-start.42 = (bf16[224,1152]{1,0:T(8,128)(2,1)S(1)}, bf16[224,1152]{1,0:T(8,128)(2,1)S(1)}, u32[]{:S(2)}, u32[]{:S(2)}) collective-permute-start(bf16[224,1152]{1,0:T(8,128)(2,1)S(1)} %get-tuple-element.149), channel_id=1, source_target_pairs={{0,16},{1,17},{2,18},{3,19},{4,20},{5,21},{6,22},{7,23},{8,24},{9,... | collective-permute-start | bytes 1548296 | tf_op jit(solution)/shard_map/ppermute | solution.py:33
  265.2 43.4 %collective-permute-start.43 = (bf16[224,1152]{1,0:T(8,128)(2,1)S(1)}, bf16[224,1152]{1,0:T(8,128)(2,1)S(1)}, u32[]{:S(2)}, u32[]{:S(2)}) collective-permute-start(bf16[224,1152]{1,0:T(8,128)(2,1)S(1)} %get-tuple-element.150), channel_id=1, source_target_pairs={{0,8},{1,9},{2,10},{3,11},{4,12},{5,13},{6,14},{7,15},{8,16},{9,17... | collective-permute-start | bytes 1548296 | tf_op jit(solution)/shard_map/ppermute | solution.py:33
  268.9 43.0 %collective-permute-start.39 = (bf16[4,72,2048]{2,1,0:T(8,128)(2,1)S(1)}, bf16[4,72,2048]{2,1,0:T(8,128)(2,1)S(1)}, u32[]{:S(2)}, u32[]{:S(2)}) collective-permute-start(bf16[4,72,2048]{2,1,0:T(8,128)(2,1)S(1)} %get-tuple-element.143), channel_id=1, source_target_pairs={{0,4},{1,5},{2,6},{3,7},{4,0},{5,1},{6,2},{7,3},{8,12},{9,13},{10,... | collective-permute-start | bytes 3538952 | tf_op jit(solution)/shard_map/ppermute | solution.py:33
  269.7 42.2 %collective-permute-start.40 = (bf16[4,72,2048]{2,1,0:T(8,128)(2,1)S(1)}, bf16[4,72,2048]{2,1,0:T(8,128)(2,1)S(1)}, u32[]{:S(2)}, u32[]{:S(2)}) collective-permute-start(bf16[4,72,2048]{2,1,0:T(8,128)(2,1)S(1)} %get-tuple-element.144), channel_id=1, source_target_pairs={{0,2},{1,3},{2,0},{3,1},{4,6},{5,7},{6,4},{7,5},{8,10},{9,11},{10,... | collective-permute-start | bytes 3538952 | tf_op jit(solution)/shard_map/ppermute | solution.py:33
  315.7 25.9 %collective-permute-start.46 = (bf16[72,2048]{1,0:T(8,128)(2,1)S(1)}, bf16[72,2048]{1,0:T(8,128)(2,1)S(1)}, u32[]{:S(2)}, u32[]{:S(2)}) collective-permute-start(bf16[72,2048]{1,0:T(8,128)(2,1)S(1)} %get-tuple-element.156), channel_id=1, source_target_pairs={{0,24},{1,25},{2,26},{3,27},{4,28},{5,29},{6,30},{7,31},{8,0},{9,1... | collective-permute-start | bytes 884744 | tf_op jit(solution)/shard_map/ppermute | solution.py:33
  376.5 36.8 %collective-permute-start.54 = (bf16[224,1152]{1,0:T(8,128)(2,1)S(1)}, bf16[224,1152]{1,0:T(8,128)(2,1)S(1)}, u32[]{:S(2)}, u32[]{:S(2)}) collective-permute-start(bf16[224,1152]{1,0:T(8,128)(2,1)S(1)} %get-tuple-element.172), channel_id=1, source_target_pairs={{0,24},{1,25},{2,26},{3,27},{4,28},{5,29},{6,30},{7,31},{8,0},{9,1... | collective-permute-start | bytes 1548296 | tf_op jit(solution)/shard_map/ppermute | solution.py:33
  376.5 36.8 %collective-permute-start.55 = (bf16[224,1152]{1,0:T(8,128)(2,1)S(1)}, bf16[224,1152]{1,0:T(8,128)(2,1)S(1)}, u32[]{:S(2)}, u32[]{:S(2)}) collective-permute-start(bf16[224,1152]{1,0:T(8,128)(2,1)S(1)} %get-tuple-element.173), channel_id=1, source_target_pairs={{0,16},{1,17},{2,18},{3,19},{4,20},{5,21},{6,22},{7,23},{8,24},{9,... | collective-permute-start | bytes 1548296 | tf_op jit(solution)/shard_map/ppermute | solution.py:33
  378.1 43.4 %collective-permute-start.56 = (bf16[224,1152]{1,0:T(8,128)(2,1)S(1)}, bf16[224,1152]{1,0:T(8,128)(2,1)S(1)}, u32[]{:S(2)}, u32[]{:S(2)}) collective-permute-start(bf16[224,1152]{1,0:T(8,128)(2,1)S(1)} %get-tuple-element.174), channel_id=1, source_target_pairs={{0,8},{1,9},{2,10},{3,11},{4,12},{5,13},{6,14},{7,15},{8,16},{9,17... | collective-permute-start | bytes 1548296 | tf_op jit(solution)/shard_map/ppermute | solution.py:33
  388.6 38.0 %collective-permute-start.52 = (bf16[4,576,256]{2,1,0:T(8,128)(2,1)S(1)}, bf16[4,576,256]{2,1,0:T(8,128)(2,1)S(1)}, u32[]{:S(2)}, u32[]{:S(2)}) collective-permute-start(bf16[4,576,256]{2,1,0:T(8,128)(2,1)S(1)} %get-tuple-element.167), channel_id=1, source_target_pairs={{0,4},{1,5},{2,6},{3,7},{4,0},{5,1},{6,2},{7,3},{8,12},{9,13},{10,... | collective-permute-start | bytes 3538952 | tf_op jit(solution)/shard_map/ppermute | solution.py:33
  390.0 36.6 %collective-permute-start.53 = (bf16[4,576,256]{2,1,0:T(8,128)(2,1)S(1)}, bf16[4,576,256]{2,1,0:T(8,128)(2,1)S(1)}, u32[]{:S(2)}, u32[]{:S(2)}) collective-permute-start(bf16[4,576,256]{2,1,0:T(8,128)(2,1)S(1)} %get-tuple-element.168), channel_id=1, source_target_pairs={{0,2},{1,3},{2,0},{3,1},{4,6},{5,7},{6,4},{7,5},{8,10},{9,11},{10,... | collective-permute-start | bytes 3538952 | tf_op jit(solution)/shard_map/ppermute | solution.py:33
  429.1 26.4 %collective-permute-start.57 = (bf16[576,256]{1,0:T(8,128)(2,1)}, bf16[576,256]{1,0:T(8,128)(2,1)S(1)}, u32[]{:S(2)}, u32[]{:S(2)}) collective-permute-start(bf16[576,256]{1,0:T(8,128)(2,1)} %get-tuple-element.178), channel_id=1, source_target_pairs={{0,8},{1,9},{2,10},{3,11},{4,12},{5,13},{6,14},{7,15},{8,16},{9,17... | collective-permute-start | bytes 884744 | tf_op jit(solution)/shard_map/ppermute | solution.py:33
  (79 other events, 1254.3 us)

commit v4 on v3

--- a/solution.py
+++ b/solution.py
@@ -49,16 +49,18 @@
     return moved(array, lambda z, x, y, c: ((z + by) % NZ, x, y, c))
 
 
-def call(body, outs, args, scratch=(), vmem=28, flops=0, after=()):
+def call(body, outs, args, scratch=(), vmem=28, flops=0, after=(), far_in=(), far_out=()):
     whole = pl.BlockSpec(memory_space=pltpu.VMEM)
-    moved_bytes = sum(a.size * a.dtype.itemsize for a in args)
-    for shape, kind in outs:
-        size = jnp.dtype(kind).itemsize
+    anywhere = pl.BlockSpec(memory_space=pl.ANY)
+    moved_bytes = sum(a.size * a.dtype.itemsize for at, a in enumerate(args) if at not in far_in)
+    for at, (shape, kind) in enumerate(outs):
+        size = 0 if at in far_out else jnp.dtype(kind).itemsize
         for extent in shape:
             size *= extent
         moved_bytes += size
-    specs = [pl.BlockSpec(memory_space=pltpu.SMEM)] + [whole] * (len(args) - 1)
-    specs += [pl.BlockSpec(memory_space=pl.ANY)] * len(after)
+    specs = [pl.BlockSpec(memory_space=pltpu.SMEM)]
+    specs += [anywhere if at in far_in else whole for at in range(1, len(args))]
+    specs += [anywhere] * len(after)
     count = len(args)
 
     def run(*refs):
@@ -68,11 +70,21 @@
         run,
         out_shape=[jax.ShapeDtypeStruct(shape, kind) for shape, kind in outs],
         in_specs=specs,
-        out_specs=[whole] * len(outs),
+        out_specs=[anywhere if at in far_out else whole for at in range(len(outs))],
         scratch_shapes=list(scratch),
         compiler_params=pltpu.CompilerParams(vmem_limit_bytes=vmem * MIB),
         cost_estimate=pl.CostEstimate(flops=flops, bytes_accessed=moved_bytes, transcendentals=0),
     )(*args, *after)
+
+
+ROOMY = 42 * 10**6
+
+
+def roomy(shape, kind):
+    size = jnp.dtype(kind).itemsize
+    for extent in shape:
+        size *= extent
+    return ((-(-ROOMY // size),) + shape, kind)
 
 
 EARLY = 10**11
@@ -96,16 +108,21 @@
     )(*arrays, *after)
 
 
-def pack_weight(ids, weight, along=None, after=()):
+def pack_weight(ids, weight, bias, along=None, after=()):
     rows, gates, columns = weight.shape
     own = columns // 8
     extra = [] if along is None else [along]
 
-    def body(ids, w, *rest):
-        outs, turned = rest[len(extra) : len(extra) + 2], rest[-1]
+    def body(ids, w, bias, *rest):
+        outs, column = rest[len(extra) : len(extra) + 2], rest[len(extra) + 2]
+        turned, upright = rest[-2:]
         if extra:
-            rest[-2][...] = rest[0][...]
-        z, c = ids[0], ids[3]
+            rest[-3][...] = rest[0][...]
+        z, x, c = ids[0], ids[1], ids[3]
+        mine = pl.ds(pl.multiple_of((z * 2 + x) * own, 8), own)
+        for g in range(gates):
+            upright[...] = jnp.broadcast_to(bias[g : g + 1, :], (8, columns)).T
+            column[pl.ds(g * own, own), :] = upright[mine, :1]
         for g in range(gates):
             turned[g] = w[g].astype(F32).T
         for r in range(2):
@@ -118,9 +135,11 @@
 
     return call(
         body,
-        [((NZ // 2, gates * own, 2 * rows), BF)] * 2 + [(a.shape, a.dtype) for a in extra],
-        [ids, jnp.transpose(weight, (1, 0, 2)), *extra],
-        [pltpu.VMEM((gates, columns, rows), F32)],
+        [((NZ // 2, gates * own, 2 * rows), BF)] * 2
+        + [((gates * own, 1), F32)]
+        + [(a.shape, a.dtype) for a in extra],
+        [ids, jnp.transpose(weight, (1, 0, 2)), bias, *extra],
+        [pltpu.VMEM((gates, columns, rows), F32), pltpu.VMEM((columns, 8), F32)],
         after=after,
     )
 
@@ -288,7 +307,7 @@
     first = [sum(len(group) for group in groups[:at]) for at in range(len(groups))]
 
     def body(ids, w, *rest):
-        ins, (u, mine, theirs) = rest[:-3], rest[-3:]
+        ins, (kept, mine, theirs, u, done) = rest[:-5], rest[-5:]
         z, x, y, c = ids[0], ids[1], ids[2], ids[3]
         for dz in range(NZ):
             refs = []
@@ -321,6 +340,8 @@
                 u[pl.ds(low, rows), here] = at_y[...]
                 u[pl.ds(low, rows // 2), there] = diag_a[...]
                 u[pl.ds(pl.multiple_of(low + rows // 2, 16), rows // 2), there] = diag_b[...]
+        keep = pltpu.make_async_copy(u, kept.at[0], done)
+        keep.start()
         lane = lax.broadcasted_iota(jnp.int32, (part, SPAN), 1)
 
         def step(cols, k, carry):
@@ -335,13 +356,16 @@
 
         zero = jnp.zeros((part, 1), F32)
         spans(length, step, (zero, zero))
+        keep.wait()
 
     return call(
         body,
-        [((depth, length), BF), ((part, length), F32), ((part, length), F32)],
+        [roomy((depth, length), BF), ((part, length), F32), ((part, length), F32)],
         [ids, wide, *found],
+        [pltpu.VMEM((depth, length), BF), pltpu.SemaphoreType.DMA],
         after=after,
         flops=2 * total * depth * length,
+        far_out=(0,),
     )
 
 
@@ -426,17 +450,26 @@
     part, length = mine.shape
     own = part // 3
 
-    def body(ids, mine, theirs, bias, hidden, cand, forg, outg, cells):
+    def body(ids, mine, theirs, bias, hidden, kept, *rest):
+        made, done = rest[:4], rest[4]
+
         def result(cols, value):
             hidden[:, cols] = value.astype(BF)
 
-        forward_scan(mine, theirs, bias, cand, forg, outg, cells, result)
+        forward_scan(mine, theirs, bias, *made, result)
+        copies = [pltpu.make_async_copy(made[at], kept.at[at], done.at[at]) for at in range(4)]
+        for copy in copies:
+            copy.start()
+        for copy in copies:
+            copy.wait()
 
     return call(
         body,
-        [((own, length), BF)] + [((own, length), F32)] * 4,
+        [((own, length), BF), roomy((own, length), F32)],
         [ids, mine, theirs, bias],
+        [pltpu.VMEM((own, length), F32)] * 4 + [pltpu.SemaphoreType.DMA((4,))],
         after=after,
+        far_out=(1,),
     )
 
 
@@ -444,7 +477,7 @@
     channels, length = own.shape
 
     def body(ids, own, *rest):
-        ins, (cand, forg, outg, cells), gate_grad = rest[: len(others)], rest[-5:-1], rest[-1]
+        ins, held, gate_grad = rest[: len(others)], rest[-5:-1], rest[-1]
 
         def grad_of(cols):
             total = own[:, cols]
@@ -452,9 +485,10 @@
                 total = total + other[:, cols].astype(F32)
             return total
 
-        backward_scan(grad_of, cand, forg, outg, cells, gate_grad)
-
-    return call(body, [((3 * channels, length), BF)], [ids, own, *others, *saved], after=after)[0]
+        backward_scan(grad_of, *held, gate_grad)
+
+    args = [ids, own, *others, *[saved[at] for at in range(4)]]
+    return call(body, [((3 * channels, length), BF)], args, after=after)[0]
 
 
 def second_cells(ids, mine, theirs, bias, cot_pieces):
@@ -659,11 +693,6 @@
     return grad, bias
 
 
-def owned_bias(bias, own):
-    i = lax.axis_index("tm")
-    return lax.dynamic_slice_in_dim(bias, i * own, own, axis=1).reshape(3 * own, 1)
-
-
 def back_rounds(ids, parts, blocks, axis, after=()):
     blocks = blocks_over_z(blocks, -1)
     parts = [*parts[:3], over_y(parts[3]), over_x(parts[4])]
@@ -677,42 +706,41 @@
 def owned_channels(inputs, first_weight, first_bias, second_weight, second_bias, cotangent):
     tm, mp = lax.axis_index("tm"), lax.axis_index("mp")
     ids = jnp.stack([tm // 2, tm % 2, mp // 2, mp % 2]).astype(jnp.int32)
-    own = first_weight.shape[2] // 8
-
-    *w1, u_piece = pack_weight(ids, first_weight, inputs[0].T)
+
+    *w1, column_1, u_piece = pack_weight(ids, first_weight, first_bias, inputs[0].T)
     near, w1 = regroup(ids, along_z(u_piece), blocks_over_x(w1))
     from_x, from_y = over_x(near), over_y(near)
     wide_1, tall_1 = join_weight(ids, blocks_over_z(w1, 1))
+    cot_here, cot_there = split_cotangent(ids, cotangent[0].T)
     diag = corner(ids, [from_x], [from_y], 0)
+    (cot_there,) = relay([cot_there], [diag[0]])
     diag = [over_y(diag[0]), over_x(diag[1])]
-    w2 = pack_weight(ids, second_weight)
-    cot_here, cot_there = split_cotangent(ids, cotangent[0].T)
     cots = pair_up(ids, cot_here, over_x(cot_there))
-
+    *w2, column_2 = pack_weight(ids, second_weight, second_bias)
+
+    cots = [cots[0]] + [over_z(cots[dz], dz) for dz in range(1, NZ)]
     u, mine, theirs = partial_gates(ids, wide_1, [near], [from_x], [from_y], diag, False, after=[*w2, *cots])
-    cots = [cots[0]] + [over_z(cots[dz], dz) for dz in range(1, NZ)]
-    w2 = blocks_over_x(relay(w2, diag))
-    (ids_2,) = relay([ids], [*w2, *cots[1:]], SOON)
-    hidden, *saved = first_cells(ids_2, mine, over_core(theirs), owned_bias(first_bias, own))
-
-    from_x, from_y = [over_x(hidden)], [over_y(hidden)]
-    far, w2 = regroup(ids, along_z(hidden)[1:], w2, after=[*from_x, *from_y])
-    from_x, from_y = [*from_x, over_x(far)], [*from_y, over_y(far)]
+    theirs = over_core(theirs)
+    hidden, saved = first_cells(ids, mine, theirs, column_1)
+
+    w2 = blocks_over_x(relay(w2, [hidden]))
+    near, w2 = regroup(ids, along_z(hidden), w2)
+    from_x, from_y = [over_x(near)], [over_y(near)]
     wide_2, tall_2 = join_weight(ids, blocks_over_z(w2, 1))
     diag = corner(ids, from_x, from_y, 1)
     diag = [over_y(diag[0]), over_x(diag[1])]
-    h, mine, theirs = partial_gates(ids, wide_2, [hidden, far], from_x, from_y, diag, True)
-    outs, gate_grad = second_cells(ids, mine, over_core(theirs), owned_bias(second_bias, own), cots)
+    h, mine, theirs = partial_gates(ids, wide_2, [near], from_x, from_y, diag, True)
+    outs, gate_grad = second_cells(ids, mine, over_core(theirs), column_2, cots)
 
     outs = pair_up(ids, outs[0], over_x(outs[1]))
     grads, parts = input_parts(ids, tall_2, gate_grad, over_core(gate_grad), True)
-    dw2 = weight_blocks(ids, grads, h, after=outs)
+    dw2 = weight_blocks(ids, grads, h[0], after=outs)
     plane, others, dw2 = back_rounds(ids, parts, dw2, 1)
     gate_grad = first_gate_grad(ids, plane, others, saved, after=dw2)
 
     grads, parts = input_parts(ids, tall_1, gate_grad, over_core(gate_grad), False)
     outs = [outs[0]] + [over_z(outs[dz], dz) for dz in range(1, NZ)]
-    dw1 = weight_blocks(ids, grads, u, after=outs)
+    dw1 = weight_blocks(ids, grads, u[0], after=outs)
     second_grad, second_bias_grad = unpack_weight(ids, dw2)
     outputs = join_outputs(ids, outs)
     plane, others, dw1 = back_rounds(ids, parts, dw1, 0, [second_grad, outputs])

time: 465 us -> 446 us (0.959)
  waiting for transfers between devices: 242 us -> 234 us
  starting transfers between devices: 86.9 us -> 79.8 us
    ppermute x62 -> x60, waiting for transfers between devices: 242 us -> 234 us  [moved(): return lax.ppermute(array, ('tm', 'mp'), pairs)]
    squeeze x0 -> x3, local copies, waits for them, and re-layouts: none -> 7.41 us  [the longest x1 2.86 us: owned_channels(): dw1 = weight_blocks(ids, grads, u[0], after=outs)]
    unnamed x83 -> x62, local copies, waits for them, and re-layouts: 21.9 us -> 14.8 us
    ppermute x62 -> x60, starting transfers between devices: 86.9 us -> 79.8 us  [moved(): return lax.ppermute(array, ('tm', 'mp'), pairs)]
  transfers between devices with their start and end apart: 62 -> 60, of which waited for: 27 -> 30; matrix products, arithmetic and copies ran while one was open for 1% -> 2% of each run, Pallas kernels for 11% -> 11%
where the time goes in v4:
time: 446 us; the launch traced here: 443 us
  waiting for transfers between devices  234 us (52%)
  Pallas kernels  105 us (24%)
  starting transfers between devices  79.8 us (18%)
  local copies, waits for them, and re-layouts  23.7 us (5%)
    ppermute x60, waiting for transfers between devices, moved(): return lax.ppermute(array, ('tm', 'mp'), pairs)  234 us
    pallas_call x30, Pallas kernels, call(): pl.pallas_call(run, out_shape=[jax.ShapeDtypeStruct(shape, kind) for shap...  105 us
    ppermute x60, starting transfers between devices, moved(): return lax.ppermute(array, ('tm', 'mp'), pairs)  79.8 us
    unnamed x62, local copies, waits for them, and re-layouts  14.8 us
  transfers between devices with their start and end apart: 60, of which 30 were waited for; matrix products, arithmetic and copies ran while one was open for 2% of the time, Pallas kernels for 11%

profile of v4, /device:TPU:8, one launch (start us, length us, event | category | flops | bytes accessed | tf_op | source)
XLA Modules:
  0.0 443.4 jit_solution(9550713850284094408)
XLA Ops:
  20.5 12.5 %collective-permute-done.1.refs_3_ = bf16[576,256]{1,0:T(8,128)(2,1)S(1)} collective-permute-done((bf16[576,256]{1,0:T(8,128)(2,1)S(1)}, bf16[576,256]{1,0:T(8,128)(2,1)S(1)}, u32[]{:S(2)}, u32[]{:S(2)}) %collective-permute-start.1) | collective-permute-done | bytes 294944 | tf_op jit(solution)/shard_map/ppermute | solution.py:33
  33.0 5.5 %collective-permute-done.refs_2_ = bf16[576,256]{1,0:T(8,128)(2,1)S(1)} collective-permute-done((bf16[576,256]{1,0:T(8,128)(2,1)S(1)}, bf16[576,256]{1,0:T(8,128)(2,1)S(1)}, u32[]{:S(2)}, u32[]{:S(2)}) %collective-permute-start) | collective-permute-done | bytes 294944 | tf_op jit(solution)/shard_map/ppermute | solution.py:33
  49.7 18.7 %collective-permute-done.9.refs_2_.refs_4_ = bf16[4,576,256]{2,1,0:T(8,128)(2,1)S(1)} collective-permute-done((bf16[4,576,256]{2,1,0:T(8,128)(2,1)S(1)}, bf16[4,576,256]{2,1,0:T(8,128)(2,1)S(1)}, u32[]{:S(2)}, u32[]{:S(2)}) %collective-permute-start.9) | collective-permute-done | bytes 1179680 | tf_op jit(solution)/shard_map/ppermute | solution.py:33
  83.1 9.1 %collective-permute-done.6.refs_3_ = bf16[216,1152]{1,0:T(8,128)(2,1)} collective-permute-done((bf16[216,1152]{1,0:T(8,128)(2,1)}, bf16[216,1152]{1,0:T(8,128)(2,1)}, u32[]{:S(2)}, u32[]{:S(2)}) %collective-permute-start.6) | collective-permute-done | bytes 497696 | tf_op jit(solution)/shard_map/ppermute | solution.py:33
  100.0 6.8 %shard_map.117 = (bf16[9,1152,2048]{2,1,0:T(8,128)(2,1)}, f32[216,2048]{1,0:T(8,128)S(1)}, f32[216,2048]{1,0:T(8,128)S(1)}) custom-call(s32[4]{0:T(128)S(1)} %pad_add_fusion.refs_0_, bf16[864,1152]{1,0:T(8,128)(2,1)S(1)} %get-tuple-element.101.refs_1_, bf16[4,576,256]{2,1,0:T(8,128)(2,1)S(1)} %copy-done.24, bf16[4,576,256]{2,1,0:T(8,128)(2,1)S(1)} %copy-done.7, ...), custom_call_target="tpu_custom_call" | custom-call | flops 4076863488 | bytes 10248208 | tf_op jit(solution)/shard_map/pallas_call | solution.py:69
  110.6 5.0 %shard_map.118 = (bf16[72,2048]{1,0:T(8,128)(2,1)S(1)}, f32[72,72,2048]{2,1,0:T(8,128)}) custom-call(s32[4]{0:T(128)S(1)} %pad_add_fusion.refs_0_, f32[216,2048]{1,0:T(8,128)S(1)} %get-tuple-element.113.refs_1_, f32[216,2048]{1,0:T(8,128)S(1)} %collective-permute-done.16.refs_2_, f32[216,1]{1,0:T(8,128)S(1)} %copy-done.20), custom_call_target="tpu_custom_call" | custom-call | bytes 3834736 | tf_op jit(solution)/shard_map/pallas_call | solution.py:69
  124.9 17.9 %collective-permute-done.19.refs_4_ = bf16[72,2048]{1,0:T(8,128)(2,1)S(1)} collective-permute-done((bf16[72,2048]{1,0:T(8,128)(2,1)S(1)}, bf16[72,2048]{1,0:T(8,128)(2,1)S(1)}, u32[]{:S(2)}, u32[]{:S(2)}) %collective-permute-start.19) | collective-permute-done | bytes 294944 | tf_op jit(solution)/shard_map/ppermute | solution.py:33
  154.4 21.5 %collective-permute-done.26.refs_2_.refs_4_ = bf16[4,72,2048]{2,1,0:T(8,128)(2,1)S(1)} collective-permute-done((bf16[4,72,2048]{2,1,0:T(8,128)(2,1)S(1)}, bf16[4,72,2048]{2,1,0:T(8,128)(2,1)S(1)}, u32[]{:S(2)}, u32[]{:S(2)}) %collective-permute-start.26) | collective-permute-done | bytes 1179680 | tf_op jit(solution)/shard_map/ppermute | solution.py:33
  180.1 5.8 %collective-permute-done.22.refs_2_ = bf16[216,1152]{1,0:T(8,128)(2,1)S(1)} collective-permute-done((bf16[216,1152]{1,0:T(8,128)(2,1)S(1)}, bf16[216,1152]{1,0:T(8,128)(2,1)S(1)}, u32[]{:S(2)}, u32[]{:S(2)}) %collective-permute-start.22) | collective-permute-done | bytes 497696 | tf_op jit(solution)/shard_map/ppermute | solution.py:33
  185.9 9.1 %collective-permute-done.23.refs_3_ = bf16[216,1152]{1,0:T(8,128)(2,1)S(1)} collective-permute-done((bf16[216,1152]{1,0:T(8,128)(2,1)S(1)}, bf16[216,1152]{1,0:T(8,128)(2,1)S(1)}, u32[]{:S(2)}, u32[]{:S(2)}) %collective-permute-start.23) | collective-permute-done | bytes 497696 | tf_op jit(solution)/shard_map/ppermute | solution.py:33
  198.2 7.3 %shard_map.123 = (bf16[9,1152,2048]{2,1,0:T(8,128)(2,1)}, f32[216,2048]{1,0:T(8,128)S(1)}, f32[216,2048]{1,0:T(8,128)S(1)}) custom-call(s32[4]{0:T(128)S(1)} %pad_add_fusion.refs_0_, bf16[864,1152]{1,0:T(8,128)(2,1)S(1)} %get-tuple-element.123.refs_1_, bf16[4,72,2048]{2,1,0:T(8,128)(2,1)S(1)} %get-tuple-element.124.refs_2_, ...), custom_call_target="tpu_custom_call" | custom-call | flops 4076863488 | bytes 10248208 | tf_op jit(solution)/shard_map/pallas_call | solution.py:69
  209.3 7.8 %shard_map.124 = (bf16[4,72,256]{2,1,0:T(8,128)(2,1)S(1)}, bf16[4,72,256]{2,1,0:T(8,128)(2,1)S(1)}, bf16[216,2048]{1,0:T(8,128)(2,1)S(1)}) custom-call(s32[4]{0:T(128)S(1)} %pad_add_fusion.refs_0_, f32[216,2048]{1,0:T(8,128)S(1)} %get-tuple-element.127.refs_1_, f32[216,2048]{1,0:T(8,128)S(1)} %collective-permute-done.29.refs_2_, f32[216,1]{1,0:T(8,128)S(1)} %copy-done.18, ...), custom_call_target="tpu_custom_call" | custom-call | bytes 5014384 | tf_op jit(solution)/shard_map/pallas_call | solution.py:69
  223.6 7.8 %shard_map.127 = (bf16[864,2048]{1,0:T(8,128)(2,1)S(1)}, f32[4,72,2048]{2,1,0:T(8,128)S(1)}, f32[4,72,2048]{2,1,0:T(8,128)S(1)}, f32[4,72,2048]{2,1,0:T(8,128)S(...) custom-call(s32[4]{0:T(128)S(1)} %pad_add_fusion.refs_0_, ...), custom_call_target="tpu_custom_call" | custom-call | flops 4076863488 | bytes 15556624 | tf_op jit(solution)/shard_map/pallas_call | solution.py:69
  233.3 7.4 %shard_map.129 = (bf16[224,1152]{1,0:T(8,128)(2,1)S(1)}, bf16[224,1152]{1,0:T(8,128)(2,1)S(1)}, bf16[224,1152]{1,0:T(8,128)(2,1)S(1)}, bf16[224,1152]{1,0:T(8,128)(2,1)S(1)}) custom-call(s32[4]{0:T(128)S(1)} %pad_add_fusion.refs_0_, bf16[864,2048]{1,0:T(8,128)(2,1)S(1)} %get-tuple-element.146.refs_1_, bf16[1152,2048]{1,0:T(8,128)(2,1)S(1)} %slice_bitcast_fusion.1.refs_2_, ...), custom_call_target="tpu_custom_call" | custom-call | flops 4076863488 | bytes 10321936 | tf_op jit(solution)/shard_map/pallas_call | solution.py:69
  249.0 28.5 %collective-permute-done.39.refs_2_ = bf16[224,1152]{1,0:T(8,128)(2,1)S(1)} collective-permute-done((bf16[224,1152]{1,0:T(8,128)(2,1)S(1)}, bf16[224,1152]{1,0:T(8,128)(2,1)S(1)}, u32[]{:S(2)}, u32[]{:S(2)}) %collective-permute-start.39) | collective-permute-done | bytes 516128 | tf_op jit(solution)/shard_map/ppermute | solution.py:33
  277.6 8.6 %collective-permute-done.41.refs_4_ = bf16[224,1152]{1,0:T(8,128)(2,1)S(1)} collective-permute-done((bf16[224,1152]{1,0:T(8,128)(2,1)S(1)}, bf16[224,1152]{1,0:T(8,128)(2,1)S(1)}, u32[]{:S(2)}, u32[]{:S(2)}) %collective-permute-start.41) | collective-permute-done | bytes 516128 | tf_op jit(solution)/shard_map/ppermute | solution.py:33
  297.7 16.7 %collective-permute-done.46.refs_10_.refs_2_ = bf16[2,224,1152]{2,1,0:T(8,128)(2,1)S(1)} collective-permute-done((bf16[2,224,1152]{2,1,0:T(8,128)(2,1)S(1)}, bf16[2,224,1152]{2,1,0:T(8,128)(2,1)S(1)}, u32[]{:S(2)}, u32[]{:S(2)}) %collective-permute-start.46) | collective-permute-done | bytes 1032224 | tf_op jit(solution)/shard_map/ppermute | solution.py:33
  314.4 5.3 %collective-permute-done.43.refs_3_ = bf16[72,2048]{1,0:T(8,128)(2,1)S(1)} collective-permute-done((bf16[72,2048]{1,0:T(8,128)(2,1)S(1)}, bf16[72,2048]{1,0:T(8,128)(2,1)S(1)}, u32[]{:S(2)}, u32[]{:S(2)}) %collective-permute-start.43) | collective-permute-done | bytes 294944 | tf_op jit(solution)/shard_map/ppermute | solution.py:33
  320.9 13.6 %shard_map.132.refs_2_ = bf16[216,2048]{1,0:T(8,128)(2,1)S(1)} custom-call(s32[4]{0:T(128)S(1)} %pad_add_fusion.refs_0_, f32[72,2048]{1,0:T(8,128)S(1)} %get-tuple-element.154.refs_1_, bf16[72,2048]{1,0:T(8,128)(2,1)S(1)} %collective-permute-done.42.refs_2_, bf16[72,2048]{1,0:T(8,128)(2,1)S(1)} %collective-permute-done.43.refs_3_, ...), custom_call_target="tpu_custom_call" | custom-call | bytes 4718608 | tf_op jit(solution)/shard_map/pallas_call | solution.py:69
  341.7 7.9 %shard_map.133 = (bf16[864,2048]{1,0:T(8,128)(2,1)S(1)}, f32[4,576,256]{2,1,0:T(8,128)S(1)}, f32[4,576,256]{2,1,0:T(8,128)S(1)}, f32[4,576,256]{2,1,0:T(8,128)S(...) custom-call(s32[4]{0:T(128)S(1)} %pad_add_fusion.refs_0_, bf16[1152,864]{1,0:T(8,128)(2,1)S(1)} %copy-done.30, ...), custom_call_target="tpu_custom_call" | custom-call | flops 4076863488 | bytes 15556624 | tf_op jit(solution)/shard_map/pallas_call | solution.py:69
  350.6 7.4 %shard_map.136 = (bf16[224,1152]{1,0:T(8,128)(2,1)S(1)}, bf16[224,1152]{1,0:T(8,128)(2,1)S(1)}, bf16[224,1152]{1,0:T(8,128)(2,1)S(1)}, bf16[224,1152]{1,0:T(8,128)(2,1)S(1)}) custom-call(s32[4]{0:T(128)S(1)} %pad_add_fusion.refs_0_, bf16[864,2048]{1,0:T(8,128)(2,1)S(1)} %get-tuple-element.167.refs_1_, bf16[1152,2048]{1,0:T(8,128)(2,1)S(1)} %slice_bitcast_fusion.refs_2_, ...), custom_call_target="tpu_custom_call" | custom-call | flops 4076863488 | bytes 10321936 | tf_op jit(solution)/shard_map/pallas_call | solution.py:69
  373.8 21.0 %collective-permute-done.52.refs_2_ = bf16[224,1152]{1,0:T(8,128)(2,1)S(1)} collective-permute-done((bf16[224,1152]{1,0:T(8,128)(2,1)S(1)}, bf16[224,1152]{1,0:T(8,128)(2,1)S(1)}, u32[]{:S(2)}, u32[]{:S(2)}) %collective-permute-start.52) | collective-permute-done | bytes 516128 | tf_op jit(solution)/shard_map/ppermute | solution.py:33
  394.8 8.2 %collective-permute-done.54.refs_4_ = bf16[224,1152]{1,0:T(8,128)(2,1)S(1)} collective-permute-done((bf16[224,1152]{1,0:T(8,128)(2,1)S(1)}, bf16[224,1152]{1,0:T(8,128)(2,1)S(1)}, u32[]{:S(2)}, u32[]{:S(2)}) %collective-permute-start.54) | collective-permute-done | bytes 516128 | tf_op jit(solution)/shard_map/ppermute | solution.py:33
  416.6 15.7 %collective-permute-done.59.refs_2_ = bf16[2,224,1152]{2,1,0:T(8,128)(2,1)S(1)} collective-permute-done((bf16[2,224,1152]{2,1,0:T(8,128)(2,1)S(1)}, bf16[2,224,1152]{2,1,0:T(8,128)(2,1)S(1)}, u32[]{:S(2)}, u32[]{:S(2)}) %collective-permute-start.59) | collective-permute-done | bytes 1032224 | tf_op jit(solution)/shard_map/ppermute | solution.py:33
  (200 shorter events, 166.9 us)
Async XLA Ops:
  6.6 31.9 %collective-permute-start.3 = (bf16[2,216,1152]{2,1,0:T(8,128)(2,1)S(1)}, bf16[2,216,1152]{2,1,0:T(8,128)(2,1)S(1)}, u32[]{:S(2)}, u32[]{:S(2)}) collective-permute-start(bf16[2,216,1152]{2,1,0:T(8,128)(2,1)S(1)} %get-tuple-element.95), channel_id=1, source_target_pairs={{0,0},{1,4},{2,2},{3,6},{4,1},{5,5},{6,3},{7,7},{8,8},{9,12},{10,1... | collective-permute-start | bytes 2985992 | tf_op jit(solution)/shard_map/ppermute | solution.py:33
  7.4 31.1 %collective-permute-start.4 = (bf16[2,216,1152]{2,1,0:T(8,128)(2,1)S(1)}, bf16[2,216,1152]{2,1,0:T(8,128)(2,1)S(1)}, u32[]{:S(2)}, u32[]{:S(2)}) collective-permute-start(bf16[2,216,1152]{2,1,0:T(8,128)(2,1)S(1)} %get-tuple-element.96), channel_id=1, source_target_pairs={{0,4},{1,0},{2,6},{3,2},{4,5},{5,1},{6,7},{7,3},{8,12},{9,8},{10,1... | collective-permute-start | bytes 2985992 | tf_op jit(solution)/shard_map/ppermute | solution.py:33
  41.3 27.1 %collective-permute-start.9 = (bf16[4,576,256]{2,1,0:T(8,128)(2,1)S(1)}, bf16[4,576,256]{2,1,0:T(8,128)(2,1)S(1)}, u32[]{:S(2)}, u32[]{:S(2)}) collective-permute-start(bf16[4,576,256]{2,1,0:T(8,128)(2,1)S(1)} %get-tuple-element.102.refs_2_), channel_id=1, source_target_pairs={{0,2},{1,3},{2,0},{3,1},{4,6},{5,7},{6,4},{7,5},{8,10},{9,11},{10,... | collective-permute-start | bytes 3538952 | tf_op jit(solution)/shard_map/ppermute | solution.py:33
  42.8 27.1 %collective-permute-start.8 = (bf16[4,576,256]{2,1,0:T(8,128)(2,1)S(1)}, bf16[4,576,256]{2,1,0:T(8,128)(2,1)S(1)}, u32[]{:S(2)}, u32[]{:S(2)}) collective-permute-start(bf16[4,576,256]{2,1,0:T(8,128)(2,1)S(1)} %get-tuple-element.102.refs_2_), channel_id=1, source_target_pairs={{0,4},{1,5},{2,6},{3,7},{4,0},{5,1},{6,2},{7,3},{8,12},{9,13},{10,... | collective-permute-start | bytes 3538952 | tf_op jit(solution)/shard_map/ppermute | solution.py:33
  44.5 36.6 %collective-permute-start.5 = (bf16[216,1152]{1,0:T(8,128)(2,1)}, bf16[216,1152]{1,0:T(8,128)(2,1)}, u32[]{:S(2)}, u32[]{:S(2)}) collective-permute-start(bf16[216,1152]{1,0:T(8,128)(2,1)} %get-tuple-element.98), channel_id=1, source_target_pairs={{0,8},{1,9},{2,10},{3,11},{4,12},{5,13},{6,14},{7,15},{8,16},{9,17... | collective-permute-start | bytes 1493000 | tf_op jit(solution)/shard_map/ppermute | solution.py:33
  47.0 45.3 %collective-permute-start.6 = (bf16[216,1152]{1,0:T(8,128)(2,1)}, bf16[216,1152]{1,0:T(8,128)(2,1)}, u32[]{:S(2)}, u32[]{:S(2)}) collective-permute-start(bf16[216,1152]{1,0:T(8,128)(2,1)} %get-tuple-element.99), channel_id=1, source_target_pairs={{0,16},{1,17},{2,18},{3,19},{4,20},{5,21},{6,22},{7,23},{8,24},{9,... | collective-permute-start | bytes 1493000 | tf_op jit(solution)/shard_map/ppermute | solution.py:33
  47.4 48.2 %collective-permute-start.7 = (bf16[216,1152]{1,0:T(8,128)(2,1)}, bf16[216,1152]{1,0:T(8,128)(2,1)}, u32[]{:S(2)}, u32[]{:S(2)}) collective-permute-start(bf16[216,1152]{1,0:T(8,128)(2,1)} %get-tuple-element.100), channel_id=1, source_target_pairs={{0,24},{1,25},{2,26},{3,27},{4,28},{5,29},{6,30},{7,31},{8,0},{9,1... | collective-permute-start | bytes 1493000 | tf_op jit(solution)/shard_map/ppermute | solution.py:33
  116.3 30.7 %collective-permute-start.20 = (bf16[2,216,1152]{2,1,0:T(8,128)(2,1)}, bf16[2,216,1152]{2,1,0:T(8,128)(2,1)S(1)}, u32[]{:S(2)}, u32[]{:S(2)}) collective-permute-start(bf16[2,216,1152]{2,1,0:T(8,128)(2,1)} %get-tuple-element.117), channel_id=1, source_target_pairs={{0,0},{1,4},{2,2},{3,6},{4,1},{5,5},{6,3},{7,7},{8,8},{9,12},{10,1... | collective-permute-start | bytes 2985992 | tf_op jit(solution)/shard_map/ppermute | solution.py:33
  118.3 28.7 %collective-permute-start.21 = (bf16[2,216,1152]{2,1,0:T(8,128)(2,1)}, bf16[2,216,1152]{2,1,0:T(8,128)(2,1)S(1)}, u32[]{:S(2)}, u32[]{:S(2)}) collective-permute-start(bf16[2,216,1152]{2,1,0:T(8,128)(2,1)} %get-tuple-element.118), channel_id=1, source_target_pairs={{0,4},{1,0},{2,6},{3,2},{4,5},{5,1},{6,7},{7,3},{8,12},{9,8},{10,1... | collective-permute-start | bytes 2985992 | tf_op jit(solution)/shard_map/ppermute | solution.py:33
  148.0 28.0 %collective-permute-start.26 = (bf16[4,72,2048]{2,1,0:T(8,128)(2,1)S(1)}, bf16[4,72,2048]{2,1,0:T(8,128)(2,1)S(1)}, u32[]{:S(2)}, u32[]{:S(2)}) collective-permute-start(bf16[4,72,2048]{2,1,0:T(8,128)(2,1)S(1)} %get-tuple-element.124.refs_2_), channel_id=1, source_target_pairs={{0,2},{1,3},{2,0},{3,1},{4,6},{5,7},{6,4},{7,5},{8,10},{9,11},{10,... | collective-permute-start | bytes 3538952 | tf_op jit(solution)/shard_map/ppermute | solution.py:33
  148.6 27.6 %collective-permute-start.25 = (bf16[4,72,2048]{2,1,0:T(8,128)(2,1)S(1)}, bf16[4,72,2048]{2,1,0:T(8,128)(2,1)S(1)}, u32[]{:S(2)}, u32[]{:S(2)}) collective-permute-start(bf16[4,72,2048]{2,1,0:T(8,128)(2,1)S(1)} %get-tuple-element.124.refs_2_), channel_id=1, source_target_pairs={{0,4},{1,5},{2,6},{3,7},{4,0},{5,1},{6,2},{7,3},{8,12},{9,13},{10,... | collective-permute-start | bytes 3538952 | tf_op jit(solution)/shard_map/ppermute | solution.py:33
  150.3 35.6 %collective-permute-start.22 = (bf16[216,1152]{1,0:T(8,128)(2,1)S(1)}, bf16[216,1152]{1,0:T(8,128)(2,1)S(1)}, u32[]{:S(2)}, u32[]{:S(2)}) collective-permute-start(bf16[216,1152]{1,0:T(8,128)(2,1)S(1)} %get-tuple-element.120), channel_id=1, source_target_pairs={{0,8},{1,9},{2,10},{3,11},{4,12},{5,13},{6,14},{7,15},{8,16},{9,17... | collective-permute-start | bytes 1493000 | tf_op jit(solution)/shard_map/ppermute | solution.py:33
  152.7 42.2 %collective-permute-start.23 = (bf16[216,1152]{1,0:T(8,128)(2,1)S(1)}, bf16[216,1152]{1,0:T(8,128)(2,1)S(1)}, u32[]{:S(2)}, u32[]{:S(2)}) collective-permute-start(bf16[216,1152]{1,0:T(8,128)(2,1)S(1)} %get-tuple-element.121), channel_id=1, source_target_pairs={{0,16},{1,17},{2,18},{3,19},{4,20},{5,21},{6,22},{7,23},{8,24},{9,... | collective-permute-start | bytes 1493000 | tf_op jit(solution)/shard_map/ppermute | solution.py:33
  154.1 42.1 %collective-permute-start.24 = (bf16[216,1152]{1,0:T(8,128)(2,1)S(1)}, bf16[216,1152]{1,0:T(8,128)(2,1)S(1)}, u32[]{:S(2)}, u32[]{:S(2)}) collective-permute-start(bf16[216,1152]{1,0:T(8,128)(2,1)S(1)} %get-tuple-element.122), channel_id=1, source_target_pairs={{0,24},{1,25},{2,26},{3,27},{4,28},{5,29},{6,30},{7,31},{8,0},{9,1... | collective-permute-start | bytes 1493000 | tf_op jit(solution)/shard_map/ppermute | solution.py:33
  240.7 36.8 %collective-permute-start.39 = (bf16[224,1152]{1,0:T(8,128)(2,1)S(1)}, bf16[224,1152]{1,0:T(8,128)(2,1)S(1)}, u32[]{:S(2)}, u32[]{:S(2)}) collective-permute-start(bf16[224,1152]{1,0:T(8,128)(2,1)S(1)} %get-tuple-element.149), channel_id=1, source_target_pairs={{0,24},{1,25},{2,26},{3,27},{4,28},{5,29},{6,30},{7,31},{8,0},{9,1... | collective-permute-start | bytes 1548296 | tf_op jit(solution)/shard_map/ppermute | solution.py:33
  240.8 36.8 %collective-permute-start.40 = (bf16[224,1152]{1,0:T(8,128)(2,1)S(1)}, bf16[224,1152]{1,0:T(8,128)(2,1)S(1)}, u32[]{:S(2)}, u32[]{:S(2)}) collective-permute-start(bf16[224,1152]{1,0:T(8,128)(2,1)S(1)} %get-tuple-element.150), channel_id=1, source_target_pairs={{0,16},{1,17},{2,18},{3,19},{4,20},{5,21},{6,22},{7,23},{8,24},{9,... | collective-permute-start | bytes 1548296 | tf_op jit(solution)/shard_map/ppermute | solution.py:33
  243.0 43.2 %collective-permute-start.41 = (bf16[224,1152]{1,0:T(8,128)(2,1)S(1)}, bf16[224,1152]{1,0:T(8,128)(2,1)S(1)}, u32[]{:S(2)}, u32[]{:S(2)}) collective-permute-start(bf16[224,1152]{1,0:T(8,128)(2,1)S(1)} %get-tuple-element.151), channel_id=1, source_target_pairs={{0,8},{1,9},{2,10},{3,11},{4,12},{5,13},{6,14},{7,15},{8,16},{9,17... | collective-permute-start | bytes 1548296 | tf_op jit(solution)/shard_map/ppermute | solution.py:33
  248.1 42.7 %collective-permute-start.37 = (bf16[4,72,2048]{2,1,0:T(8,128)(2,1)S(1)}, bf16[4,72,2048]{2,1,0:T(8,128)(2,1)S(1)}, u32[]{:S(2)}, u32[]{:S(2)}) collective-permute-start(bf16[4,72,2048]{2,1,0:T(8,128)(2,1)S(1)} %get-tuple-element.144), channel_id=1, source_target_pairs={{0,4},{1,5},{2,6},{3,7},{4,0},{5,1},{6,2},{7,3},{8,12},{9,13},{10,... | collective-permute-start | bytes 3538952 | tf_op jit(solution)/shard_map/ppermute | solution.py:33
  248.5 42.3 %collective-permute-start.38 = (bf16[4,72,2048]{2,1,0:T(8,128)(2,1)S(1)}, bf16[4,72,2048]{2,1,0:T(8,128)(2,1)S(1)}, u32[]{:S(2)}, u32[]{:S(2)}) collective-permute-start(bf16[4,72,2048]{2,1,0:T(8,128)(2,1)S(1)} %get-tuple-element.145), channel_id=1, source_target_pairs={{0,2},{1,3},{2,0},{3,1},{4,6},{5,7},{6,4},{7,5},{8,10},{9,11},{10,... | collective-permute-start | bytes 3538952 | tf_op jit(solution)/shard_map/ppermute | solution.py:33
  358.0 36.8 %collective-permute-start.52 = (bf16[224,1152]{1,0:T(8,128)(2,1)S(1)}, bf16[224,1152]{1,0:T(8,128)(2,1)S(1)}, u32[]{:S(2)}, u32[]{:S(2)}) collective-permute-start(bf16[224,1152]{1,0:T(8,128)(2,1)S(1)} %get-tuple-element.170), channel_id=1, source_target_pairs={{0,24},{1,25},{2,26},{3,27},{4,28},{5,29},{6,30},{7,31},{8,0},{9,1... | collective-permute-start | bytes 1548296 | tf_op jit(solution)/shard_map/ppermute | solution.py:33
  358.3 36.5 %collective-permute-start.53 = (bf16[224,1152]{1,0:T(8,128)(2,1)S(1)}, bf16[224,1152]{1,0:T(8,128)(2,1)S(1)}, u32[]{:S(2)}, u32[]{:S(2)}) collective-permute-start(bf16[224,1152]{1,0:T(8,128)(2,1)S(1)} %get-tuple-element.171), channel_id=1, source_target_pairs={{0,16},{1,17},{2,18},{3,19},{4,20},{5,21},{6,22},{7,23},{8,24},{9,... | collective-permute-start | bytes 1548296 | tf_op jit(solution)/shard_map/ppermute | solution.py:33
  359.6 43.5 %collective-permute-start.54 = (bf16[224,1152]{1,0:T(8,128)(2,1)S(1)}, bf16[224,1152]{1,0:T(8,128)(2,1)S(1)}, u32[]{:S(2)}, u32[]{:S(2)}) collective-permute-start(bf16[224,1152]{1,0:T(8,128)(2,1)S(1)} %get-tuple-element.172), channel_id=1, source_target_pairs={{0,8},{1,9},{2,10},{3,11},{4,12},{5,13},{6,14},{7,15},{8,16},{9,17... | collective-permute-start | bytes 1548296 | tf_op jit(solution)/shard_map/ppermute | solution.py:33
  370.6 38.0 %collective-permute-start.50 = (bf16[4,576,256]{2,1,0:T(8,128)(2,1)S(1)}, bf16[4,576,256]{2,1,0:T(8,128)(2,1)S(1)}, u32[]{:S(2)}, u32[]{:S(2)}) collective-permute-start(bf16[4,576,256]{2,1,0:T(8,128)(2,1)S(1)} %get-tuple-element.165), channel_id=1, source_target_pairs={{0,4},{1,5},{2,6},{3,7},{4,0},{5,1},{6,2},{7,3},{8,12},{9,13},{10,... | collective-permute-start | bytes 3538952 | tf_op jit(solution)/shard_map/ppermute | solution.py:33
  372.3 36.3 %collective-permute-start.51 = (bf16[4,576,256]{2,1,0:T(8,128)(2,1)S(1)}, bf16[4,576,256]{2,1,0:T(8,128)(2,1)S(1)}, u32[]{:S(2)}, u32[]{:S(2)}) collective-permute-start(bf16[4,576,256]{2,1,0:T(8,128)(2,1)S(1)} %get-tuple-element.166), channel_id=1, source_target_pairs={{0,2},{1,3},{2,0},{3,1},{4,6},{5,7},{6,4},{7,5},{8,10},{9,11},{10,... | collective-permute-start | bytes 3538952 | tf_op jit(solution)/shard_map/ppermute | solution.py:33
  (67 other events, 855.2 us)

commit v5 on v4

--- a/solution.py
+++ b/solution.py
@@ -123,8 +123,12 @@
         for g in range(gates):
             upright[...] = jnp.broadcast_to(bias[g : g + 1, :], (8, columns)).T
             column[pl.ds(g * own, own), :] = upright[mine, :1]
-        for g in range(gates):
+
+        def turn(g, carry):
             turned[g] = w[g].astype(F32).T
+            return carry
+
+        lax.fori_loop(0, gates, turn, 0)
         for r in range(2):
             for pair in range(NZ // 2):
                 both = []
@@ -298,23 +302,17 @@
     part = total // 4
     rows = depth // 2
     if channel_pieces:
-        own, length = near[0].shape[-2:]
+        own, length = near.shape[-2:]
     else:
-        length = near[0].shape[-1] * 8
-    groups = [list(near), list(from_x), list(from_y), *[[part] for part in diagonal]]
-    found = [array for group in groups for array in group]
-    places = [stacked(group, 2) for group in groups]
-    first = [sum(len(group) for group in groups[:at]) for at in range(len(groups))]
+        length = near.shape[-1] * 8
+    found = [near, from_x, from_y, *diagonal]
 
     def body(ids, w, *rest):
         ins, (kept, mine, theirs, u, done) = rest[:-5], rest[-5:]
         z, x, y, c = ids[0], ids[1], ids[2], ids[3]
-        for dz in range(NZ):
-            refs = []
-            for base, place in zip(first, places):
-                at, index = place[dz]
-                refs.append(ins[base + at] if index is None else ins[base + at].at[index])
-            near, at_x, at_y, diag_a, diag_b = refs
+
+        def lay(dz, carry):
+            near, at_x, at_y, diag_a, diag_b = [part.at[dz] for part in ins]
             source = mod(z - dz)
             if channel_pieces:
                 half = length // 2
@@ -340,6 +338,9 @@
                 u[pl.ds(low, rows), here] = at_y[...]
                 u[pl.ds(low, rows // 2), there] = diag_a[...]
                 u[pl.ds(pl.multiple_of(low + rows // 2, 16), rows // 2), there] = diag_b[...]
+            return carry
+
+        lax.fori_loop(0, NZ, lay, 0)
         keep = pltpu.make_async_copy(u, kept.at[0], done)
         keep.start()
         lane = lax.broadcasted_iota(jnp.int32, (part, SPAN), 1)
@@ -591,7 +592,8 @@
 
         zero = jnp.zeros((part, 1), F32)
         spans(length, product, (zero, zero), True)
-        for step in range(NZ):
+
+        def hand_out(step, carry):
             target = mod(z + 1 + step)
 
             def piece(dx, dy, k=None):
@@ -611,6 +613,9 @@
             outs[2][step] = piece(0, 1)
             outs[3][step] = piece(1, 1, 0).astype(BF)
             outs[4][step] = piece(1, 1, 1).astype(BF)
+            return carry
+
+        lax.fori_loop(0, NZ, hand_out, 0)
 
     made = call(
         body,
@@ -632,10 +637,13 @@
         outs, made = rest[:NZ], rest[NZ]
         z, x = ids[0], ids[1]
         contract = (((1,), (1,)), ((), ()))
-        for y in range(2):
-            made[y] = lax.dot_general(
-                grads[...], u[pl.ds(y * rows, rows), :], contract, preferred_element_type=F32
-            )
+
+        def product(y, carry):
+            at = pl.ds(pl.multiple_of(y * rows, 16), rows)
+            made[y] = lax.dot_general(grads[...], u[at, :], contract, preferred_element_type=F32)
+            return carry
+
+        lax.fori_loop(0, 2, product, 0)
         sums = lax.dot_general(jnp.ones((8, length), BF), grads[...], contract, preferred_element_type=F32)
         line = lax.broadcasted_iota(jnp.int32, (8, part), 0)
         tails = []
@@ -680,8 +688,12 @@
                         at = pl.ds(pl.multiple_of(i * own, 8), own)
                         joined[g, at, :] = block[g * own : (g + 1) * own]
                     bias[pl.ds(i, 1), :] = (block[part : part + 1] + block[part + 1 : part + 2])[:, :part]
-        for g in range(3):
+
+        def turn(g, carry):
             out[g] = joined[g].T
+            return carry
+
+        lax.fori_loop(0, 3, turn, 0)
 
     grad, bias = call(
         body,
@@ -707,8 +719,8 @@
     tm, mp = lax.axis_index("tm"), lax.axis_index("mp")
     ids = jnp.stack([tm // 2, tm % 2, mp // 2, mp % 2]).astype(jnp.int32)
 
-    *w1, column_1, u_piece = pack_weight(ids, first_weight, first_bias, inputs[0].T)
-    near, w1 = regroup(ids, along_z(u_piece), blocks_over_x(w1))
+    *w1, column_1 = pack_weight(ids, first_weight, first_bias)
+    near, w1 = regroup(ids, along_z(inputs[0].T), blocks_over_x(w1))
     from_x, from_y = over_x(near), over_y(near)
     wide_1, tall_1 = join_weight(ids, blocks_over_z(w1, 1))
     cot_here, cot_there = split_cotangent(ids, cotangent[0].T)
@@ -719,7 +731,7 @@
     *w2, column_2 = pack_weight(ids, second_weight, second_bias)
 
     cots = [cots[0]] + [over_z(cots[dz], dz) for dz in range(1, NZ)]
-    u, mine, theirs = partial_gates(ids, wide_1, [near], [from_x], [from_y], diag, False, after=[*w2, *cots])
+    u, mine, theirs = partial_gates(ids, wide_1, near, from_x, from_y, diag, False, after=[*w2, *cots])
     theirs = over_core(theirs)
     hidden, saved = first_cells(ids, mine, theirs, column_1)
 
@@ -729,18 +741,18 @@
     wide_2, tall_2 = join_weight(ids, blocks_over_z(w2, 1))
     diag = corner(ids, from_x, from_y, 1)
     diag = [over_y(diag[0]), over_x(diag[1])]
-    h, mine, theirs = partial_gates(ids, wide_2, [near], from_x, from_y, diag, True)
+    h, mine, theirs = partial_gates(ids, wide_2, near, *from_x, *from_y, diag, True)
     outs, gate_grad = second_cells(ids, mine, over_core(theirs), column_2, cots)
 
-    outs = pair_up(ids, outs[0], over_x(outs[1]))
     grads, parts = input_parts(ids, tall_2, gate_grad, over_core(gate_grad), True)
+    outs = pair_up(ids, outs[0], over_x(outs[1]), after=[grads])
     dw2 = weight_blocks(ids, grads, h[0], after=outs)
     plane, others, dw2 = back_rounds(ids, parts, dw2, 1)
     gate_grad = first_gate_grad(ids, plane, others, saved, after=dw2)
 
     grads, parts = input_parts(ids, tall_1, gate_grad, over_core(gate_grad), False)
     outs = [outs[0]] + [over_z(outs[dz], dz) for dz in range(1, NZ)]
-    dw1 = weight_blocks(ids, grads, u[0], after=outs)
+    dw1 = weight_blocks(ids, grads, u[0])
     second_grad, second_bias_grad = unpack_weight(ids, dw2)
     outputs = join_outputs(ids, outs)
     plane, others, dw1 = back_rounds(ids, parts, dw1, 0, [second_grad, outputs])

time: 446 us -> 432 us (0.969)
  Pallas kernels: 105 us -> 97 us
    pallas_call x30, Pallas kernels: 105 us -> 97 us  [call(): pl.pallas_call(run, out_shape=[jax.ShapeDtypeStruct(shape, kind) for shap...]
  transfers between devices with their start and end apart: 60 -> 60, of which waited for: 30 -> 27; matrix products, arithmetic and copies ran while one was open for 2% -> 2% of each run, Pallas kernels for 11% -> 14%
where the time goes in v5:
time: 432 us
  waiting for transfers between devices  230 us (53%)
  Pallas kernels  97 us (22%)
  starting transfers between devices  80.7 us (19%)
  local copies, waits for them, and re-layouts  22.8 us (5%)
    ppermute x60, waiting for transfers between devices, moved(): return lax.ppermute(array, ('tm', 'mp'), pairs)  230 us
    pallas_call x30, Pallas kernels, call(): pl.pallas_call(run, out_shape=[jax.ShapeDtypeStruct(shape, kind) for shap...  97 us
    ppermute x60, starting transfers between devices, moved(): return lax.ppermute(array, ('tm', 'mp'), pairs)  80.7 us
    unnamed x62, local copies, waits for them, and re-layouts  13.8 us
  transfers between devices with their start and end apart: 60, of which 27 were waited for; matrix products, arithmetic and copies ran while one was open for 2% of the time, Pallas kernels for 14%

profile of v5, /device:TPU:8, one launch (start us, length us, event | category | flops | bytes accessed | tf_op | source)
XLA Modules:
  0.0 432.0 jit_solution(16720347449870334982)
XLA Ops:
  14.9 4.8 %collective-permute-done.2.refs_4_ = bf16[576,256]{1,0:T(8,128)(2,1)S(1)} collective-permute-done((bf16[576,256]{1,0:T(8,128)(2,1)S(1)}, bf16[576,256]{1,0:T(8,128)(2,1)S(1)}, u32[]{:S(2)}, u32[]{:S(2)}) %collective-permute-start.2) | collective-permute-done | bytes 294944 | tf_op jit(solution)/shard_map/ppermute | solution.py:33
  19.7 12.5 %collective-permute-done.1.refs_3_ = bf16[576,256]{1,0:T(8,128)(2,1)S(1)} collective-permute-done((bf16[576,256]{1,0:T(8,128)(2,1)S(1)}, bf16[576,256]{1,0:T(8,128)(2,1)S(1)}, u32[]{:S(2)}, u32[]{:S(2)}) %collective-permute-start.1) | collective-permute-done | bytes 294944 | tf_op jit(solution)/shard_map/ppermute | solution.py:33
  32.3 5.5 %collective-permute-done.refs_2_ = bf16[576,256]{1,0:T(8,128)(2,1)S(1)} collective-permute-done((bf16[576,256]{1,0:T(8,128)(2,1)S(1)}, bf16[576,256]{1,0:T(8,128)(2,1)S(1)}, u32[]{:S(2)}, u32[]{:S(2)}) %collective-permute-start) | collective-permute-done | bytes 294944 | tf_op jit(solution)/shard_map/ppermute | solution.py:33
  49.0 18.7 %collective-permute-done.9.refs_2_.refs_4_ = bf16[4,576,256]{2,1,0:T(8,128)(2,1)S(1)} collective-permute-done((bf16[4,576,256]{2,1,0:T(8,128)(2,1)S(1)}, bf16[4,576,256]{2,1,0:T(8,128)(2,1)S(1)}, u32[]{:S(2)}, u32[]{:S(2)}) %collective-permute-start.9) | collective-permute-done | bytes 1179680 | tf_op jit(solution)/shard_map/ppermute | solution.py:33
  82.4 9.1 %collective-permute-done.6.refs_3_ = bf16[216,1152]{1,0:T(8,128)(2,1)} collective-permute-done((bf16[216,1152]{1,0:T(8,128)(2,1)}, bf16[216,1152]{1,0:T(8,128)(2,1)}, u32[]{:S(2)}, u32[]{:S(2)}) %collective-permute-start.6) | collective-permute-done | bytes 497696 | tf_op jit(solution)/shard_map/ppermute | solution.py:33
  99.3 6.8 %shard_map.117 = (bf16[9,1152,2048]{2,1,0:T(8,128)(2,1)}, f32[216,2048]{1,0:T(8,128)S(1)}, f32[216,2048]{1,0:T(8,128)S(1)}) custom-call(s32[4]{0:T(128)S(1)} %pad_add_fusion.refs_0_, bf16[864,1152]{1,0:T(8,128)(2,1)S(1)} %get-tuple-element.99.refs_1_, bf16[4,576,256]{2,1,0:T(8,128)(2,1)S(1)} %copy-done.24, bf16[4,576,256]{2,1,0:T(8,128)(2,1)S(1)} %copy-done.7, ...), custom_call_target="tpu_custom_call" | custom-call | flops 4076863488 | bytes 10248208 | tf_op jit(solution)/shard_map/pallas_call | solution.py:69
  109.8 5.0 %shard_map.118 = (bf16[72,2048]{1,0:T(8,128)(2,1)S(1)}, f32[72,72,2048]{2,1,0:T(8,128)}) custom-call(s32[4]{0:T(128)S(1)} %pad_add_fusion.refs_0_, f32[216,2048]{1,0:T(8,128)S(1)} %get-tuple-element.111.refs_1_, f32[216,2048]{1,0:T(8,128)S(1)} %collective-permute-done.16.refs_2_, f32[216,1]{1,0:T(8,128)S(1)} %copy-done.20), custom_call_target="tpu_custom_call" | custom-call | bytes 3834736 | tf_op jit(solution)/shard_map/pallas_call | solution.py:69
  124.1 17.9 %collective-permute-done.19.refs_4_ = bf16[72,2048]{1,0:T(8,128)(2,1)S(1)} collective-permute-done((bf16[72,2048]{1,0:T(8,128)(2,1)S(1)}, bf16[72,2048]{1,0:T(8,128)(2,1)S(1)}, u32[]{:S(2)}, u32[]{:S(2)}) %collective-permute-start.19) | collective-permute-done | bytes 294944 | tf_op jit(solution)/shard_map/ppermute | solution.py:33
  153.5 21.8 %collective-permute-done.26.refs_2_.refs_4_ = bf16[4,72,2048]{2,1,0:T(8,128)(2,1)S(1)} collective-permute-done((bf16[4,72,2048]{2,1,0:T(8,128)(2,1)S(1)}, bf16[4,72,2048]{2,1,0:T(8,128)(2,1)S(1)}, u32[]{:S(2)}, u32[]{:S(2)}) %collective-permute-start.26) | collective-permute-done | bytes 1179680 | tf_op jit(solution)/shard_map/ppermute | solution.py:33
  179.4 5.8 %collective-permute-done.22.refs_2_ = bf16[216,1152]{1,0:T(8,128)(2,1)S(1)} collective-permute-done((bf16[216,1152]{1,0:T(8,128)(2,1)S(1)}, bf16[216,1152]{1,0:T(8,128)(2,1)S(1)}, u32[]{:S(2)}, u32[]{:S(2)}) %collective-permute-start.22) | collective-permute-done | bytes 497696 | tf_op jit(solution)/shard_map/ppermute | solution.py:33
  185.2 9.1 %collective-permute-done.23.refs_3_ = bf16[216,1152]{1,0:T(8,128)(2,1)S(1)} collective-permute-done((bf16[216,1152]{1,0:T(8,128)(2,1)S(1)}, bf16[216,1152]{1,0:T(8,128)(2,1)S(1)}, u32[]{:S(2)}, u32[]{:S(2)}) %collective-permute-start.23) | collective-permute-done | bytes 497696 | tf_op jit(solution)/shard_map/ppermute | solution.py:33
  197.5 7.3 %shard_map.123 = (bf16[9,1152,2048]{2,1,0:T(8,128)(2,1)}, f32[216,2048]{1,0:T(8,128)S(1)}, f32[216,2048]{1,0:T(8,128)S(1)}) custom-call(s32[4]{0:T(128)S(1)} %pad_add_fusion.refs_0_, bf16[864,1152]{1,0:T(8,128)(2,1)S(1)} %get-tuple-element.121.refs_1_, bf16[4,72,2048]{2,1,0:T(8,128)(2,1)S(1)} %get-tuple-element.122.refs_2_, ...), custom_call_target="tpu_custom_call" | custom-call | flops 4076863488 | bytes 10248208 | tf_op jit(solution)/shard_map/pallas_call | solution.py:69
  208.6 7.8 %shard_map.124 = (bf16[4,72,256]{2,1,0:T(8,128)(2,1)S(1)}, bf16[4,72,256]{2,1,0:T(8,128)(2,1)S(1)}, bf16[216,2048]{1,0:T(8,128)(2,1)S(1)}) custom-call(s32[4]{0:T(128)S(1)} %pad_add_fusion.refs_0_, f32[216,2048]{1,0:T(8,128)S(1)} %get-tuple-element.125.refs_1_, f32[216,2048]{1,0:T(8,128)S(1)} %collective-permute-done.29.refs_2_, f32[216,1]{1,0:T(8,128)S(1)} %copy-done.18, ...), custom_call_target="tpu_custom_call" | custom-call | bytes 5014384 | tf_op jit(solution)/shard_map/pallas_call | solution.py:69
  219.7 7.8 %shard_map.125 = (bf16[864,2048]{1,0:T(8,128)(2,1)S(1)}, f32[4,72,2048]{2,1,0:T(8,128)S(1)}, f32[4,72,2048]{2,1,0:T(8,128)S(1)}, f32[4,72,2048]{2,1,0:T(8,128)S(...) custom-call(s32[4]{0:T(128)S(1)} %pad_add_fusion.refs_0_, ...), custom_call_target="tpu_custom_call" | custom-call | flops 4076863488 | bytes 15556624 | tf_op jit(solution)/shard_map/pallas_call | solution.py:69
  231.4 7.8 %shard_map.129 = (bf16[224,1152]{1,0:T(8,128)(2,1)S(1)}, bf16[224,1152]{1,0:T(8,128)(2,1)S(1)}, bf16[224,1152]{1,0:T(8,128)(2,1)S(1)}, bf16[224,1152]{1,0:T(8,128)(2,1)S(1)}) custom-call(s32[4]{0:T(128)S(1)} %pad_add_fusion.refs_0_, bf16[864,2048]{1,0:T(8,128)(2,1)S(1)} %get-tuple-element.132.refs_3_.refs_1_, ...), custom_call_target="tpu_custom_call" | custom-call | flops 4076863488 | bytes 10321936 | tf_op jit(solution)/shard_map/pallas_call | solution.py:69
  247.3 28.7 %collective-permute-done.39.refs_2_ = bf16[224,1152]{1,0:T(8,128)(2,1)S(1)} collective-permute-done((bf16[224,1152]{1,0:T(8,128)(2,1)S(1)}, bf16[224,1152]{1,0:T(8,128)(2,1)S(1)}, u32[]{:S(2)}, u32[]{:S(2)}) %collective-permute-start.39) | collective-permute-done | bytes 516128 | tf_op jit(solution)/shard_map/ppermute | solution.py:33
  276.0 9.4 %collective-permute-done.41.refs_4_ = bf16[224,1152]{1,0:T(8,128)(2,1)S(1)} collective-permute-done((bf16[224,1152]{1,0:T(8,128)(2,1)S(1)}, bf16[224,1152]{1,0:T(8,128)(2,1)S(1)}, u32[]{:S(2)}, u32[]{:S(2)}) %collective-permute-start.41) | collective-permute-done | bytes 516128 | tf_op jit(solution)/shard_map/ppermute | solution.py:33
  295.5 17.1 %collective-permute-done.46.refs_10_.refs_2_ = bf16[2,224,1152]{2,1,0:T(8,128)(2,1)S(1)} collective-permute-done((bf16[2,224,1152]{2,1,0:T(8,128)(2,1)S(1)}, bf16[2,224,1152]{2,1,0:T(8,128)(2,1)S(1)}, u32[]{:S(2)}, u32[]{:S(2)}) %collective-permute-start.46) | collective-permute-done | bytes 1032224 | tf_op jit(solution)/shard_map/ppermute | solution.py:33
  312.6 4.9 %collective-permute-done.43.refs_3_ = bf16[72,2048]{1,0:T(8,128)(2,1)S(1)} collective-permute-done((bf16[72,2048]{1,0:T(8,128)(2,1)S(1)}, bf16[72,2048]{1,0:T(8,128)(2,1)S(1)}, u32[]{:S(2)}, u32[]{:S(2)}) %collective-permute-start.43) | collective-permute-done | bytes 294944 | tf_op jit(solution)/shard_map/ppermute | solution.py:33
  330.1 7.9 %shard_map.133 = (bf16[864,2048]{1,0:T(8,128)(2,1)S(1)}, f32[4,576,256]{2,1,0:T(8,128)S(1)}, f32[4,576,256]{2,1,0:T(8,128)S(1)}, f32[4,576,256]{2,1,0:T(8,128)S(...) custom-call(s32[4]{0:T(128)S(1)} %pad_add_fusion.refs_0_, bf16[1152,864]{1,0:T(8,128)(2,1)S(1)} %copy-done.30, ...), custom_call_target="tpu_custom_call" | custom-call | flops 4076863488 | bytes 15556624 | tf_op jit(solution)/shard_map/pallas_call | solution.py:69
  339.5 7.7 %shard_map.136 = (bf16[224,1152]{1,0:T(8,128)(2,1)S(1)}, bf16[224,1152]{1,0:T(8,128)(2,1)S(1)}, bf16[224,1152]{1,0:T(8,128)(2,1)S(1)}, bf16[224,1152]{1,0:T(8,128)(2,1)S(1)}) custom-call(s32[4]{0:T(128)S(1)} %pad_add_fusion.refs_0_, bf16[864,2048]{1,0:T(8,128)(2,1)S(1)} %get-tuple-element.165.refs_1_, bf16[1152,2048]{1,0:T(8,128)(2,1)S(1)} %slice_bitcast_fusion.refs_2_), custom_call_target="tpu_custom_call" | custom-call | flops 4076863488 | bytes 10321936 | tf_op jit(solution)/shard_map/pallas_call | solution.py:69
  362.8 21.3 %collective-permute-done.52.refs_2_ = bf16[224,1152]{1,0:T(8,128)(2,1)S(1)} collective-permute-done((bf16[224,1152]{1,0:T(8,128)(2,1)S(1)}, bf16[224,1152]{1,0:T(8,128)(2,1)S(1)}, u32[]{:S(2)}, u32[]{:S(2)}) %collective-permute-start.52) | collective-permute-done | bytes 516128 | tf_op jit(solution)/shard_map/ppermute | solution.py:33
  384.1 8.2 %collective-permute-done.54.refs_4_ = bf16[224,1152]{1,0:T(8,128)(2,1)S(1)} collective-permute-done((bf16[224,1152]{1,0:T(8,128)(2,1)S(1)}, bf16[224,1152]{1,0:T(8,128)(2,1)S(1)}, u32[]{:S(2)}, u32[]{:S(2)}) %collective-permute-start.54) | collective-permute-done | bytes 516128 | tf_op jit(solution)/shard_map/ppermute | solution.py:33
  405.4 16.0 %collective-permute-done.59.refs_2_ = bf16[2,224,1152]{2,1,0:T(8,128)(2,1)S(1)} collective-permute-done((bf16[2,224,1152]{2,1,0:T(8,128)(2,1)S(1)}, bf16[2,224,1152]{2,1,0:T(8,128)(2,1)S(1)}, u32[]{:S(2)}, u32[]{:S(2)}) %collective-permute-start.59) | collective-permute-done | bytes 1032224 | tf_op jit(solution)/shard_map/ppermute | solution.py:33
  (200 shorter events, 162.0 us)
Async XLA Ops:
  5.8 31.9 %collective-permute-start.3 = (bf16[2,216,1152]{2,1,0:T(8,128)(2,1)S(1)}, bf16[2,216,1152]{2,1,0:T(8,128)(2,1)S(1)}, u32[]{:S(2)}, u32[]{:S(2)}) collective-permute-start(bf16[2,216,1152]{2,1,0:T(8,128)(2,1)S(1)} %get-tuple-element.93), channel_id=1, source_target_pairs={{0,0},{1,4},{2,2},{3,6},{4,1},{5,5},{6,3},{7,7},{8,8},{9,12},{10,1... | collective-permute-start | bytes 2985992 | tf_op jit(solution)/shard_map/ppermute | solution.py:33
  6.7 31.1 %collective-permute-start.4 = (bf16[2,216,1152]{2,1,0:T(8,128)(2,1)S(1)}, bf16[2,216,1152]{2,1,0:T(8,128)(2,1)S(1)}, u32[]{:S(2)}, u32[]{:S(2)}) collective-permute-start(bf16[2,216,1152]{2,1,0:T(8,128)(2,1)S(1)} %get-tuple-element.94), channel_id=1, source_target_pairs={{0,4},{1,0},{2,6},{3,2},{4,5},{5,1},{6,7},{7,3},{8,12},{9,8},{10,1... | collective-permute-start | bytes 2985992 | tf_op jit(solution)/shard_map/ppermute | solution.py:33
  40.5 27.1 %collective-permute-start.9 = (bf16[4,576,256]{2,1,0:T(8,128)(2,1)S(1)}, bf16[4,576,256]{2,1,0:T(8,128)(2,1)S(1)}, u32[]{:S(2)}, u32[]{:S(2)}) collective-permute-start(bf16[4,576,256]{2,1,0:T(8,128)(2,1)S(1)} %get-tuple-element.100.refs_2_), channel_id=1, source_target_pairs={{0,2},{1,3},{2,0},{3,1},{4,6},{5,7},{6,4},{7,5},{8,10},{9,11},{10,... | collective-permute-start | bytes 3538952 | tf_op jit(solution)/shard_map/ppermute | solution.py:33
  42.0 27.1 %collective-permute-start.8 = (bf16[4,576,256]{2,1,0:T(8,128)(2,1)S(1)}, bf16[4,576,256]{2,1,0:T(8,128)(2,1)S(1)}, u32[]{:S(2)}, u32[]{:S(2)}) collective-permute-start(bf16[4,576,256]{2,1,0:T(8,128)(2,1)S(1)} %get-tuple-element.100.refs_2_), channel_id=1, source_target_pairs={{0,4},{1,5},{2,6},{3,7},{4,0},{5,1},{6,2},{7,3},{8,12},{9,13},{10,... | collective-permute-start | bytes 3538952 | tf_op jit(solution)/shard_map/ppermute | solution.py:33
  43.8 36.5 %collective-permute-start.5 = (bf16[216,1152]{1,0:T(8,128)(2,1)}, bf16[216,1152]{1,0:T(8,128)(2,1)}, u32[]{:S(2)}, u32[]{:S(2)}) collective-permute-start(bf16[216,1152]{1,0:T(8,128)(2,1)} %get-tuple-element.96), channel_id=1, source_target_pairs={{0,8},{1,9},{2,10},{3,11},{4,12},{5,13},{6,14},{7,15},{8,16},{9,17... | collective-permute-start | bytes 1493000 | tf_op jit(solution)/shard_map/ppermute | solution.py:33
  46.2 45.2 %collective-permute-start.6 = (bf16[216,1152]{1,0:T(8,128)(2,1)}, bf16[216,1152]{1,0:T(8,128)(2,1)}, u32[]{:S(2)}, u32[]{:S(2)}) collective-permute-start(bf16[216,1152]{1,0:T(8,128)(2,1)} %get-tuple-element.97), channel_id=1, source_target_pairs={{0,16},{1,17},{2,18},{3,19},{4,20},{5,21},{6,22},{7,23},{8,24},{9,... | collective-permute-start | bytes 1493000 | tf_op jit(solution)/shard_map/ppermute | solution.py:33
  46.7 48.2 %collective-permute-start.7 = (bf16[216,1152]{1,0:T(8,128)(2,1)}, bf16[216,1152]{1,0:T(8,128)(2,1)}, u32[]{:S(2)}, u32[]{:S(2)}) collective-permute-start(bf16[216,1152]{1,0:T(8,128)(2,1)} %get-tuple-element.98), channel_id=1, source_target_pairs={{0,24},{1,25},{2,26},{3,27},{4,28},{5,29},{6,30},{7,31},{8,0},{9,1... | collective-permute-start | bytes 1493000 | tf_op jit(solution)/shard_map/ppermute | solution.py:33
  115.6 30.7 %collective-permute-start.20 = (bf16[2,216,1152]{2,1,0:T(8,128)(2,1)}, bf16[2,216,1152]{2,1,0:T(8,128)(2,1)S(1)}, u32[]{:S(2)}, u32[]{:S(2)}) collective-permute-start(bf16[2,216,1152]{2,1,0:T(8,128)(2,1)} %get-tuple-element.115), channel_id=1, source_target_pairs={{0,0},{1,4},{2,2},{3,6},{4,1},{5,5},{6,3},{7,7},{8,8},{9,12},{10,1... | collective-permute-start | bytes 2985992 | tf_op jit(solution)/shard_map/ppermute | solution.py:33
  117.6 28.7 %collective-permute-start.21 = (bf16[2,216,1152]{2,1,0:T(8,128)(2,1)}, bf16[2,216,1152]{2,1,0:T(8,128)(2,1)S(1)}, u32[]{:S(2)}, u32[]{:S(2)}) collective-permute-start(bf16[2,216,1152]{2,1,0:T(8,128)(2,1)} %get-tuple-element.116), channel_id=1, source_target_pairs={{0,4},{1,0},{2,6},{3,2},{4,5},{5,1},{6,7},{7,3},{8,12},{9,8},{10,1... | collective-permute-start | bytes 2985992 | tf_op jit(solution)/shard_map/ppermute | solution.py:33
  147.3 28.0 %collective-permute-start.26 = (bf16[4,72,2048]{2,1,0:T(8,128)(2,1)S(1)}, bf16[4,72,2048]{2,1,0:T(8,128)(2,1)S(1)}, u32[]{:S(2)}, u32[]{:S(2)}) collective-permute-start(bf16[4,72,2048]{2,1,0:T(8,128)(2,1)S(1)} %get-tuple-element.122.refs_2_), channel_id=1, source_target_pairs={{0,2},{1,3},{2,0},{3,1},{4,6},{5,7},{6,4},{7,5},{8,10},{9,11},{10,... | collective-permute-start | bytes 3538952 | tf_op jit(solution)/shard_map/ppermute | solution.py:33
  147.9 27.6 %collective-permute-start.25 = (bf16[4,72,2048]{2,1,0:T(8,128)(2,1)S(1)}, bf16[4,72,2048]{2,1,0:T(8,128)(2,1)S(1)}, u32[]{:S(2)}, u32[]{:S(2)}) collective-permute-start(bf16[4,72,2048]{2,1,0:T(8,128)(2,1)S(1)} %get-tuple-element.122.refs_2_), channel_id=1, source_target_pairs={{0,4},{1,5},{2,6},{3,7},{4,0},{5,1},{6,2},{7,3},{8,12},{9,13},{10,... | collective-permute-start | bytes 3538952 | tf_op jit(solution)/shard_map/ppermute | solution.py:33
  149.5 35.6 %collective-permute-start.22 = (bf16[216,1152]{1,0:T(8,128)(2,1)S(1)}, bf16[216,1152]{1,0:T(8,128)(2,1)S(1)}, u32[]{:S(2)}, u32[]{:S(2)}) collective-permute-start(bf16[216,1152]{1,0:T(8,128)(2,1)S(1)} %get-tuple-element.118), channel_id=1, source_target_pairs={{0,8},{1,9},{2,10},{3,11},{4,12},{5,13},{6,14},{7,15},{8,16},{9,17... | collective-permute-start | bytes 1493000 | tf_op jit(solution)/shard_map/ppermute | solution.py:33
  152.0 42.2 %collective-permute-start.23 = (bf16[216,1152]{1,0:T(8,128)(2,1)S(1)}, bf16[216,1152]{1,0:T(8,128)(2,1)S(1)}, u32[]{:S(2)}, u32[]{:S(2)}) collective-permute-start(bf16[216,1152]{1,0:T(8,128)(2,1)S(1)} %get-tuple-element.119), channel_id=1, source_target_pairs={{0,16},{1,17},{2,18},{3,19},{4,20},{5,21},{6,22},{7,23},{8,24},{9,... | collective-permute-start | bytes 1493000 | tf_op jit(solution)/shard_map/ppermute | solution.py:33
  153.3 42.2 %collective-permute-start.24 = (bf16[216,1152]{1,0:T(8,128)(2,1)S(1)}, bf16[216,1152]{1,0:T(8,128)(2,1)S(1)}, u32[]{:S(2)}, u32[]{:S(2)}) collective-permute-start(bf16[216,1152]{1,0:T(8,128)(2,1)S(1)} %get-tuple-element.120), channel_id=1, source_target_pairs={{0,24},{1,25},{2,26},{3,27},{4,28},{5,29},{6,30},{7,31},{8,0},{9,1... | collective-permute-start | bytes 1493000 | tf_op jit(solution)/shard_map/ppermute | solution.py:33
  239.2 36.8 %collective-permute-start.39 = (bf16[224,1152]{1,0:T(8,128)(2,1)S(1)}, bf16[224,1152]{1,0:T(8,128)(2,1)S(1)}, u32[]{:S(2)}, u32[]{:S(2)}) collective-permute-start(bf16[224,1152]{1,0:T(8,128)(2,1)S(1)} %get-tuple-element.147), channel_id=1, source_target_pairs={{0,24},{1,25},{2,26},{3,27},{4,28},{5,29},{6,30},{7,31},{8,0},{9,1... | collective-permute-start | bytes 1548296 | tf_op jit(solution)/shard_map/ppermute | solution.py:33
  239.2 36.8 %collective-permute-start.40 = (bf16[224,1152]{1,0:T(8,128)(2,1)S(1)}, bf16[224,1152]{1,0:T(8,128)(2,1)S(1)}, u32[]{:S(2)}, u32[]{:S(2)}) collective-permute-start(bf16[224,1152]{1,0:T(8,128)(2,1)S(1)} %get-tuple-element.148), channel_id=1, source_target_pairs={{0,16},{1,17},{2,18},{3,19},{4,20},{5,21},{6,22},{7,23},{8,24},{9,... | collective-permute-start | bytes 1548296 | tf_op jit(solution)/shard_map/ppermute | solution.py:33
  241.5 43.9 %collective-permute-start.41 = (bf16[224,1152]{1,0:T(8,128)(2,1)S(1)}, bf16[224,1152]{1,0:T(8,128)(2,1)S(1)}, u32[]{:S(2)}, u32[]{:S(2)}) collective-permute-start(bf16[224,1152]{1,0:T(8,128)(2,1)S(1)} %get-tuple-element.149), channel_id=1, source_target_pairs={{0,8},{1,9},{2,10},{3,11},{4,12},{5,13},{6,14},{7,15},{8,16},{9,17... | collective-permute-start | bytes 1548296 | tf_op jit(solution)/shard_map/ppermute | solution.py:33
  245.2 43.6 %collective-permute-start.37 = (bf16[4,72,2048]{2,1,0:T(8,128)(2,1)S(1)}, bf16[4,72,2048]{2,1,0:T(8,128)(2,1)S(1)}, u32[]{:S(2)}, u32[]{:S(2)}) collective-permute-start(bf16[4,72,2048]{2,1,0:T(8,128)(2,1)S(1)} %get-tuple-element.143), channel_id=1, source_target_pairs={{0,4},{1,5},{2,6},{3,7},{4,0},{5,1},{6,2},{7,3},{8,12},{9,13},{10,... | collective-permute-start | bytes 3538952 | tf_op jit(solution)/shard_map/ppermute | solution.py:33
  246.8 41.9 %collective-permute-start.38 = (bf16[4,72,2048]{2,1,0:T(8,128)(2,1)S(1)}, bf16[4,72,2048]{2,1,0:T(8,128)(2,1)S(1)}, u32[]{:S(2)}, u32[]{:S(2)}) collective-permute-start(bf16[4,72,2048]{2,1,0:T(8,128)(2,1)S(1)} %get-tuple-element.144), channel_id=1, source_target_pairs={{0,2},{1,3},{2,0},{3,1},{4,6},{5,7},{6,4},{7,5},{8,10},{9,11},{10,... | collective-permute-start | bytes 3538952 | tf_op jit(solution)/shard_map/ppermute | solution.py:33
  347.2 36.9 %collective-permute-start.52 = (bf16[224,1152]{1,0:T(8,128)(2,1)S(1)}, bf16[224,1152]{1,0:T(8,128)(2,1)S(1)}, u32[]{:S(2)}, u32[]{:S(2)}) collective-permute-start(bf16[224,1152]{1,0:T(8,128)(2,1)S(1)} %get-tuple-element.168), channel_id=1, source_target_pairs={{0,24},{1,25},{2,26},{3,27},{4,28},{5,29},{6,30},{7,31},{8,0},{9,1... | collective-permute-start | bytes 1548296 | tf_op jit(solution)/shard_map/ppermute | solution.py:33
  347.6 36.5 %collective-permute-start.53 = (bf16[224,1152]{1,0:T(8,128)(2,1)S(1)}, bf16[224,1152]{1,0:T(8,128)(2,1)S(1)}, u32[]{:S(2)}, u32[]{:S(2)}) collective-permute-start(bf16[224,1152]{1,0:T(8,128)(2,1)S(1)} %get-tuple-element.169), channel_id=1, source_target_pairs={{0,16},{1,17},{2,18},{3,19},{4,20},{5,21},{6,22},{7,23},{8,24},{9,... | collective-permute-start | bytes 1548296 | tf_op jit(solution)/shard_map/ppermute | solution.py:33
  348.8 43.5 %collective-permute-start.54 = (bf16[224,1152]{1,0:T(8,128)(2,1)S(1)}, bf16[224,1152]{1,0:T(8,128)(2,1)S(1)}, u32[]{:S(2)}, u32[]{:S(2)}) collective-permute-start(bf16[224,1152]{1,0:T(8,128)(2,1)S(1)} %get-tuple-element.170), channel_id=1, source_target_pairs={{0,8},{1,9},{2,10},{3,11},{4,12},{5,13},{6,14},{7,15},{8,16},{9,17... | collective-permute-start | bytes 1548296 | tf_op jit(solution)/shard_map/ppermute | solution.py:33
  360.0 37.4 %collective-permute-start.50 = (bf16[4,576,256]{2,1,0:T(8,128)(2,1)S(1)}, bf16[4,576,256]{2,1,0:T(8,128)(2,1)S(1)}, u32[]{:S(2)}, u32[]{:S(2)}) collective-permute-start(bf16[4,576,256]{2,1,0:T(8,128)(2,1)S(1)} %get-tuple-element.163), channel_id=1, source_target_pairs={{0,4},{1,5},{2,6},{3,7},{4,0},{5,1},{6,2},{7,3},{8,12},{9,13},{10,... | collective-permute-start | bytes 3538952 | tf_op jit(solution)/shard_map/ppermute | solution.py:33
  361.3 36.2 %collective-permute-start.51 = (bf16[4,576,256]{2,1,0:T(8,128)(2,1)S(1)}, bf16[4,576,256]{2,1,0:T(8,128)(2,1)S(1)}, u32[]{:S(2)}, u32[]{:S(2)}) collective-permute-start(bf16[4,576,256]{2,1,0:T(8,128)(2,1)S(1)} %get-tuple-element.164), channel_id=1, source_target_pairs={{0,2},{1,3},{2,0},{3,1},{4,6},{5,7},{6,4},{7,5},{8,10},{9,11},{10,... | collective-permute-start | bytes 3538952 | tf_op jit(solution)/shard_map/ppermute | solution.py:33
  (67 other events, 892.5 us)

commit v6 on v5

--- a/solution.py
+++ b/solution.py
@@ -9,6 +9,7 @@
 F32 = jnp.float32
 LANES = 128
 SPAN = 512
+WIDE = 1024
 MIB = 2**20
 
 NZ = 4
@@ -343,7 +344,7 @@
         lax.fori_loop(0, NZ, lay, 0)
         keep = pltpu.make_async_copy(u, kept.at[0], done)
         keep.start()
-        lane = lax.broadcasted_iota(jnp.int32, (part, SPAN), 1)
+        lane = lax.broadcasted_iota(jnp.int32, (part, WIDE), 1)
 
         def step(cols, k, carry):
             lasts = []
@@ -352,11 +353,11 @@
                 made = jnp.dot(w[rows, :], u[:, cols], preferred_element_type=F32)
                 prev = made[:part]
                 out[:, cols] = made[part:] + jnp.where(lane == 0, before, pltpu.roll(prev, 1, 1))
-                lasts.append(prev[:, SPAN - 1 :])
+                lasts.append(prev[:, WIDE - 1 :])
             return tuple(lasts)
 
         zero = jnp.zeros((part, 1), F32)
-        spans(length, step, (zero, zero))
+        spans(length, step, (zero, zero), span=WIDE)
         keep.wait()
 
     return call(
@@ -370,12 +371,12 @@
     )
 
 
-def spans(length, step, carry, backward=False):
-    count = length // SPAN
+def spans(length, step, carry, backward=False, span=SPAN):
+    count = length // span
 
     def run(n, carry):
         k = count - 1 - n if backward else n
-        return step(pl.ds(pl.multiple_of(k * SPAN, SPAN), SPAN), k, carry)
+        return step(pl.ds(pl.multiple_of(k * span, span), span), k, carry)
 
     return lax.fori_loop(0, count, run, carry)
 
@@ -577,13 +578,13 @@
     def body(ids, w, mine, theirs, grads, *rest):
         outs, v = rest[:5], rest[5]
         z, x, y, c = ids[0], ids[1], ids[2], ids[3]
-        lane = lax.broadcasted_iota(jnp.int32, (part, SPAN), 1)
+        lane = lax.broadcasted_iota(jnp.int32, (part, WIDE), 1)
 
         def product(cols, k, carry):
             firsts = []
             for given, core, first in ((mine, c, carry[0]), (theirs, 1 - c, carry[1])):
                 now = given[:, cols].astype(F32)
-                later = jnp.where(lane == SPAN - 1, first, pltpu.roll(now, SPAN - 1, 1))
+                later = jnp.where(lane == WIDE - 1, first, pltpu.roll(now, WIDE - 1, 1))
                 at = pl.ds(pl.multiple_of(core * 2 * part, 16), 2 * part)
                 grads[at, cols] = jnp.concatenate([later, now], axis=0).astype(BF)
                 firsts.append(now[:, :1])
@@ -591,7 +592,7 @@
             return tuple(firsts)
 
         zero = jnp.zeros((part, 1), F32)
-        spans(length, product, (zero, zero), True)
+        spans(length, product, (zero, zero), True, WIDE)
 
         def hand_out(step, carry):
             target = mod(z + 1 + step)

time: 432 us -> 431 us (level)
  transfers between devices with their start and end apart: 60 -> 60, of which waited for: 27 -> 27; matrix products, arithmetic and copies ran while one was open for 2% -> 2% of each run, Pallas kernels for 14% -> 13%
where the time goes in v6:
time: 431 us; the launch traced here: 430 us
  waiting for transfers between devices  230 us (53%)
  Pallas kernels  95.2 us (22%)
  starting transfers between devices  80.7 us (19%)
  local copies, waits for them, and re-layouts  22.8 us (5%)
    ppermute x60, waiting for transfers between devices, moved(): return lax.ppermute(array, ('tm', 'mp'), pairs)  230 us
    pallas_call x30, Pallas kernels, call(): pl.pallas_call(run, out_shape=[jax.ShapeDtypeStruct(shape, kind) for shap...  95.2 us
    ppermute x60, starting transfers between devices, moved(): return lax.ppermute(array, ('tm', 'mp'), pairs)  80.7 us
    unnamed x62, local copies, waits for them, and re-layouts  13.8 us
  transfers between devices with their start and end apart: 60, of which 27 were waited for; matrix products, arithmetic and copies ran while one was open for 2% of the time, Pallas kernels for 13%

profile of v6, /device:TPU:8, one launch (start us, length us, event | category | flops | bytes accessed | tf_op | source)
XLA Modules:
  0.0 430.2 jit_solution(13604798437695859578)
XLA Ops:
  14.9 4.8 %collective-permute-done.2.refs_4_ = bf16[576,256]{1,0:T(8,128)(2,1)S(1)} collective-permute-done((bf16[576,256]{1,0:T(8,128)(2,1)S(1)}, bf16[576,256]{1,0:T(8,128)(2,1)S(1)}, u32[]{:S(2)}, u32[]{:S(2)}) %collective-permute-start.2) | collective-permute-done | bytes 294944 | tf_op jit(solution)/shard_map/ppermute | solution.py:34
  19.7 12.5 %collective-permute-done.1.refs_3_ = bf16[576,256]{1,0:T(8,128)(2,1)S(1)} collective-permute-done((bf16[576,256]{1,0:T(8,128)(2,1)S(1)}, bf16[576,256]{1,0:T(8,128)(2,1)S(1)}, u32[]{:S(2)}, u32[]{:S(2)}) %collective-permute-start.1) | collective-permute-done | bytes 294944 | tf_op jit(solution)/shard_map/ppermute | solution.py:34
  32.3 5.5 %collective-permute-done.refs_2_ = bf16[576,256]{1,0:T(8,128)(2,1)S(1)} collective-permute-done((bf16[576,256]{1,0:T(8,128)(2,1)S(1)}, bf16[576,256]{1,0:T(8,128)(2,1)S(1)}, u32[]{:S(2)}, u32[]{:S(2)}) %collective-permute-start) | collective-permute-done | bytes 294944 | tf_op jit(solution)/shard_map/ppermute | solution.py:34
  49.0 18.7 %collective-permute-done.9.refs_2_.refs_4_ = bf16[4,576,256]{2,1,0:T(8,128)(2,1)S(1)} collective-permute-done((bf16[4,576,256]{2,1,0:T(8,128)(2,1)S(1)}, bf16[4,576,256]{2,1,0:T(8,128)(2,1)S(1)}, u32[]{:S(2)}, u32[]{:S(2)}) %collective-permute-start.9) | collective-permute-done | bytes 1179680 | tf_op jit(solution)/shard_map/ppermute | solution.py:34
  82.4 9.1 %collective-permute-done.6.refs_3_ = bf16[216,1152]{1,0:T(8,128)(2,1)} collective-permute-done((bf16[216,1152]{1,0:T(8,128)(2,1)}, bf16[216,1152]{1,0:T(8,128)(2,1)}, u32[]{:S(2)}, u32[]{:S(2)}) %collective-permute-start.6) | collective-permute-done | bytes 497696 | tf_op jit(solution)/shard_map/ppermute | solution.py:34
  99.3 6.3 %shard_map.117 = (bf16[9,1152,2048]{2,1,0:T(8,128)(2,1)}, f32[216,2048]{1,0:T(8,128)S(1)}, f32[216,2048]{1,0:T(8,128)S(1)}) custom-call(s32[4]{0:T(128)S(1)} %pad_add_fusion.refs_0_, bf16[864,1152]{1,0:T(8,128)(2,1)S(1)} %get-tuple-element.99.refs_1_, bf16[4,576,256]{2,1,0:T(8,128)(2,1)S(1)} %copy-done.24, bf16[4,576,256]{2,1,0:T(8,128)(2,1)S(1)} %copy-done.7, ...), custom_call_target="tpu_custom_call" | custom-call | flops 4076863488 | bytes 10248208 | tf_op jit(solution)/shard_map/pallas_call | solution.py:70
  109.4 5.0 %shard_map.118 = (bf16[72,2048]{1,0:T(8,128)(2,1)S(1)}, f32[72,72,2048]{2,1,0:T(8,128)}) custom-call(s32[4]{0:T(128)S(1)} %pad_add_fusion.refs_0_, f32[216,2048]{1,0:T(8,128)S(1)} %get-tuple-element.111.refs_1_, f32[216,2048]{1,0:T(8,128)S(1)} %collective-permute-done.16.refs_2_, f32[216,1]{1,0:T(8,128)S(1)} %copy-done.20), custom_call_target="tpu_custom_call" | custom-call | bytes 3834736 | tf_op jit(solution)/shard_map/pallas_call | solution.py:70
  123.7 17.9 %collective-permute-done.19.refs_4_ = bf16[72,2048]{1,0:T(8,128)(2,1)S(1)} collective-permute-done((bf16[72,2048]{1,0:T(8,128)(2,1)S(1)}, bf16[72,2048]{1,0:T(8,128)(2,1)S(1)}, u32[]{:S(2)}, u32[]{:S(2)}) %collective-permute-start.19) | collective-permute-done | bytes 294944 | tf_op jit(solution)/shard_map/ppermute | solution.py:34
  153.0 21.8 %collective-permute-done.26.refs_2_.refs_4_ = bf16[4,72,2048]{2,1,0:T(8,128)(2,1)S(1)} collective-permute-done((bf16[4,72,2048]{2,1,0:T(8,128)(2,1)S(1)}, bf16[4,72,2048]{2,1,0:T(8,128)(2,1)S(1)}, u32[]{:S(2)}, u32[]{:S(2)}) %collective-permute-start.26) | collective-permute-done | bytes 1179680 | tf_op jit(solution)/shard_map/ppermute | solution.py:34
  178.9 5.8 %collective-permute-done.22.refs_2_ = bf16[216,1152]{1,0:T(8,128)(2,1)S(1)} collective-permute-done((bf16[216,1152]{1,0:T(8,128)(2,1)S(1)}, bf16[216,1152]{1,0:T(8,128)(2,1)S(1)}, u32[]{:S(2)}, u32[]{:S(2)}) %collective-permute-start.22) | collective-permute-done | bytes 497696 | tf_op jit(solution)/shard_map/ppermute | solution.py:34
  184.7 9.1 %collective-permute-done.23.refs_3_ = bf16[216,1152]{1,0:T(8,128)(2,1)S(1)} collective-permute-done((bf16[216,1152]{1,0:T(8,128)(2,1)S(1)}, bf16[216,1152]{1,0:T(8,128)(2,1)S(1)}, u32[]{:S(2)}, u32[]{:S(2)}) %collective-permute-start.23) | collective-permute-done | bytes 497696 | tf_op jit(solution)/shard_map/ppermute | solution.py:34
  197.1 6.9 %shard_map.123 = (bf16[9,1152,2048]{2,1,0:T(8,128)(2,1)}, f32[216,2048]{1,0:T(8,128)S(1)}, f32[216,2048]{1,0:T(8,128)S(1)}) custom-call(s32[4]{0:T(128)S(1)} %pad_add_fusion.refs_0_, bf16[864,1152]{1,0:T(8,128)(2,1)S(1)} %get-tuple-element.121.refs_1_, bf16[4,72,2048]{2,1,0:T(8,128)(2,1)S(1)} %get-tuple-element.122.refs_2_, ...), custom_call_target="tpu_custom_call" | custom-call | flops 4076863488 | bytes 10248208 | tf_op jit(solution)/shard_map/pallas_call | solution.py:70
  207.7 7.8 %shard_map.124 = (bf16[4,72,256]{2,1,0:T(8,128)(2,1)S(1)}, bf16[4,72,256]{2,1,0:T(8,128)(2,1)S(1)}, bf16[216,2048]{1,0:T(8,128)(2,1)S(1)}) custom-call(s32[4]{0:T(128)S(1)} %pad_add_fusion.refs_0_, f32[216,2048]{1,0:T(8,128)S(1)} %get-tuple-element.125.refs_1_, f32[216,2048]{1,0:T(8,128)S(1)} %collective-permute-done.29.refs_2_, f32[216,1]{1,0:T(8,128)S(1)} %copy-done.18, ...), custom_call_target="tpu_custom_call" | custom-call | bytes 5014384 | tf_op jit(solution)/shard_map/pallas_call | solution.py:70
  218.8 7.4 %shard_map.125 = (bf16[864,2048]{1,0:T(8,128)(2,1)S(1)}, f32[4,72,2048]{2,1,0:T(8,128)S(1)}, f32[4,72,2048]{2,1,0:T(8,128)S(1)}, f32[4,72,2048]{2,1,0:T(8,128)S(...) custom-call(s32[4]{0:T(128)S(1)} %pad_add_fusion.refs_0_, ...), custom_call_target="tpu_custom_call" | custom-call | flops 4076863488 | bytes 15556624 | tf_op jit(solution)/shard_map/pallas_call | solution.py:70
  230.1 7.8 %shard_map.129 = (bf16[224,1152]{1,0:T(8,128)(2,1)S(1)}, bf16[224,1152]{1,0:T(8,128)(2,1)S(1)}, bf16[224,1152]{1,0:T(8,128)(2,1)S(1)}, bf16[224,1152]{1,0:T(8,128)(2,1)S(1)}) custom-call(s32[4]{0:T(128)S(1)} %pad_add_fusion.refs_0_, bf16[864,2048]{1,0:T(8,128)(2,1)S(1)} %get-tuple-element.132.refs_3_.refs_1_, ...), custom_call_target="tpu_custom_call" | custom-call | flops 4076863488 | bytes 10321936 | tf_op jit(solution)/shard_map/pallas_call | solution.py:70
  246.0 28.7 %collective-permute-done.39.refs_2_ = bf16[224,1152]{1,0:T(8,128)(2,1)S(1)} collective-permute-done((bf16[224,1152]{1,0:T(8,128)(2,1)S(1)}, bf16[224,1152]{1,0:T(8,128)(2,1)S(1)}, u32[]{:S(2)}, u32[]{:S(2)}) %collective-permute-start.39) | collective-permute-done | bytes 516128 | tf_op jit(solution)/shard_map/ppermute | solution.py:34
  274.7 9.3 %collective-permute-done.41.refs_4_ = bf16[224,1152]{1,0:T(8,128)(2,1)S(1)} collective-permute-done((bf16[224,1152]{1,0:T(8,128)(2,1)S(1)}, bf16[224,1152]{1,0:T(8,128)(2,1)S(1)}, u32[]{:S(2)}, u32[]{:S(2)}) %collective-permute-start.41) | collective-permute-done | bytes 516128 | tf_op jit(solution)/shard_map/ppermute | solution.py:34
  294.2 17.1 %collective-permute-done.46.refs_10_.refs_2_ = bf16[2,224,1152]{2,1,0:T(8,128)(2,1)S(1)} collective-permute-done((bf16[2,224,1152]{2,1,0:T(8,128)(2,1)S(1)}, bf16[2,224,1152]{2,1,0:T(8,128)(2,1)S(1)}, u32[]{:S(2)}, u32[]{:S(2)}) %collective-permute-start.46) | collective-permute-done | bytes 1032224 | tf_op jit(solution)/shard_map/ppermute | solution.py:34
  311.3 4.9 %collective-permute-done.43.refs_3_ = bf16[72,2048]{1,0:T(8,128)(2,1)S(1)} collective-permute-done((bf16[72,2048]{1,0:T(8,128)(2,1)S(1)}, bf16[72,2048]{1,0:T(8,128)(2,1)S(1)}, u32[]{:S(2)}, u32[]{:S(2)}) %collective-permute-start.43) | collective-permute-done | bytes 294944 | tf_op jit(solution)/shard_map/ppermute | solution.py:34
  328.8 7.5 %shard_map.133 = (bf16[864,2048]{1,0:T(8,128)(2,1)S(1)}, f32[4,576,256]{2,1,0:T(8,128)S(1)}, f32[4,576,256]{2,1,0:T(8,128)S(1)}, f32[4,576,256]{2,1,0:T(8,128)S(...) custom-call(s32[4]{0:T(128)S(1)} %pad_add_fusion.refs_0_, bf16[1152,864]{1,0:T(8,128)(2,1)S(1)} %copy-done.30, ...), custom_call_target="tpu_custom_call" | custom-call | flops 4076863488 | bytes 15556624 | tf_op jit(solution)/shard_map/pallas_call | solution.py:70
  337.6 7.7 %shard_map.136 = (bf16[224,1152]{1,0:T(8,128)(2,1)S(1)}, bf16[224,1152]{1,0:T(8,128)(2,1)S(1)}, bf16[224,1152]{1,0:T(8,128)(2,1)S(1)}, bf16[224,1152]{1,0:T(8,128)(2,1)S(1)}) custom-call(s32[4]{0:T(128)S(1)} %pad_add_fusion.refs_0_, bf16[864,2048]{1,0:T(8,128)(2,1)S(1)} %get-tuple-element.165.refs_1_, bf16[1152,2048]{1,0:T(8,128)(2,1)S(1)} %slice_bitcast_fusion.refs_2_), custom_call_target="tpu_custom_call" | custom-call | flops 4076863488 | bytes 10321936 | tf_op jit(solution)/shard_map/pallas_call | solution.py:70
  361.0 21.2 %collective-permute-done.52.refs_2_ = bf16[224,1152]{1,0:T(8,128)(2,1)S(1)} collective-permute-done((bf16[224,1152]{1,0:T(8,128)(2,1)S(1)}, bf16[224,1152]{1,0:T(8,128)(2,1)S(1)}, u32[]{:S(2)}, u32[]{:S(2)}) %collective-permute-start.52) | collective-permute-done | bytes 516128 | tf_op jit(solution)/shard_map/ppermute | solution.py:34
  382.3 8.2 %collective-permute-done.54.refs_4_ = bf16[224,1152]{1,0:T(8,128)(2,1)S(1)} collective-permute-done((bf16[224,1152]{1,0:T(8,128)(2,1)S(1)}, bf16[224,1152]{1,0:T(8,128)(2,1)S(1)}, u32[]{:S(2)}, u32[]{:S(2)}) %collective-permute-start.54) | collective-permute-done | bytes 516128 | tf_op jit(solution)/shard_map/ppermute | solution.py:34
  403.6 16.0 %collective-permute-done.59.refs_2_ = bf16[2,224,1152]{2,1,0:T(8,128)(2,1)S(1)} collective-permute-done((bf16[2,224,1152]{2,1,0:T(8,128)(2,1)S(1)}, bf16[2,224,1152]{2,1,0:T(8,128)(2,1)S(1)}, u32[]{:S(2)}, u32[]{:S(2)}) %collective-permute-start.59) | collective-permute-done | bytes 1032224 | tf_op jit(solution)/shard_map/ppermute | solution.py:34
  (200 shorter events, 161.9 us)
Async XLA Ops:
  5.8 31.9 %collective-permute-start.3 = (bf16[2,216,1152]{2,1,0:T(8,128)(2,1)S(1)}, bf16[2,216,1152]{2,1,0:T(8,128)(2,1)S(1)}, u32[]{:S(2)}, u32[]{:S(2)}) collective-permute-start(bf16[2,216,1152]{2,1,0:T(8,128)(2,1)S(1)} %get-tuple-element.93), channel_id=1, source_target_pairs={{0,0},{1,4},{2,2},{3,6},{4,1},{5,5},{6,3},{7,7},{8,8},{9,12},{10,1... | collective-permute-start | bytes 2985992 | tf_op jit(solution)/shard_map/ppermute | solution.py:34
  6.7 31.1 %collective-permute-start.4 = (bf16[2,216,1152]{2,1,0:T(8,128)(2,1)S(1)}, bf16[2,216,1152]{2,1,0:T(8,128)(2,1)S(1)}, u32[]{:S(2)}, u32[]{:S(2)}) collective-permute-start(bf16[2,216,1152]{2,1,0:T(8,128)(2,1)S(1)} %get-tuple-element.94), channel_id=1, source_target_pairs={{0,4},{1,0},{2,6},{3,2},{4,5},{5,1},{6,7},{7,3},{8,12},{9,8},{10,1... | collective-permute-start | bytes 2985992 | tf_op jit(solution)/shard_map/ppermute | solution.py:34
  40.5 27.1 %collective-permute-start.9 = (bf16[4,576,256]{2,1,0:T(8,128)(2,1)S(1)}, bf16[4,576,256]{2,1,0:T(8,128)(2,1)S(1)}, u32[]{:S(2)}, u32[]{:S(2)}) collective-permute-start(bf16[4,576,256]{2,1,0:T(8,128)(2,1)S(1)} %get-tuple-element.100.refs_2_), channel_id=1, source_target_pairs={{0,2},{1,3},{2,0},{3,1},{4,6},{5,7},{6,4},{7,5},{8,10},{9,11},{10,... | collective-permute-start | bytes 3538952 | tf_op jit(solution)/shard_map/ppermute | solution.py:34
  42.0 27.1 %collective-permute-start.8 = (bf16[4,576,256]{2,1,0:T(8,128)(2,1)S(1)}, bf16[4,576,256]{2,1,0:T(8,128)(2,1)S(1)}, u32[]{:S(2)}, u32[]{:S(2)}) collective-permute-start(bf16[4,576,256]{2,1,0:T(8,128)(2,1)S(1)} %get-tuple-element.100.refs_2_), channel_id=1, source_target_pairs={{0,4},{1,5},{2,6},{3,7},{4,0},{5,1},{6,2},{7,3},{8,12},{9,13},{10,... | collective-permute-start | bytes 3538952 | tf_op jit(solution)/shard_map/ppermute | solution.py:34
  43.8 36.5 %collective-permute-start.5 = (bf16[216,1152]{1,0:T(8,128)(2,1)}, bf16[216,1152]{1,0:T(8,128)(2,1)}, u32[]{:S(2)}, u32[]{:S(2)}) collective-permute-start(bf16[216,1152]{1,0:T(8,128)(2,1)} %get-tuple-element.96), channel_id=1, source_target_pairs={{0,8},{1,9},{2,10},{3,11},{4,12},{5,13},{6,14},{7,15},{8,16},{9,17... | collective-permute-start | bytes 1493000 | tf_op jit(solution)/shard_map/ppermute | solution.py:34
  46.2 45.2 %collective-permute-start.6 = (bf16[216,1152]{1,0:T(8,128)(2,1)}, bf16[216,1152]{1,0:T(8,128)(2,1)}, u32[]{:S(2)}, u32[]{:S(2)}) collective-permute-start(bf16[216,1152]{1,0:T(8,128)(2,1)} %get-tuple-element.97), channel_id=1, source_target_pairs={{0,16},{1,17},{2,18},{3,19},{4,20},{5,21},{6,22},{7,23},{8,24},{9,... | collective-permute-start | bytes 1493000 | tf_op jit(solution)/shard_map/ppermute | solution.py:34
  46.7 48.2 %collective-permute-start.7 = (bf16[216,1152]{1,0:T(8,128)(2,1)}, bf16[216,1152]{1,0:T(8,128)(2,1)}, u32[]{:S(2)}, u32[]{:S(2)}) collective-permute-start(bf16[216,1152]{1,0:T(8,128)(2,1)} %get-tuple-element.98), channel_id=1, source_target_pairs={{0,24},{1,25},{2,26},{3,27},{4,28},{5,29},{6,30},{7,31},{8,0},{9,1... | collective-permute-start | bytes 1493000 | tf_op jit(solution)/shard_map/ppermute | solution.py:34
  115.1 30.7 %collective-permute-start.20 = (bf16[2,216,1152]{2,1,0:T(8,128)(2,1)}, bf16[2,216,1152]{2,1,0:T(8,128)(2,1)S(1)}, u32[]{:S(2)}, u32[]{:S(2)}) collective-permute-start(bf16[2,216,1152]{2,1,0:T(8,128)(2,1)} %get-tuple-element.115), channel_id=1, source_target_pairs={{0,0},{1,4},{2,2},{3,6},{4,1},{5,5},{6,3},{7,7},{8,8},{9,12},{10,1... | collective-permute-start | bytes 2985992 | tf_op jit(solution)/shard_map/ppermute | solution.py:34
  117.1 28.7 %collective-permute-start.21 = (bf16[2,216,1152]{2,1,0:T(8,128)(2,1)}, bf16[2,216,1152]{2,1,0:T(8,128)(2,1)S(1)}, u32[]{:S(2)}, u32[]{:S(2)}) collective-permute-start(bf16[2,216,1152]{2,1,0:T(8,128)(2,1)} %get-tuple-element.116), channel_id=1, source_target_pairs={{0,4},{1,0},{2,6},{3,2},{4,5},{5,1},{6,7},{7,3},{8,12},{9,8},{10,1... | collective-permute-start | bytes 2985992 | tf_op jit(solution)/shard_map/ppermute | solution.py:34
  146.8 28.0 %collective-permute-start.26 = (bf16[4,72,2048]{2,1,0:T(8,128)(2,1)S(1)}, bf16[4,72,2048]{2,1,0:T(8,128)(2,1)S(1)}, u32[]{:S(2)}, u32[]{:S(2)}) collective-permute-start(bf16[4,72,2048]{2,1,0:T(8,128)(2,1)S(1)} %get-tuple-element.122.refs_2_), channel_id=1, source_target_pairs={{0,2},{1,3},{2,0},{3,1},{4,6},{5,7},{6,4},{7,5},{8,10},{9,11},{10,... | collective-permute-start | bytes 3538952 | tf_op jit(solution)/shard_map/ppermute | solution.py:34
  147.4 27.6 %collective-permute-start.25 = (bf16[4,72,2048]{2,1,0:T(8,128)(2,1)S(1)}, bf16[4,72,2048]{2,1,0:T(8,128)(2,1)S(1)}, u32[]{:S(2)}, u32[]{:S(2)}) collective-permute-start(bf16[4,72,2048]{2,1,0:T(8,128)(2,1)S(1)} %get-tuple-element.122.refs_2_), channel_id=1, source_target_pairs={{0,4},{1,5},{2,6},{3,7},{4,0},{5,1},{6,2},{7,3},{8,12},{9,13},{10,... | collective-permute-start | bytes 3538952 | tf_op jit(solution)/shard_map/ppermute | solution.py:34
  149.1 35.6 %collective-permute-start.22 = (bf16[216,1152]{1,0:T(8,128)(2,1)S(1)}, bf16[216,1152]{1,0:T(8,128)(2,1)S(1)}, u32[]{:S(2)}, u32[]{:S(2)}) collective-permute-start(bf16[216,1152]{1,0:T(8,128)(2,1)S(1)} %get-tuple-element.118), channel_id=1, source_target_pairs={{0,8},{1,9},{2,10},{3,11},{4,12},{5,13},{6,14},{7,15},{8,16},{9,17... | collective-permute-start | bytes 1493000 | tf_op jit(solution)/shard_map/ppermute | solution.py:34
  151.6 42.2 %collective-permute-start.23 = (bf16[216,1152]{1,0:T(8,128)(2,1)S(1)}, bf16[216,1152]{1,0:T(8,128)(2,1)S(1)}, u32[]{:S(2)}, u32[]{:S(2)}) collective-permute-start(bf16[216,1152]{1,0:T(8,128)(2,1)S(1)} %get-tuple-element.119), channel_id=1, source_target_pairs={{0,16},{1,17},{2,18},{3,19},{4,20},{5,21},{6,22},{7,23},{8,24},{9,... | collective-permute-start | bytes 1493000 | tf_op jit(solution)/shard_map/ppermute | solution.py:34
  152.9 42.2 %collective-permute-start.24 = (bf16[216,1152]{1,0:T(8,128)(2,1)S(1)}, bf16[216,1152]{1,0:T(8,128)(2,1)S(1)}, u32[]{:S(2)}, u32[]{:S(2)}) collective-permute-start(bf16[216,1152]{1,0:T(8,128)(2,1)S(1)} %get-tuple-element.120), channel_id=1, source_target_pairs={{0,24},{1,25},{2,26},{3,27},{4,28},{5,29},{6,30},{7,31},{8,0},{9,1... | collective-permute-start | bytes 1493000 | tf_op jit(solution)/shard_map/ppermute | solution.py:34
  237.8 36.8 %collective-permute-start.39 = (bf16[224,1152]{1,0:T(8,128)(2,1)S(1)}, bf16[224,1152]{1,0:T(8,128)(2,1)S(1)}, u32[]{:S(2)}, u32[]{:S(2)}) collective-permute-start(bf16[224,1152]{1,0:T(8,128)(2,1)S(1)} %get-tuple-element.147), channel_id=1, source_target_pairs={{0,24},{1,25},{2,26},{3,27},{4,28},{5,29},{6,30},{7,31},{8,0},{9,1... | collective-permute-start | bytes 1548296 | tf_op jit(solution)/shard_map/ppermute | solution.py:34
  237.9 36.8 %collective-permute-start.40 = (bf16[224,1152]{1,0:T(8,128)(2,1)S(1)}, bf16[224,1152]{1,0:T(8,128)(2,1)S(1)}, u32[]{:S(2)}, u32[]{:S(2)}) collective-permute-start(bf16[224,1152]{1,0:T(8,128)(2,1)S(1)} %get-tuple-element.148), channel_id=1, source_target_pairs={{0,16},{1,17},{2,18},{3,19},{4,20},{5,21},{6,22},{7,23},{8,24},{9,... | collective-permute-start | bytes 1548296 | tf_op jit(solution)/shard_map/ppermute | solution.py:34
  240.1 43.9 %collective-permute-start.41 = (bf16[224,1152]{1,0:T(8,128)(2,1)S(1)}, bf16[224,1152]{1,0:T(8,128)(2,1)S(1)}, u32[]{:S(2)}, u32[]{:S(2)}) collective-permute-start(bf16[224,1152]{1,0:T(8,128)(2,1)S(1)} %get-tuple-element.149), channel_id=1, source_target_pairs={{0,8},{1,9},{2,10},{3,11},{4,12},{5,13},{6,14},{7,15},{8,16},{9,17... | collective-permute-start | bytes 1548296 | tf_op jit(solution)/shard_map/ppermute | solution.py:34
  243.8 43.6 %collective-permute-start.37 = (bf16[4,72,2048]{2,1,0:T(8,128)(2,1)S(1)}, bf16[4,72,2048]{2,1,0:T(8,128)(2,1)S(1)}, u32[]{:S(2)}, u32[]{:S(2)}) collective-permute-start(bf16[4,72,2048]{2,1,0:T(8,128)(2,1)S(1)} %get-tuple-element.143), channel_id=1, source_target_pairs={{0,4},{1,5},{2,6},{3,7},{4,0},{5,1},{6,2},{7,3},{8,12},{9,13},{10,... | collective-permute-start | bytes 3538952 | tf_op jit(solution)/shard_map/ppermute | solution.py:34
  245.5 41.9 %collective-permute-start.38 = (bf16[4,72,2048]{2,1,0:T(8,128)(2,1)S(1)}, bf16[4,72,2048]{2,1,0:T(8,128)(2,1)S(1)}, u32[]{:S(2)}, u32[]{:S(2)}) collective-permute-start(bf16[4,72,2048]{2,1,0:T(8,128)(2,1)S(1)} %get-tuple-element.144), channel_id=1, source_target_pairs={{0,2},{1,3},{2,0},{3,1},{4,6},{5,7},{6,4},{7,5},{8,10},{9,11},{10,... | collective-permute-start | bytes 3538952 | tf_op jit(solution)/shard_map/ppermute | solution.py:34
  345.4 36.9 %collective-permute-start.52 = (bf16[224,1152]{1,0:T(8,128)(2,1)S(1)}, bf16[224,1152]{1,0:T(8,128)(2,1)S(1)}, u32[]{:S(2)}, u32[]{:S(2)}) collective-permute-start(bf16[224,1152]{1,0:T(8,128)(2,1)S(1)} %get-tuple-element.168), channel_id=1, source_target_pairs={{0,24},{1,25},{2,26},{3,27},{4,28},{5,29},{6,30},{7,31},{8,0},{9,1... | collective-permute-start | bytes 1548296 | tf_op jit(solution)/shard_map/ppermute | solution.py:34
  345.7 36.5 %collective-permute-start.53 = (bf16[224,1152]{1,0:T(8,128)(2,1)S(1)}, bf16[224,1152]{1,0:T(8,128)(2,1)S(1)}, u32[]{:S(2)}, u32[]{:S(2)}) collective-permute-start(bf16[224,1152]{1,0:T(8,128)(2,1)S(1)} %get-tuple-element.169), channel_id=1, source_target_pairs={{0,16},{1,17},{2,18},{3,19},{4,20},{5,21},{6,22},{7,23},{8,24},{9,... | collective-permute-start | bytes 1548296 | tf_op jit(solution)/shard_map/ppermute | solution.py:34
  347.0 43.5 %collective-permute-start.54 = (bf16[224,1152]{1,0:T(8,128)(2,1)S(1)}, bf16[224,1152]{1,0:T(8,128)(2,1)S(1)}, u32[]{:S(2)}, u32[]{:S(2)}) collective-permute-start(bf16[224,1152]{1,0:T(8,128)(2,1)S(1)} %get-tuple-element.170), channel_id=1, source_target_pairs={{0,8},{1,9},{2,10},{3,11},{4,12},{5,13},{6,14},{7,15},{8,16},{9,17... | collective-permute-start | bytes 1548296 | tf_op jit(solution)/shard_map/ppermute | solution.py:34
  358.2 37.4 %collective-permute-start.50 = (bf16[4,576,256]{2,1,0:T(8,128)(2,1)S(1)}, bf16[4,576,256]{2,1,0:T(8,128)(2,1)S(1)}, u32[]{:S(2)}, u32[]{:S(2)}) collective-permute-start(bf16[4,576,256]{2,1,0:T(8,128)(2,1)S(1)} %get-tuple-element.163), channel_id=1, source_target_pairs={{0,4},{1,5},{2,6},{3,7},{4,0},{5,1},{6,2},{7,3},{8,12},{9,13},{10,... | collective-permute-start | bytes 3538952 | tf_op jit(solution)/shard_map/ppermute | solution.py:34
  359.5 36.1 %collective-permute-start.51 = (bf16[4,576,256]{2,1,0:T(8,128)(2,1)S(1)}, bf16[4,576,256]{2,1,0:T(8,128)(2,1)S(1)}, u32[]{:S(2)}, u32[]{:S(2)}) collective-permute-start(bf16[4,576,256]{2,1,0:T(8,128)(2,1)S(1)} %get-tuple-element.164), channel_id=1, source_target_pairs={{0,2},{1,3},{2,0},{3,1},{4,6},{5,7},{6,4},{7,5},{8,10},{9,11},{10,... | collective-permute-start | bytes 3538952 | tf_op jit(solution)/shard_map/ppermute | solution.py:34
  (67 other events, 889.7 us)
